TPU v7x, 32 devices: a whole 2x2x4 slice. The times are simulated.
32 devices in a mesh: dp: 4 (over y, x), mp: 8 (over z, core).
Axes of the slice: x: 2, y: 2, z: 4, core: 2. Of those that a mesh axis runs over, the one named last changes fastest.
Arguments:
- tokens: bfloat16 [1536, 2048], P('dp'), may hold values from -6 to 6
- cotangent: bfloat16 [1536, 2048], P('dp'), may hold values from -6 to 6
- norm_gains: float32 [2, 2048], replicated, may hold values from 0.1 to 1.9
- w_attn: bfloat16 [4, 2048, 2048], P(None, 'mp'), may hold values from -0.125 to 0.125
- w_in: bfloat16 [2, 2048, 5632], P(None, 'mp'), may hold values from -0.125 to 0.125
- w_down: bfloat16 [5632, 2048], P('mp'), may hold values from -0.078125 to 0.078125
- segments: int32 [4, 384], P('dp'), may hold values from 0 to 5, never falling along the last dimension, each value on 1 to 288 neighbouring positions
- owners: int32 [637], replicated, may hold values from 0 to 31, as said below
- master: float32 [1280, 1024], P(('dp', 'mp'))
- first_moment: float32 [1280, 1024], P(('dp', 'mp'))
- second_moment: float32 [1280, 1024], P(('dp', 'mp'))
Outputs:
- layer_out: bfloat16 [1536, 2048], P('dp')
- input_grad: float32 [1536, 2048], P('dp')
- new_master: float32 [1280, 1024], P(('dp', 'mp'))
- new_first: float32 [1280, 1024], P(('dp', 'mp'))
- new_second: float32 [1280, 1024], P(('dp', 'mp'))
Inputs may be any that keep to these rules, and one draw needn't show every extreme that they name: `segments`: segment numbers never fall along a row. `owners`: no device keeps more than 40 blocks, and some device keeps exactly 40.
All inputs are finite; a program needn't handle non-finite values.
Results may differ from a plain program's by a relative error of at most 0.014.
The roundings to bfloat16 on the way count: a program that leaves them out, or rounds other values in their place, can miss the bound.
Values may be sent and summed in bfloat16 or wider, within the bound.
No kernel may reach another device: no remote copies, remote signals or barrier semaphores. Data moves between devices by JAX's collectives and lax.ppermute only.
A program may use at most 320 MiB of HBM per device.

v0:
```python
import functools

import jax
import jax.numpy as jnp
import numpy as np
from jax import lax
from jax.experimental import pallas as pl
from jax.experimental.pallas import tpu as pltpu
from jax.sharding import PartitionSpec as P

D = 2048
FF = 5632
HEADS = 16
HEAD_DIM = 128
RANK = 16
BLOCK = 1024
STEP = 5


dora_scale = 2.0
rope_base = 10000.0
norm_eps = 1e-05
column_eps = 1e-06
beta_one = 0.5
beta_two = 0.5
adam_eps = 1e-08
weight_decay = 0.01
rate_lower = 0.02
rate_upper = 0.1
rate_magnitude = 1.0
highest = lax.Precision.HIGHEST


def proj_dims():
    return [(D, D), (D, D), (D, D), (D, D), (D, FF), (D, FF), (FF, D)]


def unpack(flat):
    offset = 0
    lowers = []
    for inner, outer in proj_dims():
        lowers.append(flat[offset : offset + inner * RANK].reshape(inner, RANK))
        offset += inner * RANK
    uppers = []
    for inner, outer in proj_dims():
        uppers.append(flat[offset : offset + outer * RANK].reshape(outer, RANK))
        offset += outer * RANK
    magnitudes = []
    for inner, outer in proj_dims():
        magnitudes.append(flat[offset : offset + outer])
        offset += outer
    return (lowers, uppers, magnitudes)


def slot_positions(owners, capacity):
    order = jnp.arange(owners.shape[0], dtype=jnp.int32)
    same = (owners[:, None] == owners[None, :]) & (order[None, :] < order[:, None])
    ranks = jnp.sum(same.astype(jnp.int32), axis=1)
    return owners * capacity + ranks


def block_rates(block_ids):
    count_lower = RANK * (6 * D + FF) // BLOCK
    count_upper = RANK * (5 * D + 2 * FF) // BLOCK
    rates = jnp.where(block_ids < count_lower + count_upper, rate_upper, rate_magnitude)
    rates = jnp.where(block_ids < count_lower, rate_lower, rates)
    return jnp.where(block_ids < 0, 0.0, rates).astype(jnp.float32)


def adam_update(weight, grad, first, second, rates):
    first_new = beta_one * first + (1.0 - beta_one) * grad
    second_new = beta_two * second + (1.0 - beta_two) * grad * grad
    first_hat = first_new / (1.0 - beta_one**STEP)
    second_hat = second_new / (1.0 - beta_two**STEP)
    weight_new = weight - rates[:, None] * (
        first_hat / (jnp.sqrt(second_hat) + adam_eps) + weight_decay * weight
    )
    return (weight_new, first_new, second_new)


def rms_norm(values, gain):
    return values * lax.rsqrt(jnp.mean(values * values, axis=-1, keepdims=True) + norm_eps) * gain


def rms_back(values, grad, gain):
    inverse = lax.rsqrt(jnp.mean(values * values, axis=-1, keepdims=True) + norm_eps)
    scaled = grad * gain
    return inverse * (
        scaled - values * inverse * inverse * jnp.mean(scaled * values, axis=-1, keepdims=True)
    )


def segment_positions(row):
    order = jnp.arange(row.shape[0], dtype=jnp.int32)
    change = jnp.concatenate([jnp.ones((1,), dtype=bool), row[1:] != row[:-1]])
    starts = lax.cummax(jnp.where(change, order, 0), axis=0)
    return order - starts


def rotary_tables(positions):
    half = HEAD_DIM // 2
    freqs = rope_base ** (-(jnp.arange(half).astype(jnp.float32) * 2.0 / HEAD_DIM))
    angles = positions.astype(jnp.float32)[:, None] * freqs[None, :]
    return (jnp.cos(angles)[:, None, :], jnp.sin(angles)[:, None, :])


def rotate(values, cosine, sine):
    half = values.shape[-1] // 2
    first_half = values[..., :half]
    second_half = values[..., half:]
    return jnp.concatenate(
        [first_half * cosine - second_half * sine, second_half * cosine + first_half * sine],
        axis=-1,
    )


def unrotate(values, cosine, sine):
    half = values.shape[-1] // 2
    first_half = values[..., :half]
    second_half = values[..., half:]
    return jnp.concatenate(
        [first_half * cosine + second_half * sine, second_half * cosine - first_half * sine],
        axis=-1,
    )


def body(
    tokens,
    cotangent,
    norm_gains,
    w_attn,
    w_in,
    w_down,
    segments,
    owners,
    master,
    first_moment,
    second_moment,
):
    group_rows = tokens.shape[0]
    model_size = lax.axis_size("mp")
    model_index = lax.axis_index("mp")
    share = group_rows // model_size
    share_start = model_index * share
    capacity = master.shape[0]
    everyone = lax.axis_size(("dp", "mp"))
    score_scale = HEAD_DIM ** (-0.5)
    widths = [outer for inner, outer in proj_dims()]
    slot_index = slot_positions(owners, capacity)
    copies = lax.all_gather(master.astype(jnp.bfloat16), ("dp", "mp"), axis=0, tiled=True)
    lowers, uppers, magnitudes = unpack(jnp.take(copies, slot_index, axis=0).reshape(-1))
    frozen = [w_attn[0], w_attn[1], w_attn[2], w_attn[3], w_in[0], w_in[1], w_down]
    lower_local = []
    combined = []
    square_parts = []
    for index in range(7):
        rows_here = frozen[index].shape[0]
        piece = lax.dynamic_slice_in_dim(lowers[index], model_index * rows_here, rows_here, 0)
        lower_local.append(piece)
        joined = frozen[index].astype(jnp.float32) + dora_scale * jnp.dot(
            piece.astype(jnp.float32), uppers[index].astype(jnp.float32).T, precision=highest
        )
        combined.append(joined)
        square_parts.append(jnp.sum(joined * joined, axis=0))

    def rows_of(values):
        return lax.dynamic_slice_in_dim(values, share_start, share, 0)

    def split_parts(values, indices, axis):
        pieces = []
        offset = 0
        for index in indices:
            pieces.append(lax.slice_in_dim(values, offset, offset + widths[index], axis=axis))
            offset += widths[index]
        return pieces

    norms = [None] * 7
    mixed_share = [None] * 7
    low_share = [None] * 7
    mixed_full = [None] * 7
    grads = [None] * 7

    def set_scales(indices):
        summed = lax.psum(jnp.concatenate([square_parts[index] for index in indices]), "mp")
        squares = split_parts(summed, indices, 0)
        for index, value in zip(indices, squares):
            norms[index] = jnp.sqrt(value + column_eps)

    def scale(index):
        return magnitudes[index].astype(jnp.float32) / norms[index]

    def local_partials(inputs_local, indices):
        mixed_list = []
        low_list = []
        for index in indices:
            low_part = jnp.dot(inputs_local, lower_local[index], preferred_element_type=jnp.float32)
            mixed = jnp.dot(
                inputs_local, frozen[index], preferred_element_type=jnp.float32
            ) + dora_scale * jnp.dot(
                low_part, uppers[index].astype(jnp.float32).T, precision=highest
            )
            mixed_list.append(mixed)
            low_list.append(low_part)
        return (
            inputs_local,
            jnp.concatenate(mixed_list, axis=1),
            jnp.concatenate(low_list, axis=1),
        )

    def group_partials(inputs_b, indices):
        rows_here = frozen[indices[0]].shape[0]
        inputs_local = lax.dynamic_slice_in_dim(inputs_b, model_index * rows_here, rows_here, 1)
        return local_partials(inputs_local, indices)

    def finish(indices, local_mixed, local_low):
        summed_mixed, summed_low = lax.psum((local_mixed, local_low), "mp")
        pieces = split_parts(summed_mixed, indices, 1)
        for position, index in enumerate(indices):
            mixed_full[index] = pieces[position]
            mixed_share[index] = rows_of(pieces[position])
            low_share[index] = rows_of(summed_low[:, position * RANK : (position + 1) * RANK])
        return pieces

    def gather_inputs(local):
        return lax.all_gather(local, "mp", axis=1, tiled=True)

    xf = tokens.astype(jnp.float32)
    row = segments[0]
    cosine, sine = rotary_tables(segment_positions(row))
    order = jnp.arange(group_rows)
    allowed = (row[:, None] == row[None, :]) & (order[None, :] <= order[:, None])
    features = rms_norm(xf, norm_gains[0]).astype(jnp.bfloat16)
    first_local, first_mixed, first_low = group_partials(features, (0, 1, 2))
    set_scales((0, 1, 2))
    summed_mixed, summed_low = lax.psum((first_mixed, first_low), "mp")
    pieces = split_parts(summed_mixed, (0, 1, 2), 1)
    heads_in = []
    for index in range(3):
        mixed_full[index] = pieces[index]
        mixed_share[index] = rows_of(pieces[index])
        low_share[index] = rows_of(summed_low[:, index * RANK : (index + 1) * RANK])
        projected = (pieces[index] * scale(index)).reshape(group_rows, HEADS, HEAD_DIM)
        if index < 2:
            projected = rotate(projected, cosine, sine)
        heads_in.append(projected.astype(jnp.bfloat16))
    query_b, key_b, value_b = heads_in

    def attention_scores(query_h, key_h):
        scores = (
            jnp.einsum("thd,shd->hts", query_h, key_h, preferred_element_type=jnp.float32)
            * score_scale
        )
        return jnp.where(allowed[None], scores, -1e30)

    scores = attention_scores(query_b, key_b)
    top = jnp.max(scores, axis=-1, keepdims=True)
    expd = jnp.exp(scores - top)
    total = jnp.sum(expd, axis=-1, keepdims=True)
    probs = (expd / total).astype(jnp.bfloat16)
    attended_h = jnp.einsum("hts,shd->thd", probs, value_b, preferred_element_type=jnp.float32)
    attended_h, log_total = (attended_h, top + jnp.log(total))
    attended = attended_h.reshape(group_rows, D).astype(jnp.bfloat16)
    out_local, out_mixed, out_low = group_partials(attended, (3,))
    set_scales((3,))
    x_two = xf + finish((3,), out_mixed, out_low)[0] * scale(3)
    second_features = rms_norm(x_two, norm_gains[1]).astype(jnp.bfloat16)
    ffn_local, ffn_mixed, ffn_low = group_partials(second_features, (4, 5))
    set_scales((4, 5))
    gate_pre, up_pre = finish((4, 5), ffn_mixed, ffn_low)
    gate = gate_pre * scale(4)
    upward = up_pre * scale(5)
    sigmoid_gate = jax.nn.sigmoid(gate)
    act = (gate * sigmoid_gate * upward).astype(jnp.bfloat16)
    down_local, down_mixed, down_low = group_partials(act, (6,))
    set_scales((6,))
    down_pre = finish((6,), down_mixed, down_low)[0]
    layer_out = (x_two + down_pre * scale(6)).astype(jnp.bfloat16)

    def whole_dot(index, grad):
        return jnp.sum(grad * mixed_full[index], axis=0)

    def project_back(index, grad, inputs_local, group_dot):
        norm = norms[index]
        magnitude = magnitudes[index].astype(jnp.float32)
        grad_b = (grad * (magnitude / norm)).astype(jnp.bfloat16)
        share_dot = jnp.sum(rows_of(grad) * mixed_share[index], axis=0)
        grad_full = combined[index] * (-group_dot * magnitude / (norm * norm * norm))[None, :]
        upper_f = uppers[index].astype(jnp.float32)
        lower_f = lower_local[index].astype(jnp.float32)
        through = dora_scale * jnp.dot(grad_b, uppers[index], preferred_element_type=jnp.float32)
        grad_lower = jnp.dot(
            inputs_local.astype(jnp.float32).T, through, precision=highest
        ) + dora_scale * jnp.dot(grad_full, upper_f, precision=highest)
        grad_upper = dora_scale * jnp.dot(
            rows_of(grad_b).astype(jnp.float32).T, low_share[index], precision=highest
        ) + dora_scale * jnp.dot(grad_full.T, lower_f, precision=highest)
        grads[index] = (grad_lower, grad_upper, share_dot / norm)
        return jnp.dot(grad_b, frozen[index].T, preferred_element_type=jnp.float32) + jnp.dot(
            through, lower_f.T, precision=highest
        )

    grad_out = cotangent.astype(jnp.float32)
    grad_act = gather_inputs(project_back(6, grad_out, down_local, whole_dot(6, grad_out)))
    grad_gate = grad_act * upward * sigmoid_gate * (1.0 + gate * (1.0 - sigmoid_gate))
    grad_up = grad_act * gate * sigmoid_gate
    ffn_back = project_back(4, grad_gate, ffn_local, whole_dot(4, grad_gate)) + project_back(
        5, grad_up, ffn_local, whole_dot(5, grad_up)
    )
    grad_two = grad_out + rms_back(x_two, gather_inputs(ffn_back), norm_gains[1])
    grad_att = gather_inputs(project_back(3, grad_two, out_local, whole_dot(3, grad_two)))
    grad_att = grad_att.astype(jnp.bfloat16).reshape(group_rows, HEADS, HEAD_DIM)
    weights = jnp.exp(attention_scores(query_b, key_b) - log_total)
    weights_b = weights.astype(jnp.bfloat16)
    grad_weights = jnp.einsum("thd,shd->hts", grad_att, value_b, preferred_element_type=jnp.float32)
    grad_value = jnp.einsum("hts,thd->shd", weights_b, grad_att, preferred_element_type=jnp.float32)
    centred = jnp.sum(weights * grad_weights, axis=-1, keepdims=True)
    grad_scores = (weights * (grad_weights - centred)).astype(jnp.bfloat16)
    grad_query = (
        jnp.einsum("hts,shd->thd", grad_scores, key_b, preferred_element_type=jnp.float32)
        * score_scale
    )
    grad_key = (
        jnp.einsum("hts,thd->shd", grad_scores, query_b, preferred_element_type=jnp.float32)
        * score_scale
    )
    grad_query, grad_key, grad_value = (
        unrotate(grad_query, cosine, sine),
        unrotate(grad_key, cosine, sine),
        grad_value,
    )
    incoming = [
        grad_query.reshape(group_rows, D),
        grad_key.reshape(group_rows, D),
        grad_value.reshape(group_rows, D),
    ]
    group_dots = [whole_dot(index, incoming[index]) for index in range(3)]
    first_back = project_back(0, incoming[0], first_local, group_dots[0])
    first_back = first_back + project_back(1, incoming[1], first_local, group_dots[1])
    first_back = first_back + project_back(2, incoming[2], first_local, group_dots[2])
    input_grad = grad_two + rms_back(xf, gather_inputs(first_back), norm_gains[0])
    pieces = []
    for index in range(7):
        rows_total = proj_dims()[index][0]
        grad_lower = grads[index][0]
        placed = lax.dynamic_update_slice_in_dim(
            jnp.zeros((rows_total, RANK), jnp.float32),
            grad_lower,
            model_index * grad_lower.shape[0],
            0,
        )
        pieces.append(placed.reshape(-1))
    for index in range(7):
        pieces.append(grads[index][1].reshape(-1))
    for index in range(7):
        pieces.append(grads[index][2])
    blocks = jnp.concatenate(pieces).reshape(-1, BLOCK)
    buffer = jnp.zeros((capacity * everyone, BLOCK), jnp.float32).at[slot_index].set(blocks)
    owned = lax.psum_scatter(buffer, ("dp", "mp"), scatter_dimension=0, tiled=True)
    slot_block = (
        jnp.full((capacity * everyone,), -1, jnp.int32)
        .at[slot_index]
        .set(jnp.arange(blocks.shape[0], dtype=jnp.int32))
    )
    local_blocks = lax.dynamic_slice_in_dim(
        slot_block, lax.axis_index(("dp", "mp")) * capacity, capacity, 0
    )
    new_master, new_first, new_second = adam_update(
        master, owned, first_moment, second_moment, block_rates(local_blocks)
    )
    return (layer_out, input_grad, new_master, new_first, new_second)


f32 = jnp.float32
bf16 = jnp.bfloat16
VM = pl.BlockSpec(memory_space=pltpu.VMEM)
SM = pl.BlockSpec(memory_space=pltpu.SMEM)
ANY = pl.BlockSpec(memory_space=pl.ANY)
HBM = pl.BlockSpec(memory_space=pltpu.HBM)
TILE = 128
CHUNK = 256
N_DP = 4
N_MP = 8
N_Z = 4
WIDE = 768
FILL = 64


def mm(left, right):
    return lax.dot_general(left, right, (((1,), (0,)), ((), ())), preferred_element_type=f32)


def mm_t(left, right):
    return lax.dot_general(left, right, (((1,), (1,)), ((), ())), preferred_element_type=f32)


def mm_f(left, right):
    return lax.dot_general(left, right, (((0,), (0,)), ((), ())), preferred_element_type=f32)


def halves(value):
    high = value.astype(bf16)
    return high, (value - high.astype(f32)).astype(bf16)


def mm2(left, right):
    high, low = halves(left)
    return mm(high, right) + mm(low, right)


def mm2_t(left, right):
    high, low = halves(left)
    return mm_t(high, right) + mm_t(low, right)


def mm2_f(left, right):
    high, low = halves(left)
    return mm_f(high, right) + mm_f(low, right)


def swap64(value):
    return pltpu.roll(value, 64, 1)


def low_lanes(rows):
    return lax.broadcasted_iota(jnp.int32, (rows, TILE), 1) < 64


def merge(first, second):
    low = low_lanes(first.shape[0])
    return (
        jnp.where(low, first, swap64(second)),
        jnp.where(low, swap64(first), second),
    )


def tile(value, index):
    return value[:, index * TILE : (index + 1) * TILE]


def to_dp_order(value):
    out = [None] * 16
    for core in range(2):
        for pair in range(2):
            for part in range(2):
                first = 8 * pair + 2 * core + part
                low, high = merge(tile(value, first), tile(value, first + 4))
                out[8 * part + 2 * core + pair] = low
                out[8 * part + 4 + 2 * core + pair] = high
    return jnp.concatenate(out, axis=1)


def to_mp_order(value):
    out = [None] * 16
    for core in range(2):
        for pair in range(2):
            for part in range(2):
                first = 8 * part + 2 * core + pair
                low, high = merge(tile(value, first), tile(value, first + 4))
                out[8 * pair + 2 * core + part] = low
                out[8 * pair + 2 * core + part + 4] = high
    return jnp.concatenate(out, axis=1)


def shape_of(shape, dtype):
    return jax.ShapeDtypeStruct(shape, dtype)


def run(kernel, ins, specs, outs, scratch=(), name=None, after=(), megabytes=4, us=1.0):
    n_in, n_after = len(ins), len(after)

    def body(*refs):
        kernel(*refs[:n_in], *refs[n_in + n_after :])

    kinds = {"s": SM, "v": VM, "h": VM, "r": ANY}
    return pl.pallas_call(
        body,
        out_shape=list(outs),
        in_specs=[kinds[kind] for kind in specs] + [ANY] * n_after,
        out_specs=[VM] * len(outs),
        scratch_shapes=list(scratch),
        compiler_params=pltpu.CompilerParams(vmem_limit_bytes=megabytes * 2**20),
        cost_estimate=pl.CostEstimate(flops=int(us * 10**9), bytes_accessed=int(us * 10**6), transcendentals=0),
        name=name,
    )(*ins, *after)


def at(index, unit):
    return pl.ds(pl.multiple_of(index * unit, unit), unit)


def first_norm_kernel(tokens, gains, out):
    value = tokens[...].astype(f32)
    inverse = lax.rsqrt(jnp.mean(value * value, axis=-1, keepdims=True) + norm_eps)
    out[...] = to_dp_order(value * inverse * gains[0:1, :]).astype(bf16)


def line_kernel(step, where, p0, p1, p2, p3, out, forward):
    width = out.shape[2]
    for index, piece in enumerate((p0, p1, p2, p3)):
        rows = at(jnp.bitwise_xor(where[2], index), 64)
        for result, core in ((out, where[3]), (forward, 1 - where[3])):
            lanes = pl.ds(pl.multiple_of(core * step, TILE), width)
            result[:, rows, :] = piece[:, :, lanes]


def stack_kernel(first, second, out):
    out[0] = first[...]
    out[1] = second[...]


def join_all_kernel(p0, p1, p2, p3, p4, p5, first, second):
    for out, pieces in ((first, (p0, p1, p2)), (second, (p3, p4, p5))):
        begin = 0
        for piece in pieces:
            out[begin : begin + piece.shape[0]] = piece[...]
            begin += piece.shape[0]


def thirds(first, second):
    parts = []
    for value in (first, second):
        for _ in range(3):
            part = value.astype(bf16).astype(f32)
            parts.append(part)
            value = value - part
    parts += [jnp.zeros_like(first)] * 2
    return jnp.concatenate(parts, axis=0).astype(bf16)


def from_thirds(rows):
    value = rows.astype(f32)
    return [value[k : k + 1] + value[k + 1 : k + 2] + value[k + 2 : k + 3] for k in (0, 3)]


def eight(a, ax, y2, b, by, x2):
    return [
        lambda p: a[p],
        lambda p: ax[p],
        lambda p: y2[0, p],
        lambda p: y2[1, p],
        lambda p: b[p],
        lambda p: by[p],
        lambda p: x2[0, p],
        lambda p: x2[1, p],
    ]


def order_matrix():
    rows = lax.broadcasted_iota(jnp.int32, (BLOCK, BLOCK), 0)
    cols = lax.broadcasted_iota(jnp.int32, (BLOCK, BLOCK), 1)
    target = jnp.bitwise_and(rows, RANK - 1) * (BLOCK // RANK) + jnp.right_shift(rows, 4)
    return jnp.where(cols == target, 1.0, 0.0).astype(bf16)


def pick(indices, pieces):
    total = None
    first = 0
    for piece in pieces:
        rows = piece.shape[0]
        lanes = lax.broadcasted_iota(jnp.int32, (indices.shape[0], rows), 1) + first
        part = mm(jnp.where(lanes == indices, 1.0, 0.0).astype(bf16), piece[...])
        total = part if total is None else total + part
        first += rows
    return total


def adapters_kernel(even_at, odd_at, flat_at, *rest):
    pieces, (out, out_m, tiles) = rest[:-3], rest[-3:]
    order = order_matrix()
    even = mm(pick(even_at[...], pieces).astype(bf16), order)
    odd = mm(pick(odd_at[...], pieces).astype(bf16), order)
    for part in range(8):
        low, high = merge(tile(even, part), tile(odd, part))
        tiles[:, part, :] = low
        tiles[:, 8 + part, :] = high
    for index in range(out.shape[1] // TILE):
        out[:, index * TILE : (index + 1) * TILE] = tiles[index].astype(bf16)
    flat = pick(flat_at[...], pieces)
    for index in range(out_m.shape[1] // BLOCK):
        out_m[0:1, index * BLOCK : (index + 1) * BLOCK] = flat[index : index + 1, :]


def column_norm(weights, lowers, uppers):
    joined = weights.astype(f32) + dora_scale * mm_f(lowers, uppers)
    return jnp.sum(joined * joined, axis=0, keepdims=True)


def split_rows(where, part, send, keep, share):
    core = where[3]
    for line in range(N_Z):
        send[line * share : (line + 1) * share] = part[at(2 * line + 1 - core, share)].astype(bf16)
    for line in range(N_Z):
        keep[line * share : (line + 1) * share] = part[at(2 * line + core, share)]


def attention_kernel(spans, where, x, b0, b1, b2, b3, b4, b5, w_out, flat, mags, cos, sin, seg_row, seg_col, squares,
                     send, keep, mixed, qkv, probs, att, low_qkv, low_out, stats, part):
    blocks = eight(b0, b1, b2, b3, b4, b5)
    width = CHUNK
    rows = x.shape[0]
    la = [spans[("A", p)][0] for p in range(3)]
    lb = [spans[("B", p)][0] for p in range(3)]
    allowed = seg_col[...] == seg_row[...]
    t_index = lax.broadcasted_iota(jnp.int32, (rows, rows), 0)
    s_index = lax.broadcasted_iota(jnp.int32, (rows, rows), 1)
    allowed = jnp.logical_and(allowed, s_index <= t_index)
    for p in range(3):
        upper = flat[:, lb[p] : lb[p] + width]
        low = mm_t(x[...], flat[:, la[p] : la[p] + D])
        total = dora_scale * mm2(low, upper)
        square = jnp.zeros((1, width), f32)
        for index, block in enumerate(blocks):
            chunk = where[4 + index]
            weights = block(p)
            total += mm(x[:, at(chunk, CHUNK)], weights)
            lowers = flat[:, pl.ds(pl.multiple_of(la[p] + chunk * CHUNK, TILE), CHUNK)]
            square += column_norm(weights, lowers, upper)
        norm = jnp.sqrt(square + column_eps)
        magnitude = mags[:, pl.ds(pl.multiple_of(p * D + where[1] * width, TILE), width)]
        scale = magnitude / norm
        lanes = slice(p * width, (p + 1) * width)
        mixed[:, lanes] = total
        low_qkv[:, p * RANK : (p + 1) * RANK] = low
        stats[0:1, lanes] = scale
        stats[1:2, lanes] = norm
        stats[2:3, lanes] = magnitude
        value = total * scale
        for head in range(width // HEAD_DIM):
            one = value[:, head * HEAD_DIM : (head + 1) * HEAD_DIM]
            if p < 2:
                one = one * cos[...] + swap64(one) * sin[...]
            begin = p * width + head * HEAD_DIM
            qkv[:, begin : begin + HEAD_DIM] = one.astype(bf16)
    for head in range(width // HEAD_DIM):
        lanes = slice(head * HEAD_DIM, (head + 1) * HEAD_DIM)
        query = qkv[:, lanes]
        keys = qkv[:, width + head * HEAD_DIM : width + (head + 1) * HEAD_DIM]
        value = qkv[:, 2 * width + head * HEAD_DIM : 2 * width + (head + 1) * HEAD_DIM]
        scores = mm_t(query, keys) * HEAD_DIM ** (-0.5)
        scores = jnp.where(allowed, scores, -1e30)
        expd = jnp.exp(scores - jnp.max(scores, axis=-1, keepdims=True))
        weights = expd / jnp.sum(expd, axis=-1, keepdims=True)
        probs[head] = weights
        att[:, lanes] = mm(weights.astype(bf16), value).astype(bf16)
    a_out, b_out = spans[("A", 3)][0], spans[("B", 3)][0]
    low = mm_t(att[...], flat[:, a_out : a_out + width])
    low_out[...] = low
    part[...] = mm(att[...], w_out[...]) + dora_scale * mm2(low, flat[:, b_out : b_out + D])
    split_rows(where, part, send, keep, keep.shape[0] // N_Z)
    send[keep.shape[0] :] = thirds(squares[0:1], squares[1:2])


def pair_kernel(where, keep, received, p1, p2, p3, own):
    share = own.shape[0]

    def line(index):
        rows = at(index, share)
        return keep[rows] + received[rows].astype(f32)

    own[...] = line(where[2])
    for step, piece in ((1, p1), (2, p2), (3, p3)):
        piece[...] = line(jnp.bitwise_xor(where[2], step)).astype(bf16)


def pair_more_kernel(where, keep, received, squares, p1, p2, p3, own, more):
    share = own.shape[0]

    def line(index):
        rows = at(index, share)
        return keep[rows] + received[rows].astype(f32)

    own[...] = line(where[2])
    first, second = from_thirds(received[keep.shape[0] :])
    first, second = first + squares[0:1], second + squares[1:2]
    more[0:1], more[1:2] = first, second
    rows = thirds(first, second)
    for step, piece in ((1, p1), (2, p2), (3, p3)):
        piece[0:share] = line(jnp.bitwise_xor(where[2], step)).astype(bf16)
        piece[share:] = rows


def total_of(own, r1, r2, r3):
    return own[...] + r1[...].astype(f32) + r2[...].astype(f32) + r3[...].astype(f32)


def second_norm_kernel(own, more, r1, r2, r3, tokens, gains, mags, x_two, mixed, out, scale_o, norm_o, scale_d, norm_d):
    share = own.shape[0]
    total = own[...]
    squares = [more[0:1], more[1:2]]
    for piece in (r1, r2, r3):
        total = total + piece[0:share].astype(f32)
        for row, value in enumerate(from_thirds(piece[share:])):
            squares[row] = squares[row] + value
    for square, begin, scale, norm in (
        (squares[0], 3 * D, scale_o, norm_o),
        (squares[1], 4 * D + 2 * FF, scale_d, norm_d),
    ):
        value = jnp.sqrt(square + column_eps)
        norm[...] = value
        scale[...] = mags[:, begin : begin + D] / value
    mixed[...] = total
    value = tokens[...].astype(f32) + total * scale_o[...]
    x_two[...] = value
    inverse = lax.rsqrt(jnp.mean(value * value, axis=-1, keepdims=True) + norm_eps)
    out[...] = to_dp_order(value * inverse * gains[1:2, :]).astype(bf16)


def join_rows(where, pieces, out):
    share = out.shape[0] // N_MP
    for index, piece in enumerate(pieces):
        line = jnp.bitwise_xor(where[2], index % N_Z)
        core = where[3] if index < N_Z else 1 - where[3]
        out[at(2 * line + core, share)] = piece[0:share].astype(out.dtype)


def join_kernel(where, p0, p1, p2, p3, p4, p5, p6, p7, input_grad, layer_out):
    share = layer_out.shape[0] // N_MP
    pieces = (p0, p1, p2, p3, p4, p5, p6, p7)
    join_rows(where, pieces, input_grad)
    join_rows(where, [piece.at[share : 2 * share] for piece in pieces], layer_out)


def wide_squares(spans, where, blocks, chunks, flat):
    squares = []
    for p in range(2):
        a, b = spans[("A", 4 + p)][0], spans[("B", 4 + p)][0]
        square = jnp.zeros((1, WIDE), f32)
        for index, block in zip(chunks, blocks):
            begin = pl.multiple_of(a + where[4 + index] * CHUNK, TILE)
            square += column_norm(block(p), flat[:, pl.ds(begin, CHUNK)], flat[:, b : b + WIDE])
        squares.append(square)
    return jnp.concatenate(squares, axis=1)


def wide_first_kernel(spans, where, a, ax, b, by, flat, squares):
    blocks = eight(a, ax, None, b, by, None)
    squares[...] = wide_squares(spans, where, [blocks[k] for k in (0, 1, 4, 5)], (0, 1, 4, 5), flat)


def wide_norm_kernel(spans, where, y2, x2, flat, mags, squares, stats):
    blocks = eight(None, None, y2, None, None, x2)
    total = squares[...] + wide_squares(spans, where, [blocks[k] for k in (2, 3, 6, 7)], (2, 3, 6, 7), flat)
    for p in range(2):
        lanes = slice(p * WIDE, (p + 1) * WIDE)
        norm = jnp.sqrt(total[:, lanes] + column_eps)
        first = 4 * D + p * FF + where[2] * (2 * FF // N_MP) + where[3] * (WIDE - TILE)
        magnitude = mags[:, pl.ds(pl.multiple_of(first, TILE), WIDE)]
        stats[0:1, lanes] = magnitude / norm
        stats[1:2, lanes] = norm
        stats[2:3, lanes] = magnitude


def row_norm_kernel(spans, w_out, w_down, flat, squares):
    for row, (p, weights) in enumerate(((3, w_out[...]), (6, w_down[...]))):
        a, size = spans[("A", p)]
        b = spans[("B", p)][0]
        squares[row : row + 1, :] = column_norm(weights, flat[:, a : a + size], flat[:, b : b + D])


def down_back_kernel(spans, where, cotangent, scale, w_down, flat, d_act, grad_b, through, padded):
    a, size = spans[("A", 6)]
    b = spans[("B", 6)][0]
    grad = (cotangent[...].astype(f32) * scale[...]).astype(bf16)
    grad_b[...] = grad
    low = dora_scale * mm_t(grad, flat[:, b : b + D])
    through[...] = low
    padded[...] = jnp.zeros_like(padded)
    padded[:, 0:size] = mm_t(grad, w_down[...]) + mm2(low, flat[:, a : a + size])
    value = padded[...]
    d_act[...] = jnp.where(where[3] == 0, value, pltpu.roll(value, FILL, 1))


def middle_kernel(spans, where, p0, p1, p2, p3, p4, p5, p6, p7, b0, b1, b2, b3, b4, b5, d_act, flat, stats,
                  send, keep, x, act, grads, throughs, lows, dots, part, mixed):
    blocks = eight(b0, b1, b2, b3, b4, b5)
    join_rows(where, (p0, p1, p2, p3, p4, p5, p6, p7), x)
    for p in range(2):
        a, b = spans[("A", 4 + p)][0], spans[("B", 4 + p)][0]
        low = mm_t(x[...], flat[:, a : a + D])
        lows[:, p * RANK : (p + 1) * RANK] = low
        total = dora_scale * mm2(low, flat[:, b : b + WIDE])
        for index, block in enumerate(blocks):
            total += mm(x[:, at(where[4 + index], CHUNK)], block(p))
        mixed[:, p * WIDE : (p + 1) * WIDE] = total
    lanes = lax.broadcasted_iota(jnp.int32, d_act.shape, 1) - where[3] * FILL
    used = jnp.logical_and(lanes >= 0, lanes < WIDE - FILL)
    gate = mixed[:, :WIDE] * stats[0:1, :WIDE]
    upward = mixed[:, WIDE:] * stats[0:1, WIDE:]
    sigmoid_gate = jax.nn.sigmoid(gate)
    silu = gate * sigmoid_gate
    act[...] = jnp.where(used, silu * upward, 0.0).astype(bf16)
    back = jnp.where(used, d_act[...], 0.0)
    grad = back * upward * sigmoid_gate * (1.0 + gate * (1.0 - sigmoid_gate))
    dots[0:1, :WIDE] = jnp.sum(grad * mixed[:, :WIDE], axis=0, keepdims=True)
    grads[:, :WIDE] = (grad * stats[0:1, :WIDE]).astype(bf16)
    grad = back * silu
    dots[0:1, WIDE:] = jnp.sum(grad * mixed[:, WIDE:], axis=0, keepdims=True)
    grads[:, WIDE:] = (grad * stats[0:1, WIDE:]).astype(bf16)
    through = []
    for p in range(2):
        b = spans[("B", 4 + p)][0]
        low = dora_scale * mm_t(grads[:, p * WIDE : (p + 1) * WIDE], flat[:, b : b + WIDE])
        throughs[:, p * RANK : (p + 1) * RANK] = low
        through.append(halves(low))
    for index, block in enumerate(blocks):
        chunk = where[4 + index]
        total = None
        for p in range(2):
            a = spans[("A", 4 + p)][0]
            lowers = flat[:, pl.ds(pl.multiple_of(a + chunk * CHUNK, TILE), CHUNK)]
            one = mm_t(grads[:, p * WIDE : (p + 1) * WIDE], block(p))
            one += mm(through[p][0], lowers) + mm(through[p][1], lowers)
            total = one if total is None else total + one
        part[:, at(chunk, CHUNK)] = total
    split_rows(where, part, send, keep, send.shape[0] // N_Z)


def down_kernel(spans, where, act, w_down, flat, cotangent, send, keep, low_out, dots, part, local):
    a, size = spans[("A", 6)]
    b = spans[("B", 6)][0]
    value = act[...].astype(f32)
    value = jnp.where(where[3] == 0, value, pltpu.roll(value, WIDE - FILL, 1))
    local[...] = value.astype(bf16)
    inputs = local[:, 0:size]
    low = mm_t(inputs, flat[:, a : a + size])
    low_out[...] = low
    part[...] = mm(inputs, w_down[...]) + dora_scale * mm2(low, flat[:, b : b + D])
    split_rows(where, part, send, keep, send.shape[0] // N_Z)
    dots[...] = jnp.sum(cotangent[...].astype(f32) * part[...], axis=0, keepdims=True)


def norm_back(value, grad, gain):
    inverse = lax.rsqrt(jnp.mean(value * value, axis=-1, keepdims=True) + norm_eps)
    scaled = grad * gain
    inner = jnp.mean(scaled * value, axis=-1, keepdims=True)
    return inverse * (scaled - value * inverse * inverse * inner)


def second_back_kernel(own, r1, r2, r3, x_two, mixed, cotangent, gains, scale, dots_d, grad_two, grad_b, dots):
    total = to_mp_order(total_of(own, r1, r2, r3))
    grad = cotangent[...].astype(f32) + norm_back(x_two[...], total, gains[1:2, :])
    grad_two[...] = grad
    grad_b[0 : grad.shape[0]] = (grad * scale[...]).astype(bf16)
    own = jnp.sum(grad * mixed[...], axis=0, keepdims=True)
    dots[...] = own
    grad_b[grad.shape[0] :] = thirds(own, dots_d[...])


def last_rows_kernel(own, r1, r2, r3, tokens, grad_two, gains, own_d, d1, d2, d3, x_two, scale, out):
    share = own.shape[0]
    total = to_mp_order(total_of(own, r1, r2, r3))
    value = tokens[...].astype(f32)
    out[0:share] = (grad_two[...] + norm_back(value, total, gains[0:1, :])).astype(bf16)
    out[share:] = (x_two[...] + total_of(own_d, d1, d2, d3) * scale[...]).astype(bf16)


def attention_back_kernel(spans, where, p0, p1, p2, p3, p4, p5, p6, p7, b0, b1, b2, b3, b4, b5, w_out, flat,
                          cos, sin, mixed, qkv, probs, stats,
                          send, keep, grad_out, grads, throughs, through_out, dots, dots_o, dots_d, part, incoming):
    blocks = eight(b0, b1, b2, b3, b4, b5)
    width = CHUNK
    join_rows(where, (p0, p1, p2, p3, p4, p5, p6, p7), grad_out)
    sums = [jnp.zeros((1, D), f32)] * 2
    for piece in (p0, p1, p2, p3, p4, p5, p6, p7):
        for index, value in enumerate(from_thirds(piece[grad_out.shape[0] // N_MP :])):
            sums[index] = sums[index] + value
    dots_o[...], dots_d[...] = sums
    a, b = spans[("A", 3)][0], spans[("B", 3)][0]
    low = dora_scale * mm_t(grad_out[...], flat[:, b : b + D])
    through_out[...] = low
    grad_att = (mm_t(grad_out[...], w_out[...]) + mm2(low, flat[:, a : a + width])).astype(bf16)
    for head in range(width // HEAD_DIM):
        lanes = [slice(p * width + head * HEAD_DIM, p * width + (head + 1) * HEAD_DIM) for p in range(3)]
        query, keys, value = [qkv[:, one] for one in lanes]
        grad = grad_att[:, head * HEAD_DIM : (head + 1) * HEAD_DIM]
        weights = probs[head]
        grad_weights = mm_t(grad, value)
        incoming[:, lanes[2]] = mm_f(weights.astype(bf16), grad)
        centred = jnp.sum(weights * grad_weights, axis=-1, keepdims=True)
        grad_scores = (weights * (grad_weights - centred)).astype(bf16)
        grad_query = mm(grad_scores, keys) * HEAD_DIM ** (-0.5)
        grad_key = mm_f(grad_scores, query) * HEAD_DIM ** (-0.5)
        incoming[:, lanes[0]] = grad_query * cos[...] - swap64(grad_query) * sin[...]
        incoming[:, lanes[1]] = grad_key * cos[...] - swap64(grad_key) * sin[...]
    dots[...] = jnp.sum(incoming[...] * mixed[...], axis=0, keepdims=True)
    grads[...] = (incoming[...] * stats[0:1, :]).astype(bf16)
    through = []
    for p in range(3):
        b = spans[("B", p)][0]
        low = dora_scale * mm_t(grads[:, p * width : (p + 1) * width], flat[:, b : b + width])
        throughs[:, p * RANK : (p + 1) * RANK] = low
        through.append(halves(low))
    for index, block in enumerate(blocks):
        chunk = where[4 + index]
        total = None
        for p in range(3):
            a = spans[("A", p)][0]
            lowers = flat[:, pl.ds(pl.multiple_of(a + chunk * CHUNK, TILE), CHUNK)]
            one = mm_t(grads[:, p * width : (p + 1) * width], block(p))
            one += mm(through[p][0], lowers) + mm(through[p][1], lowers)
            total = one if total is None else total + one
        part[:, at(chunk, CHUNK)] = total
    split_rows(where, part, send, keep, send.shape[0] // N_Z)


def to_blocks(value, tiles, out, begin):
    pairs = value.shape[1] // TILE
    for index in range(pairs):
        tiles[index] = tile(value, index)
    for part in range(8):
        even, odd = merge(tiles[0:pairs, part, :], tiles[0:pairs, 8 + part, :])
        lanes = slice(part * TILE, (part + 1) * TILE)
        out[begin : begin + pairs, lanes] = even
        out[begin + pairs : begin + 2 * pairs, lanes] = odd


def column_grads_kernel(spans, projections, width, where, x, b0, b1, b2, b3, b4, b5, flat, stats, grads, throughs,
                        lows, dots, out_a, out_b, out_m, tiles, whole):
    blocks = eight(b0, b1, b2, b3, b4, b5)
    for position, p in enumerate(projections):
        a, b = spans[("A", p)][0], spans[("B", p)][0]
        lanes = slice(position * width, (position + 1) * width)
        ranks = slice(position * RANK, (position + 1) * RANK)
        upper = flat[:, b : b + width]
        norm = stats[1:2, lanes]
        inverse = 1.0 / norm
        e = dots[0:1, lanes]
        out_m[0:1, lanes] = e * inverse
        ratio = -e * stats[2:3, lanes] * inverse * inverse * inverse
        scaled = halves(dora_scale * upper.astype(f32) * ratio)
        through = halves(throughs[:, ranks])
        square = dora_scale * (mm_t(scaled[0], upper) + mm_t(scaled[1], upper))
        lower = flat[:, a : a + D]
        whole[...] = mm2(square, lower) + mm_f(through[0], x[...]) + mm_f(through[1], x[...])
        crossed = dora_scale * mm2(mm_t(lower, lower), upper)
        for index, block in enumerate(blocks):
            chunk = where[4 + index]
            weights = block(position)
            whole[:, at(chunk, CHUNK)] += mm_t(scaled[0], weights) + mm_t(scaled[1], weights)
            crossed += mm(flat[:, pl.ds(pl.multiple_of(a + chunk * CHUNK, TILE), CHUNK)], weights)
        to_blocks(whole[...], tiles, out_a, position * D * RANK // BLOCK)
        upper_grad = dora_scale * (mm2_f(lows[:, ranks], grads[:, lanes]) + crossed * ratio)
        to_blocks(upper_grad, tiles, out_b, position * width * RANK // BLOCK)


def row_grads_kernel(spans, p, where, x, weights_ref, flat, scale_row, norm_row, mag_row, grads, through_in, low, dots,
                     out_a, out_b, tiles, local):
    a, size = spans[("A", p)]
    b = spans[("B", p)][0]
    weights = weights_ref[...]
    inputs = x[...]
    if p == 6:
        value = inputs.astype(f32)
        value = jnp.where(where[3] == 0, value, pltpu.roll(value, WIDE - FILL, 1))
        local[...] = value.astype(bf16)
        inputs = local[:, 0:size]
    lower = flat[:, a : a + size]
    upper = flat[:, b : b + D]
    inverse = 1.0 / norm_row[...]
    ratio = -dots[...] * mag_row[...] * inverse * inverse * inverse
    scaled = halves(dora_scale * upper.astype(f32) * ratio)
    square = dora_scale * (mm_t(scaled[0], upper) + mm_t(scaled[1], upper))
    grad = mm2(square, lower) + mm2_f(through_in[...], inputs)
    grad += mm_t(scaled[0], weights) + mm_t(scaled[1], weights)
    if size % TILE:
        grad = jnp.concatenate([grad, jnp.zeros((RANK, TILE - size % TILE), f32)], axis=1)
    to_blocks(grad, tiles, out_a, 0)
    crossed = mm(lower, weights) + dora_scale * mm2(mm_t(lower, lower), upper)
    to_blocks(dora_scale * (mm2_f(low[...], grads[...]) + crossed * ratio), tiles, out_b, 0)


def pack_kernel(where, a_f, a_a, b_d, b_o, m_f, m_a, dots_o, norm_o, dots_d, norm_d, give, keep, rows, flat):
    begin = 0
    for array in (a_f, a_a, b_d, b_o):
        rows[begin : begin + array.shape[0]] = array[...]
        begin += array.shape[0]
    flat[...] = jnp.zeros_like(flat)
    for p in range(3):
        lanes = pl.ds(pl.multiple_of(p * D + where[1] * CHUNK, TILE), CHUNK)
        flat[:, lanes] = m_a[:, p * CHUNK : (p + 1) * CHUNK]
    flat[:, 3 * D : 4 * D] = dots_o[...] / norm_o[...]
    for p in range(2):
        first = 4 * D + p * FF + where[2] * (2 * FF // N_MP) + where[3] * (WIDE - TILE)
        flat[:, pl.ds(pl.multiple_of(first, TILE), WIDE)] = m_f[:, p * WIDE : (p + 1) * WIDE]
    flat[:, 4 * D + 2 * FF :] = dots_d[...] / norm_d[...]
    rows[begin:] = jnp.zeros((rows.shape[0] - begin, BLOCK), f32)
    for index in range(flat.shape[1] // BLOCK):
        rows[begin + index : begin + index + 1] = flat[:, index * BLOCK : (index + 1) * BLOCK]
    unit = rows.shape[0] // N_MP
    for line in range(N_Z):
        give[line * unit : (line + 1) * unit] = rows[at(2 * line + 1 - where[3], unit)].astype(bf16)
        keep[line * unit : (line + 1) * unit] = rows[at(2 * line + where[3], unit)]


def local_kernel(where, own, r1, r2, r3, b_f, b_a, a_d, a_o, mine, p1, p2, p3, rows):
    begin = own.shape[0]
    rows[0:begin] = total_of(own, r1, r2, r3)
    for array in (b_f, b_a, a_d, a_o):
        rows[begin : begin + array.shape[0]] = array[...]
        begin += array.shape[0]
    rows[begin:] = jnp.zeros((rows.shape[0] - begin, BLOCK), f32)
    part = mine.shape[0]
    mine[...] = rows[at(where[0], part)]
    for step, piece in ((1, p1), (2, p2), (3, p3)):
        piece[...] = rows[at(jnp.bitwise_xor(where[0], step), part)].astype(bf16)


def last_sum_kernel(own, r1, r2, r3, out):
    out[...] = total_of(own, r1, r2, r3).astype(bf16)


def update_kernel(index, mine, s0, s1, s2, s3, s4, s5, s6, s7, master, first, second, new_master, new_first, new_second):
    picked = pick(index[...], (s0, s1, s2, s3, s4, s5, s6, s7)).astype(bf16)
    grad = jnp.where(mine[...] >= COUNT_FLAT, picked.astype(f32), mm_t(picked, order_matrix()))
    grad = jnp.where(mine[...] >= 0, grad, 0.0)
    rates = jnp.where(mine[...] < COUNT_FLAT, rate_upper, rate_magnitude)
    rates = jnp.where(mine[...] < COUNT_LOWER, rate_lower, rates)
    rates = jnp.where(mine[...] < 0, 0.0, rates)
    weight = master[...]
    first_new = beta_one * first[...] + (1.0 - beta_one) * grad
    second_new = beta_two * second[...] + (1.0 - beta_two) * grad * grad
    first_hat = first_new / (1.0 - beta_one**STEP)
    second_hat = second_new / (1.0 - beta_two**STEP)
    new_master[...] = weight - rates * (
        first_hat / (jnp.sqrt(second_hat) + adam_eps) + weight_decay * weight
    )
    new_first[...] = first_new
    new_second[...] = second_new


COUNT_LOWER = RANK * (6 * D + FF) // BLOCK
COUNT_FLAT = COUNT_LOWER + RANK * (5 * D + 2 * FF) // BLOCK


def block_starts():
    starts = {}
    total = 0
    for kind, side in (("A", 0), ("B", 1)):
        for index, sizes in enumerate(proj_dims()):
            starts[(kind, index)] = total
            total += sizes[side] * RANK // BLOCK
    return starts


def fast_body(
    tokens,
    cotangent,
    norm_gains,
    w_attn,
    w_in,
    w_down,
    segments,
    owners,
    master,
    first_moment,
    second_moment,
):
    rows = tokens.shape[0]
    mi = lax.axis_index("mp")
    di = lax.axis_index("dp")
    core = mi % 2
    zi = mi // 2
    share = rows // N_MP
    capacity = master.shape[0]
    n_blocks = owners.shape[0]
    width = D // N_MP
    starts = block_starts()

    def mp_swap(values, step):
        return lax.ppermute(values, "mp", [(i, i ^ step) for i in range(N_MP)])

    def dp_swap(values, step):
        return lax.ppermute(values, "dp", [(i, i ^ step) for i in range(N_DP)])

    order = [(0, 0), (1, 0), (2, 0), (3, 0), (0, 1), (2, 1), (1, 1), (3, 1)]
    chunks = [(di ^ t) * 2 + (core ^ h) for t, h in order]
    where = jnp.stack([di, mi, zi, core] + chunks).astype(jnp.int32)

    def stack(first, second, after=()):
        shape = (2,) + first.shape
        return run(
            stack_kernel, [first, second], "hh", [shape_of(shape, bf16)], name="stack", after=after, us=0.6
        )[0]

    def plane_first(a, b):
        return a, dp_swap(a, 1), b, dp_swap(b, 2)

    def plane_second(a, ax, b, by, after=()):
        return [a, ax, dp_swap(stack(a, ax, after), 2), b, by, dp_swap(stack(b, by, after), 1)]

    def plane(a, b):
        return plane_second(*plane_first(a, b))

    sent = master.astype(bf16)
    line = [sent] + [mp_swap(sent, 2 * step) for step in range(1, N_Z)]
    first_b = plane_first(jnp.concatenate(line[:2]), jnp.concatenate(line[2:]))
    owners, segments, w_late, tokens, line_end = lax.optimization_barrier(
        (owners, segments, w_attn, tokens, first_b[2])
    )
    first_b = first_b[:2] + (line_end,) + first_b[3:]
    sheet = plane_second(*first_b)
    sheet = [one.reshape(-1, BLOCK) for one in sheet]
    features = run(
        first_norm_kernel,
        [tokens, norm_gains],
        "hh",
        [shape_of((rows, D), bf16)],
        name="first_norm",
        megabytes=6,
        us=1.2,
        after=[first_b[2]],
    )[0]
    def cut(weights, count, chip):
        pieces = []
        for index in range(N_Z):
            piece = lax.dynamic_slice(weights, (0, di * 64, (zi ^ index) * chip), (count, 64, chip))
            pieces.append(mp_swap(piece, 2 * index) if index else piece)
        return pieces

    def columns_of(pieces, size, step, name, after=()):
        count = pieces[0].shape[0]
        a, forward = run(
            functools.partial(line_kernel, step),
            [where] + pieces,
            "shhhh",
            [shape_of((count, CHUNK, size), bf16)] * 2,
            name=name,
            after=after,
        )
        return plane_first(a, mp_swap(forward, 1))

    first_a = columns_of(cut(w_attn, 3, 2 * width), width, width, "line_a", [features])
    blocks_a = plane_second(*first_a)
    sheet = run(
        join_all_kernel,
        sheet,
        "h" * 6,
        [shape_of((8 * capacity, BLOCK), bf16)] * 2,
        name="adapter_rows",
        after=[first_a[0]],
        us=0.1,
    )
    stacked = list(sheet) + [mp_swap(one, 1) for one in sheet]
    w_in_late, own_a = lax.optimization_barrier((w_in, first_a[0]))
    pieces_f = cut(w_in_late, 2, 2 * FF // N_MP)
    w_out = w_late[3]

    ranks = slot_positions(owners, 0)
    owner_d, owner_m = owners // N_MP, owners % N_MP
    piece_at = (owner_d ^ di) * N_Z + ((owner_m // 2) ^ zi)
    listed = np.array([0, 1, 8, 9, 2, 3, 12, 13, 4, 5, 10, 11, 6, 7, 14, 15], np.int32)
    piece_at = jnp.sum(jnp.where(piece_at[:, None] == np.arange(16), listed, 0), axis=1)
    slot = (((owner_m % 2) ^ core) * 16 + piece_at) * capacity + ranks
    wanted = []
    spans = {}

    def want(name, blocks, size):
        spans[name] = (sum(w.shape[0] for w in wanted) * 64, size)
        wanted.append(blocks)

    by_dp = np.array(
        [(2 * z + c) * 4 + d for d in range(N_DP) for c in range(2) for z in range(N_Z)], np.int32
    )
    all_blocks = np.arange(D * RANK // BLOCK, dtype=np.int32)
    for index in (0, 1, 2, 4, 5):
        want(("A", index), starts[("A", index)] + by_dp, D)
        if index < 3:
            want(("B", index), starts[("B", index)] + mi * 4 + np.arange(4), width)
        else:
            first_block = starts[("B", index)] + zi * 22 + core * 10
            want(("B", index), first_block + np.arange(12), WIDE)
    want(("A", 3), starts[("A", 3)] + mi * 4 + np.arange(4), width)
    want(("B", 3), starts[("B", 3)] + all_blocks, D)
    want(("A", 6), starts[("A", 6)] + mi * 11 + np.minimum(np.arange(12), 10), FF // N_MP)
    want(("B", 6), starts[("B", 6)] + all_blocks, D)
    chosen = jnp.take(slot, jnp.concatenate([jnp.asarray(w, jnp.int32) for w in wanted]))
    n_pairs = chosen.shape[0] // 2
    pairs = chosen.reshape(n_pairs, 2)
    flat, mags = run(
        adapters_kernel,
        [pairs[:, :1], pairs[:, 1:], slot[COUNT_FLAT:, None]] + stacked,
        "vvv" + "h" * len(stacked),
        [shape_of((RANK, n_pairs * TILE), bf16), shape_of((1, (n_blocks - COUNT_FLAT) * BLOCK), f32)],
        [pltpu.VMEM((n_pairs, RANK, TILE), f32)],
        name="adapters", megabytes=13, us=0.3,
    )

    def bind(kernel, *args):
        return functools.partial(kernel, spans, *args)

    def column_grads(projections, size, x, blocks, flat, stats, grads, throughs, lows, dots, after):
        count = len(projections)
        return run(
            bind(column_grads_kernel, projections, size),
            [where, x] + blocks + [flat, stats, grads, throughs, lows, dots],
            "s" + "h" * 13,
            [
                shape_of((count * D * RANK // BLOCK, BLOCK), f32),
                shape_of((count * size * RANK // BLOCK, BLOCK), f32),
                shape_of((1, count * size), f32),
            ],
            [pltpu.VMEM((D // TILE, RANK, TILE), f32), pltpu.VMEM((RANK, D), f32)],
            name="column_grads", megabytes=9, us=1,
            after=after,
        )

    def row_grads(p, x, weights, flat, scale, norm, mag, grads, through, low, dots, after):
        size = spans[("A", p)][1]
        return run(
            bind(row_grads_kernel, p),
            [where, x, weights, flat, scale, norm, mag, grads, through, low, dots],
            "s" + "h" * 10,
            [
                shape_of((-(-size // TILE) * 2, BLOCK), f32),
                shape_of((D * RANK // BLOCK, BLOCK), f32),
            ],
            [pltpu.VMEM((D // TILE, RANK, TILE), f32), pltpu.VMEM((rows, WIDE), bf16)],
            name="row_grads", megabytes=6, us=0.1,
            after=after,
        )

    row = segments[0]
    cosine, sine = rotary_tables(segment_positions(row))
    cosine, sine = cosine[:, 0], sine[:, 0]
    cos_full = jnp.concatenate([cosine, cosine], axis=-1)
    sin_full = jnp.concatenate([-sine, sine], axis=-1)
    tokens_here = lax.dynamic_slice_in_dim(tokens, mi * share, share, 0)
    cotangent_here = lax.dynamic_slice_in_dim(cotangent, mi * share, share, 0)
    half_rows = [shape_of((rows // 2, D), bf16), shape_of((rows // 2, D), f32)]

    def finish_rows(send, keep, after):
        received = mp_swap(send, 1)
        p1, p2, p3, own = run(
            pair_kernel,
            [where, keep, received],
            "shh",
            [shape_of((share, D), bf16)] * 3 + [shape_of((share, D), f32)],
            name="pair_sums", megabytes=4, us=1.2,
            after=after,
        )
        return [own, mp_swap(p1, 2), mp_swap(p2, 4), mp_swap(p3, 6)]

    def gather_rows(value):
        mine = [value] + [mp_swap(value, 2 * step) for step in range(1, N_Z)]
        return mine + [mp_swap(one, 1) for one in mine]

    squares = run(
        bind(row_norm_kernel),
        [w_out, w_down, flat],
        "hhh",
        [shape_of((2, D), f32)],
        name="row_norms",
        us=0.1,
    )[0]
    n_heads = width // HEAD_DIM
    send, keep, mixed_a, qkv, probs, att, low_a, low_o, stats_a = run(
        bind(attention_kernel),
        [where, features] + blocks_a + [w_out, flat, mags, cos_full, sin_full, segments, row[:, None], squares],
        "s" + "h" * 15,
        [shape_of((rows // 2 + 8, D), bf16), half_rows[1]]
        + [
            shape_of((rows, 3 * width), f32),
            shape_of((rows, 3 * width), bf16),
            shape_of((n_heads, rows, rows), f32),
            shape_of((rows, width), bf16),
            shape_of((rows, 3 * RANK), f32),
            shape_of((rows, RANK), f32),
            shape_of((8, 3 * width), f32),
        ],
        [pltpu.VMEM((rows, D), f32)],
        name="attention",
        megabytes=13,
        us=10,
    )

    p1, p2, p3, own_o, more_o = run(
        pair_more_kernel,
        [where, keep, mp_swap(send, 1), squares],
        "shhh",
        [shape_of((share + 8, D), bf16)] * 3 + [shape_of((share, D), f32), shape_of((2, D), f32)],
        name="pair_sums",
        us=1.2,
    )
    sums_o = [mp_swap(p1, 2), mp_swap(p2, 4), mp_swap(p3, 6)]
    first_f = columns_of(pieces_f, WIDE, WIDE - TILE, "line_f")
    blocks_f = plane_second(*first_f, after=sums_o)
    row_of = shape_of((1, D), f32)
    x_two, mixed_o, features_two, scale_o, norm_o, scale_d, norm_d = run(
        second_norm_kernel,
        [own_o, more_o] + sums_o + [tokens_here, norm_gains, mags],
        "h" * 8,
        [shape_of((share, D), f32)] * 2 + [shape_of((share, D), bf16)] + [row_of] * 4,
        name="second_norm",
        us=0.5,
    )
    mag_o = mags[:, 3 * D : 4 * D]
    mag_d = mags[:, 4 * D + 2 * FF :]
    pieces = gather_rows(features_two)
    squares_f = run(
        bind(wide_first_kernel),
        [where] + [blocks_f[k] for k in (0, 1, 3, 4)] + [flat],
        "s" + "h" * 5,
        [shape_of((1, 2 * WIDE), f32)],
        name="wide_squares", megabytes=8, us=3,
        after=[pieces[1]],
    )[0]
    d_act, grad_d, through_d = run(
        bind(down_back_kernel),
        [where, cotangent, scale_d, w_down, flat],
        "shhhh",
        [shape_of((rows, WIDE), f32), shape_of((rows, D), bf16), shape_of((rows, RANK), f32)],
        [pltpu.VMEM((rows, WIDE), f32)],
        name="down_back", megabytes=7, us=3.5,
        after=[squares_f],
    )
    stats_f = run(
        bind(wide_norm_kernel),
        [where] + [blocks_f[k] for k in (2, 5)] + [flat, mags, squares_f],
        "s" + "h" * 5,
        [shape_of((8, 2 * WIDE), f32)],
        name="wide_norms", megabytes=8, us=3,
        after=[through_d],
    )[0]
    send, keep, x_f, act, grads_f, through_f, low_f, dots_f = run(
        bind(middle_kernel),
        [where] + pieces + blocks_f + [d_act, flat, stats_f],
        "s" + "h" * 17,
        half_rows
        + [
            shape_of((rows, D), bf16),
            shape_of((rows, WIDE), bf16),
            shape_of((rows, 2 * WIDE), bf16),
            shape_of((rows, 2 * RANK), f32),
            shape_of((rows, 2 * RANK), f32),
            shape_of((1, 2 * WIDE), f32),
        ],
        [pltpu.VMEM((rows, D), f32), pltpu.VMEM((rows, 2 * WIDE), f32)],
        name="feed_forward", megabytes=22, us=14,
    )
    send_d, keep_d, low_d, dots_d = run(
        bind(down_kernel),
        [where, act, w_down, flat, cotangent],
        "shhhh",
        half_rows + [shape_of((rows, RANK), f32), shape_of((1, D), f32)],
        [pltpu.VMEM((rows, D), f32), pltpu.VMEM((rows, WIDE), bf16)],
        name="down", megabytes=9, us=3.5,
    )
    sums = finish_rows(send, keep, [low_d])
    a_f, b_f, m_f = column_grads(
        (4, 5), WIDE, x_f, blocks_f, flat, stats_f, grads_f, through_f, low_f, dots_f, [sums[1]]
    )
    grad_two, grad_o_piece, dots_o = run(
        second_back_kernel,
        sums + [x_two, mixed_o, cotangent_here, norm_gains, scale_o, dots_d],
        "h" * 10,
        [shape_of((share, D), f32), shape_of((share + 8, D), bf16), row_of],
        name="second_norm_back", megabytes=3, us=0.5,
        after=[m_f],
    )
    pieces_o = gather_rows(grad_o_piece)
    sums_d = finish_rows(send_d, keep_d, [pieces_o[0], pieces_o[7]])
    send, keep, grad_o, grads_a, through_a, through_o, dots_a, dots_all_o, dots_all_d = run(
        bind(attention_back_kernel),
        [where] + pieces_o + blocks_a + [w_out, flat, cos_full, sin_full, mixed_a, qkv, probs, stats_a],
        "s" + "h" * 22,
        half_rows
        + [
            shape_of((rows, D), bf16),
            shape_of((rows, 3 * width), bf16),
            shape_of((rows, 3 * RANK), f32),
            shape_of((rows, RANK), f32),
            shape_of((1, 3 * width), f32),
            row_of,
            row_of,
        ],
        [pltpu.VMEM((rows, D), f32), pltpu.VMEM((rows, 3 * width), f32)],
        name="attention_back",
        megabytes=10,
        us=0.1,
        after=[sums_d[0]],
    )
    a_o, b_o = row_grads(
        3, att, w_out, flat, scale_o, norm_o, mag_o, grad_o, through_o, low_o, dots_all_o, []
    )
    a_a, b_a, m_a = column_grads(
        (0, 1, 2), width, features, blocks_a, flat, stats_a, grads_a, through_a, low_a, dots_a, [a_o]
    )
    a_d, b_d = row_grads(
        6, act, w_down, flat, scale_d, norm_d, mag_d, grad_d, through_d, low_d, dots_all_d, [m_a]
    )
    unit, part = 32, 24
    give, kept = run(
        pack_kernel,
        [where, a_f, a_a, b_d, b_o, m_f, m_a, dots_o, norm_o, dots_d, norm_d],
        "s" + "h" * 10,
        [shape_of((N_Z * unit, BLOCK), bf16), shape_of((N_Z * unit, BLOCK), f32)],
        [pltpu.VMEM((N_MP * unit, BLOCK), f32), pltpu.VMEM((1, (n_blocks - COUNT_FLAT) * BLOCK), f32)],
        name="pack",
    )
    p1, p2, p3, own = run(
        pair_kernel,
        [where, kept, mp_swap(give, 1)],
        "shh",
        [shape_of((unit, BLOCK), bf16)] * 3 + [shape_of((unit, BLOCK), f32)],
        name="pack_sums",
        us=0.1,
    )
    sums = finish_rows(send, keep, [give])
    own, p1, p2, p3 = run(
        local_kernel,
        [where, own, mp_swap(p1, 2), mp_swap(p2, 4), mp_swap(p3, 6), b_f, b_a, a_d, a_o],
        "s" + "h" * 8,
        [shape_of((part, BLOCK), f32)] + [shape_of((part, BLOCK), bf16)] * 3,
        [pltpu.VMEM((N_DP * part, BLOCK), f32)],
        name="local_sums",
        us=0.1,
    )
    own = run(
        last_sum_kernel,
        [own, dp_swap(p1, 1), dp_swap(p2, 2), dp_swap(p3, 3)],
        "hhhh",
        [shape_of((part, BLOCK), bf16)],
        name="last_sums",
        us=0.1,
    )[0]
    last_piece = run(
        last_rows_kernel,
        sums + [tokens_here, grad_two, norm_gains] + sums_d + [x_two, scale_d],
        "h" * 13,
        [shape_of((2 * share, D), bf16)],
        name="last_rows",
        us=0.5,
    )[0]
    lines = jnp.concatenate([own] + [mp_swap(own, 2 * step) for step in range(1, N_Z)])
    summed = [lines] + [dp_swap(lines, step) for step in range(1, N_DP)]
    summed = summed + [mp_swap(one, 1) for one in summed]

    second = mp_swap(last_piece, 4)
    pieces = [last_piece, mp_swap(last_piece, 2), second, mp_swap(second, 2)]
    pieces = pieces + [mp_swap(one, 1) for one in pieces]
    input_grad, layer_out = run(
        join_kernel,
        [where] + pieces,
        "s" + "h" * 8,
        [shape_of((rows, D), f32), shape_of((rows, D), bf16)],
        name="join_rows",
        megabytes=8,
        us=4,
    )

    table = np.zeros((n_blocks,), np.int32)

    def note(block, m, r):
        table[block] = ((r // part) * N_MP + m) * 64 + r % part

    def split_pairs(count, r):
        return r // 2 + (r % 2) * (count // 2)

    def blocks_of(names):
        def listing(count, m):
            each = count // len(names)
            for position, blocks in enumerate(names):
                for k, block in enumerate(blocks(m)):
                    if block is not None:
                        yield position * each + split_pairs(each, k), block

        return listing

    def lower_columns(p):
        return lambda m: [starts[("A", p)] + int(k) for k in by_dp]

    def upper_rows(p):
        return lambda m: [starts[("B", p)] + int(k) for k in all_blocks]

    def lower_rows(p, per):
        return lambda m: [starts[("A", p)] + m * per + k for k in range(per)]

    def upper_columns(p):
        if p < 3:
            return lambda m: [starts[("B", p)] + m * 4 + k for k in range(4)]
        return lambda m: [
            starts[("B", p)] + (m // 2) * 22 + (m % 2) * 10 + k
            if (k < 11 if m % 2 == 0 else k >= 1)
            else None
            for k in range(12)
        ]

    begin = 0
    for listing, count in (
        (blocks_of([lower_columns(4), lower_columns(5)]), a_f.shape[0]),
        (blocks_of([lower_columns(p) for p in range(3)]), a_a.shape[0]),
        (blocks_of([upper_rows(6)]), b_d.shape[0]),
        (blocks_of([upper_rows(3)]), b_o.shape[0]),
        (lambda count, m: [(r, COUNT_FLAT + r) for r in range(count)], n_blocks - COUNT_FLAT),
    ):
        for r, block in listing(count, None):
            note(block, (begin + r) // unit, (begin + r) % unit)
        begin += count
    begin = unit
    for listing, count in (
        (blocks_of([upper_columns(4), upper_columns(5)]), b_f.shape[0]),
        (blocks_of([upper_columns(p) for p in range(3)]), b_a.shape[0]),
        (blocks_of([lower_rows(6, 11)]), a_d.shape[0]),
        (blocks_of([lower_rows(3, 4)]), a_o.shape[0]),
    ):
        for m in range(N_MP):
            for r, block in listing(count, m):
                note(block, m, begin + r)
        begin += count
    me = di * N_MP + mi
    hits = (owners * capacity + ranks)[None, :] == me * capacity + jnp.arange(capacity)[:, None]
    mine = jnp.sum(jnp.where(hits, jnp.arange(n_blocks)[None, :] + 1, 0), axis=1) - 1
    code = jnp.sum(jnp.where(hits, jnp.asarray(table)[None, :], 0), axis=1)
    device, inner = code // 64, code % 64
    d_from, m_from = device // N_MP, device % N_MP
    list_at = (((m_from % 2) ^ core) * N_DP + (d_from ^ di)) * N_Z + ((m_from // 2) ^ zi)
    index = list_at * part + inner
    new_master, new_first, new_second = run(
        update_kernel,
        [index[:, None], mine[:, None]] + summed + [master, first_moment, second_moment],
        "vv" + "h" * 11,
        [shape_of(master.shape, f32)] * 3,
        name="update", megabytes=4, us=2,
    )
    return (layer_out, input_grad, new_master, new_first, new_second)


def solution(mesh):
    fast = mesh.shape["dp"] == 4 and mesh.shape["mp"] == 8
    return jax.shard_map(
        fast_body if fast else body,
        mesh=mesh,
        in_specs=(
            P("dp", None),
            P("dp", None),
            P(),
            P(None, "mp", None),
            P(None, "mp", None),
            P("mp", None),
            P("dp", None),
            P(),
            P(("dp", "mp"), None),
            P(("dp", "mp"), None),
            P(("dp", "mp"), None),
        ),
        out_specs=(
            P("dp", None),
            P("dp", None),
            P(("dp", "mp"), None),
            P(("dp", "mp"), None),
            P(("dp", "mp"), None),
        ),
        check_vma=False,
    )
```

profile of v0, /device:TPU:1, one launch (start us, length us, event | category | flops | bytes accessed | tf_op | source)
XLA Modules:
  0.0 341.2 jit_solution(14687690753560812441)
XLA Ops:
  1.8 3.2 collective-permute-start
  11.7 2.9 collective-permute-start.4
  24.9 3.6 %collective-permute-start.7 = (bf16[3,256,256]{2,1,0:T(8,128)(2,1)S(1)}, bf16[3,256,256]{2,1,0:T(8,128)(2,1)S(1)}, u32[]{:S(2)}, u32[]{:S(2)}) collective-permute-start(bf16[3,256,256]{2,1,0:T(8,128)(2,1)S(1)} %get-tuple-element.107), channel_id=1, source_target_pairs={{0,1},{1,0},{2,3},{3,2},{4,5},{5,4},{6,7},{7,6},{8,9},{9,8},{10,11... | collective-permute-start | bytes 1179656 | tf_op jit(solution)/shard_map/ppermute | solution.py:1070
  30.9 2.2 gather_fusion
  35.4 2.2 constant_dynamic-slice_fusion.1
  37.6 3.1 collective-permute-start.28
  49.0 2.8 collective-permute-done.12
  57.2 2.5 collective-permute-start.15
  64.7 2.3 collective-permute-done.30.refs_4_
  71.5 5.2 %adapters.1 = (bf16[16,17664]{1,0:T(8,128)(2,1)S(1)}, f32[1,21504]{1,0:T(1,128)S(1)}) custom-call(s32[138,1]{1,0:T(8,128)S(1)} %get-tuple-element.216.refs_0_, s32[138,1]{1,0:T(8,128)S(1)} %get-tuple-element.215.refs_1_, s32[21,1]{1,0:T(8,128)S(1)} %copy-done.41, bf16[320,1024]{1,0:T(8,128)(2,1)} %get-tuple-element.110.refs_3_, ...), custom_call_target="tpu_custom_call" | custom-call | flops 300000000 | bytes 300000 | tf_op jit(solution)/shard_map/adapters/pallas_call | solution.py:475
  78.4 8.9 %attention.1 = (bf16[200,2048]{1,0:T(8,128)(2,1)S(1)}, f32[192,2048]{1,0:T(8,128)S(1)}, f32[384,768]{1,0:T(8,128)S(1)}, bf16[384,768]{1,0:T(8,128)(2,1)S(1)}, f3...) custom-call(s32[12]{0:T(128)S(1)} %stack.57.refs_0_, ...), custom_call_target="tpu_custom_call" | custom-call | flops 10000000000 | bytes 10000000 | tf_op jit(solution)/shard_map/attention/pallas_call | solution.py:475
  91.4 7.9 %collective-permute-start.18 = (bf16[56,2048]{1,0:T(8,128)(2,1)S(1)}, bf16[56,2048]{1,0:T(8,128)(2,1)S(1)}, u32[]{:S(2)}, u32[]{:S(2)}) collective-permute-start(bf16[56,2048]{1,0:T(8,128)(2,1)S(1)} %get-tuple-element.119), channel_id=1, source_target_pairs={{0,2},{1,3},{2,0},{3,1},{4,6},{5,7},{6,4},{7,5},{8,10},{9,11},{10,... | collective-permute-start | bytes 688136 | tf_op jit(solution)/shard_map/ppermute | solution.py:1070
  101.7 4.7 %collective-permute-done.34.refs_1_.refs_4_.refs_13_.refs_6_ = bf16[2,256,768]{2,1,0:T(8,128)(2,1)S(1)} collective-permute-done((bf16[2,256,768]{2,1,0:T(8,128)(2,1)S(1)}, bf16[2,256,768]{2,1,0:T(8,128)(2,1)S(1)}, u32[]{:S(2)}, u32[]{:S(2)}) %collective-permute-start.34) | collective-permute-done | bytes 786464 | tf_op jit(solution)/shard_map/ppermute | solution.py:1073
  106.4 3.2 collective-permute-done.18.refs_2_
  109.6 7.5 %collective-permute-done.20.refs_4_ = bf16[56,2048]{1,0:T(8,128)(2,1)S(1)} collective-permute-done((bf16[56,2048]{1,0:T(8,128)(2,1)S(1)}, bf16[56,2048]{1,0:T(8,128)(2,1)S(1)}, u32[]{:S(2)}, u32[]{:S(2)}) %collective-permute-start.20) | collective-permute-done | bytes 229408 | tf_op jit(solution)/shard_map/ppermute | solution.py:1070
  126.6 4.9 %collective-permute-start.21 = (bf16[48,2048]{1,0:T(8,128)(2,1)S(1)}, bf16[48,2048]{1,0:T(8,128)(2,1)S(1)}, u32[]{:S(2)}, u32[]{:S(2)}) collective-permute-start(bf16[48,2048]{1,0:T(8,128)(2,1)S(1)} %get-tuple-element.122.refs_1_), channel_id=1, source_target_pairs={{0,2},{1,3},{2,0},{3,1},{4,6},{5,7},{6,4},{7,5},{8,10},{9,11},{10,... | collective-permute-start | bytes 589832 | tf_op jit(solution)/shard_map/ppermute | solution.py:1070
  135.0 4.9 %collective-permute-start.24 = (bf16[48,2048]{1,0:T(8,128)(2,1)S(1)}, bf16[48,2048]{1,0:T(8,128)(2,1)S(1)}, u32[]{:S(2)}, u32[]{:S(2)}) collective-permute-start(bf16[48,2048]{1,0:T(8,128)(2,1)S(1)} %get-tuple-element.122.refs_1_), channel_id=1, source_target_pairs={{0,1},{1,0},{2,3},{3,2},{4,5},{5,4},{6,7},{7,6},{8,9},{9,8},{10,11... | collective-permute-start | bytes 589832 | tf_op jit(solution)/shard_map/ppermute | solution.py:1070
  142.9 3.6 %down_back.1 = (f32[384,768]{1,0:T(8,128)S(1)}, bf16[384,2048]{1,0:T(8,128)(2,1)S(1)}, f32[384,16]{1,0:T(8,128)S(1)}) custom-call(s32[12]{0:T(128)S(1)} %stack.57.refs_0_, bf16[384,2048]{1,0:T(8,128)(2,1)S(1)} %copy-done.43, f32[1,2048]{1,0:T(1,128)S(1)} %get-tuple-element.126.refs_2_.refs_4_.refs_12_, bf16[704,2048]{1,0:T(8,128)(2,1)S(1)} %copy-done.1, ...), custom_call_target="tpu_custom_call" | custom-call | flops 3500000000 | bytes 3500000 | tf_op jit(solution)/shard_map/down_back/pallas_call | solution.py:475
  146.5 3.8 %collective-permute-start.25 = (bf16[48,2048]{1,0:T(8,128)(2,1)S(1)}, bf16[48,2048]{1,0:T(8,128)(2,1)S(1)}, u32[]{:S(2)}, u32[]{:S(2)}) collective-permute-start(bf16[48,2048]{1,0:T(8,128)(2,1)S(1)} %collective-permute-done.21.refs_6_.refs_2_), channel_id=1, source_target_pairs={{0,1},{1,0},{2,3},{3,2},{4,5},{5,4},{6,7},{7,6},{8,9},{9,8},{10,11... | collective-permute-start | bytes 589832 | tf_op jit(solution)/shard_map/ppermute | solution.py:1070
  150.3 2.3 collective-permute-done.35.refs_2_.refs_14_.refs_7_
  152.6 2.9 collective-permute-start.27
  155.5 3.2 wide_norms.1.refs_17_.refs_9_
  158.7 14.0 %feed_forward.1 = (bf16[192,2048]{1,0:T(8,128)(2,1)S(1)}, f32[192,2048]{1,0:T(8,128)S(1)}, bf16[384,2048]{1,0:T(8,128)(2,1)S(1)}, bf16[384,768]{1,0:T(8,128)(2,1...) custom-call(s32[12]{0:T(128)S(1)} %stack.57.refs_0_, ...), custom_call_target="tpu_custom_call" | custom-call | flops 14000000000 | bytes 14000000 | tf_op jit(solution)/shard_map/feed_forward/pallas_call | solution.py:475
  172.7 2.8 collective-permute-start.36
  175.6 3.5 %down.1 = (bf16[192,2048]{1,0:T(8,128)(2,1)S(1)}, f32[192,2048]{1,0:T(8,128)S(1)}, f32[384,16]{1,0:T(8,128)S(1)}, f32[1,2048]{1,0:T(1,128)S(1)}) custom-call(s32[12]{0:T(128)S(1)} %stack.57.refs_0_, bf16[384,768]{1,0:T(8,128)(2,1)S(1)} %get-tuple-element.131.refs_1_, bf16[704,2048]{1,0:T(8,128)(2,1)S(1)} %copy-done.1, ...), custom_call_target="tpu_custom_call" | custom-call | flops 3500000000 | bytes 3500000 | tf_op jit(solution)/shard_map/down/pallas_call | solution.py:475
  179.8 4.9 %collective-permute-start.37 = (bf16[48,2048]{1,0:T(8,128)(2,1)S(1)}, bf16[48,2048]{1,0:T(8,128)(2,1)S(1)}, u32[]{:S(2)}, u32[]{:S(2)}) collective-permute-start(bf16[48,2048]{1,0:T(8,128)(2,1)S(1)} %get-tuple-element.134), channel_id=1, source_target_pairs={{0,2},{1,3},{2,0},{3,1},{4,6},{5,7},{6,4},{7,5},{8,10},{9,11},{10,... | collective-permute-start | bytes 589832 | tf_op jit(solution)/shard_map/ppermute | solution.py:1070
  187.2 5.9 %collective-permute-done.37.refs_14_.refs_1_ = bf16[48,2048]{1,0:T(8,128)(2,1)S(1)} collective-permute-done((bf16[48,2048]{1,0:T(8,128)(2,1)S(1)}, bf16[48,2048]{1,0:T(8,128)(2,1)S(1)}, u32[]{:S(2)}, u32[]{:S(2)}) %collective-permute-start.37) | collective-permute-done | bytes 196640 | tf_op jit(solution)/shard_map/ppermute | solution.py:1070
  193.1 7.9 %column_grads.2 = (f32[64,1024]{1,0:T(8,128)S(1)}, f32[24,1024]{1,0:T(8,128)S(1)}, f32[1,1536]{1,0:T(1,128)S(1)}) custom-call(s32[12]{0:T(128)S(1)} %stack.57.refs_0_, bf16[384,2048]{1,0:T(8,128)(2,1)S(1)} %get-tuple-element.141.refs_1_, bf16[2,256,768]{2,1,0:T(8,128)(2,1)S(1)} %get-tuple-element.124.refs_0_.refs_1_.refs_9_.refs_2_, ...), custom_call_target="tpu_custom_call" | custom-call | flops 1000000000 | bytes 1000000 | tf_op jit(solution)/shard_map/column_grads/pallas_call | solution.py:475
  203.2 3.1 collective-permute-start.40
  206.4 2.5 collective-permute-done.42.refs_4_
  208.9 4.6 %collective-permute-start.46 = (bf16[56,2048]{1,0:T(8,128)(2,1)S(1)}, bf16[56,2048]{1,0:T(8,128)(2,1)S(1)}, u32[]{:S(2)}, u32[]{:S(2)}) collective-permute-start(bf16[56,2048]{1,0:T(8,128)(2,1)S(1)} %collective-permute-done.42.refs_4_), channel_id=1, source_target_pairs={{0,1},{1,0},{2,3},{3,2},{4,5},{5,4},{6,7},{7,6},{8,9},{9,8},{10,11... | collective-permute-start | bytes 688136 | tf_op jit(solution)/shard_map/ppermute | solution.py:1070
  216.5 9.1 %collective-permute-done.41.refs_3_ = bf16[56,2048]{1,0:T(8,128)(2,1)S(1)} collective-permute-done((bf16[56,2048]{1,0:T(8,128)(2,1)S(1)}, bf16[56,2048]{1,0:T(8,128)(2,1)S(1)}, u32[]{:S(2)}, u32[]{:S(2)}) %collective-permute-start.41) | collective-permute-done | bytes 229408 | tf_op jit(solution)/shard_map/ppermute | solution.py:1070
  228.3 9.2 %attention_back.1 = (bf16[192,2048]{1,0:T(8,128)(2,1)S(1)}, f32[192,2048]{1,0:T(8,128)S(1)}, bf16[384,2048]{1,0:T(8,128)(2,1)S(1)}, bf16[384,768]{1,0:T(8,128)(2...) custom-call(s32[12]{0:T(128)S(1)} %stack.57.refs_0_, ...), custom_call_target="tpu_custom_call" | custom-call | flops 100000000 | bytes 100000 | tf_op jit(solution)/shard_map/attention_back/pallas_call | solution.py:475
  241.2 2.2 row_grads.2
  243.5 6.1 %column_grads.3 = (f32[96,1024]{1,0:T(8,128)S(1)}, f32[12,1024]{1,0:T(8,128)S(1)}, f32[1,768]{1,0:T(1,128)S(1)}) custom-call(s32[12]{0:T(128)S(1)} %stack.57.refs_0_, bf16[384,2048]{1,0:T(8,128)(2,1)S(1)} %copy-done.10, bf16[3,256,256]{2,1,0:T(8,128)(2,1)S(1)} %get-tuple-element.106.refs_0_.refs_6_.refs_2_.refs_9_, bf16[3,256,256]{2,1,0:T(8,128)(2,1)S(1)} %copy-done.13, ...), custom_call_target="tpu_custom_call" | custom-call | flops 1000000000 | bytes 1000000 | tf_op jit(solution)/shard_map/column_grads/pallas_call | solution.py:475
  249.6 3.7 %row_grads.3 = (f32[12,1024]{1,0:T(8,128)S(1)}, f32[32,1024]{1,0:T(8,128)S(1)}) custom-call(s32[12]{0:T(128)S(1)} %stack.57.refs_0_, bf16[384,768]{1,0:T(8,128)(2,1)S(1)} %get-tuple-element.131.refs_1_, bf16[704,2048]{1,0:T(8,128)(2,1)S(1)} %copy-done.1, bf16[16,17664]{1,0:T(8,128)(2,1)S(1)} %get-tuple-element.112.refs_2_.refs_9_.refs_5_.refs_4_.refs_3_.refs_16_.refs_8_, ...), custom_call_target="tpu_custom_call" | custom-call | flops 100000000 | bytes 100000 | tf_op jit(solution)/shard_map/row_grads/pallas_call | solution.py:475
  254.8 2.1 collective-permute-start.50
  260.6 2.5 collective-permute-done.49.refs_1_
  263.1 5.7 %collective-permute-done.51.refs_3_ = bf16[48,2048]{1,0:T(8,128)(2,1)S(1)} collective-permute-done((bf16[48,2048]{1,0:T(8,128)(2,1)S(1)}, bf16[48,2048]{1,0:T(8,128)(2,1)S(1)}, u32[]{:S(2)}, u32[]{:S(2)}) %collective-permute-start.51) | collective-permute-done | bytes 196640 | tf_op jit(solution)/shard_map/ppermute | solution.py:1070
  269.4 5.8 %collective-permute-start.56 = (bf16[96,2048]{1,0:T(8,128)(2,1)S(1)}, bf16[96,2048]{1,0:T(8,128)(2,1)S(1)}, u32[]{:S(2)}, u32[]{:S(2)}) collective-permute-start(bf16[96,2048]{1,0:T(8,128)(2,1)S(1)} %last_rows.1.refs_1_), channel_id=1, source_target_pairs={{0,4},{1,5},{2,6},{3,7},{4,0},{5,1},{6,2},{7,3},{8,12},{9,13},{10,... | collective-permute-start | bytes 1179656 | tf_op jit(solution)/shard_map/ppermute | solution.py:1070
  279.4 3.5 %collective-permute-done.63.refs_2_ = bf16[32,1024]{1,0:T(8,128)(2,1)S(1)} collective-permute-done((bf16[32,1024]{1,0:T(8,128)(2,1)S(1)}, bf16[32,1024]{1,0:T(8,128)(2,1)S(1)}, u32[]{:S(2)}, u32[]{:S(2)}) %collective-permute-start.63) | collective-permute-done | bytes 65568 | tf_op jit(solution)/shard_map/ppermute | solution.py:1070
  283.0 12.8 %collective-permute-done.64.refs_3_ = bf16[32,1024]{1,0:T(8,128)(2,1)S(1)} collective-permute-done((bf16[32,1024]{1,0:T(8,128)(2,1)S(1)}, bf16[32,1024]{1,0:T(8,128)(2,1)S(1)}, u32[]{:S(2)}, u32[]{:S(2)}) %collective-permute-start.64) | collective-permute-done | bytes 65568 | tf_op jit(solution)/shard_map/ppermute | solution.py:1070
  296.7 2.3 collective-permute-start.68
  312.3 7.1 %collective-permute-start.75 = (bf16[96,1024]{1,0:T(8,128)(2,1)S(1)}, bf16[96,1024]{1,0:T(8,128)(2,1)S(1)}, u32[]{:S(2)}, u32[]{:S(2)}) collective-permute-start(bf16[96,1024]{1,0:T(8,128)(2,1)S(1)} %pad_maximum_fusion.2.refs_2_), channel_id=1, source_target_pairs={{0,1},{1,0},{2,3},{3,2},{4,5},{5,4},{6,7},{7,6},{8,9},{9,8},{10,11... | collective-permute-start | bytes 589832 | tf_op jit(solution)/shard_map/ppermute | solution.py:1070
  319.4 2.9 collective-permute-start.76
  327.5 2.8 collective-permute-start.61
  335.0 2.9 update.1
  338.0 3.0 join_rows.1
  (368 shorter events, 118.4 us)
Async XLA Ops:
  7.6 15.9 %collective-permute-start.2 = (bf16[3,64,512]{2,1,0:T(8,128)(2,1)S(1)}, bf16[3,64,512]{2,1,0:T(8,128)(2,1)S(1)}, u32[]{:S(2)}, u32[]{:S(2)}) collective-permute-start(bf16[3,64,512]{2,1,0:T(8,128)(2,1)S(1)} %get-tuple-element.210), channel_id=1, source_target_pairs={{0,2},{1,3},{2,0},{3,1},{4,6},{5,7},{6,4},{7,5},{8,10},{9,11},{10,... | collective-permute-start | bytes 589832 | tf_op jit(solution)/shard_map/ppermute | solution.py:1070
  8.9 14.6 %collective-permute-start.3 = (bf16[3,64,512]{2,1,0:T(8,128)(2,1)S(1)}, bf16[3,64,512]{2,1,0:T(8,128)(2,1)S(1)}, u32[]{:S(2)}, u32[]{:S(2)}) collective-permute-start(bf16[3,64,512]{2,1,0:T(8,128)(2,1)S(1)} %get-tuple-element.212), channel_id=1, source_target_pairs={{0,4},{1,5},{2,6},{3,7},{4,0},{5,1},{6,2},{7,3},{8,12},{9,13},{10,... | collective-permute-start | bytes 589832 | tf_op jit(solution)/shard_map/ppermute | solution.py:1070
  11.7 12.6 %collective-permute-start.4 = (bf16[3,64,512]{2,1,0:T(8,128)(2,1)S(1)}, bf16[3,64,512]{2,1,0:T(8,128)(2,1)S(1)}, u32[]{:S(2)}, u32[]{:S(2)}) collective-permute-start(bf16[3,64,512]{2,1,0:T(8,128)(2,1)S(1)} %get-tuple-element.209), channel_id=1, source_target_pairs={{0,6},{1,7},{2,4},{3,5},{4,2},{5,3},{6,0},{7,1},{8,14},{9,15},{10,... | collective-permute-start | bytes 589832 | tf_op jit(solution)/shard_map/ppermute | solution.py:1070
  14.6 20.5 %collective-permute-start.13 = (bf16[80,1024]{1,0:T(8,128)(2,1)S(1)}, bf16[80,1024]{1,0:T(8,128)(2,1)S(1)}, u32[]{:S(2)}, u32[]{:S(2)}) collective-permute-start(bf16[80,1024]{1,0:T(8,128)(2,1)S(1)} %constant_dynamic-update-slice_fusion.refs_2_.refs_0_.refs_3_), channel_id=1, source_target_pairs={{0,16},{8,24},{16,0},{24,8},{1,17},{9,25},{17,1},{25,9},{2,18},{10... | collective-permute-start | bytes 491528 | tf_op jit(solution)/shard_map/ppermute | solution.py:1073
  16.0 24.8 %collective-permute-start.11 = (bf16[80,1024]{1,0:T(8,128)(2,1)S(1)}, bf16[80,1024]{1,0:T(8,128)(2,1)}, u32[]{:S(2)}, u32[]{:S(2)}) collective-permute-start(bf16[80,1024]{1,0:T(8,128)(2,1)S(1)} %pad_maximum_fusion.3.refs_0_), channel_id=1, source_target_pairs={{0,8},{8,0},{16,24},{24,16},{1,9},{9,1},{17,25},{25,17},{2,10},{10... | collective-permute-start | bytes 491528 | tf_op jit(solution)/shard_map/ppermute | solution.py:1073
  28.9 14.7 %collective-permute-start.5 = (bf16[3,256,256]{2,1,0:T(8,128)(2,1)S(1)}, bf16[3,256,256]{2,1,0:T(8,128)(2,1)S(1)}, u32[]{:S(2)}, u32[]{:S(2)}) collective-permute-start(bf16[3,256,256]{2,1,0:T(8,128)(2,1)S(1)} %get-tuple-element.106.refs_0_.refs_6_.refs_2_.refs_9_), channel_id=1, source_target_pairs={{0,8},{8,0},{16,24},{24,16},{1,9},{9,1},{17,25},{25,17},{2,10},{10... | collective-permute-start | bytes 1179656 | tf_op jit(solution)/shard_map/ppermute | solution.py:1073
  33.9 11.1 %collective-permute-start.8 = (bf16[3,256,256]{2,1,0:T(8,128)(2,1)S(1)}, bf16[3,256,256]{2,1,0:T(8,128)(2,1)S(1)}, u32[]{:S(2)}, u32[]{:S(2)}) collective-permute-start(bf16[3,256,256]{2,1,0:T(8,128)(2,1)S(1)} %collective-permute-done.7.refs_0_.refs_5_.refs_12_), channel_id=1, source_target_pairs={{0,16},{8,24},{16,0},{24,8},{1,17},{9,25},{17,1},{25,9},{2,18},{10... | collective-permute-start | bytes 1179656 | tf_op jit(solution)/shard_map/ppermute | solution.py:1073
  35.1 12.0 %collective-permute-start.14 = (bf16[2,80,1024]{2,1,0:T(8,128)(2,1)S(1)}, bf16[2,80,1024]{2,1,0:T(8,128)(2,1)S(1)}, u32[]{:S(2)}, u32[]{:S(2)}) collective-permute-start(bf16[2,80,1024]{2,1,0:T(8,128)(2,1)S(1)} %stack.61), channel_id=1, source_target_pairs={{0,8},{8,0},{16,24},{24,16},{1,9},{9,1},{17,25},{25,17},{2,10},{10... | collective-permute-start | bytes 983048 | tf_op jit(solution)/shard_map/ppermute | solution.py:1073
  37.6 18.9 %collective-permute-start.28 = (bf16[2,64,1408]{2,1,0:T(8,128)(2,1)S(1)}, bf16[2,64,1408]{2,1,0:T(8,128)(2,1)S(1)}, u32[]{:S(2)}, u32[]{:S(2)}) collective-permute-start(bf16[2,64,1408]{2,1,0:T(8,128)(2,1)S(1)} %get-tuple-element.207), channel_id=1, source_target_pairs={{0,2},{1,3},{2,0},{3,1},{4,6},{5,7},{6,4},{7,5},{8,10},{9,11},{10,... | collective-permute-start | bytes 1081352 | tf_op jit(solution)/shard_map/ppermute | solution.py:1070
  40.7 19.0 %collective-permute-start.29 = (bf16[2,64,1408]{2,1,0:T(8,128)(2,1)S(1)}, bf16[2,64,1408]{2,1,0:T(8,128)(2,1)S(1)}, u32[]{:S(2)}, u32[]{:S(2)}) collective-permute-start(bf16[2,64,1408]{2,1,0:T(8,128)(2,1)S(1)} %get-tuple-element.206), channel_id=1, source_target_pairs={{0,4},{1,5},{2,6},{3,7},{4,0},{5,1},{6,2},{7,3},{8,12},{9,13},{10,... | collective-permute-start | bytes 1081352 | tf_op jit(solution)/shard_map/ppermute | solution.py:1070
  44.9 33.4 %collective-permute-start.6 = (bf16[2,3,256,256]{3,2,1,0:T(8,128)(2,1)}, bf16[2,3,256,256]{3,2,1,0:T(8,128)(2,1)}, u32[]{:S(2)}, u32[]{:S(2)}) collective-permute-start(bf16[2,3,256,256]{3,2,1,0:T(8,128)(2,1)} %stack.58), channel_id=1, source_target_pairs={{0,16},{8,24},{16,0},{24,8},{1,17},{9,25},{17,1},{25,9},{2,18},{10... | collective-permute-start | bytes 2359304 | tf_op jit(solution)/shard_map/ppermute | solution.py:1073
  47.2 31.2 %collective-permute-start.9 = (bf16[2,3,256,256]{3,2,1,0:T(8,128)(2,1)}, bf16[2,3,256,256]{3,2,1,0:T(8,128)(2,1)}, u32[]{:S(2)}, u32[]{:S(2)}) collective-permute-start(bf16[2,3,256,256]{3,2,1,0:T(8,128)(2,1)} %stack.59), channel_id=1, source_target_pairs={{0,8},{8,0},{16,24},{24,16},{1,9},{9,1},{17,25},{25,17},{2,10},{10... | collective-permute-start | bytes 2359304 | tf_op jit(solution)/shard_map/ppermute | solution.py:1073
  51.8 15.1 %collective-permute-start.30 = (bf16[2,64,1408]{2,1,0:T(8,128)(2,1)}, bf16[2,64,1408]{2,1,0:T(8,128)(2,1)S(1)}, u32[]{:S(2)}, u32[]{:S(2)}) collective-permute-start(bf16[2,64,1408]{2,1,0:T(8,128)(2,1)} %get-tuple-element.205), channel_id=1, source_target_pairs={{0,6},{1,7},{2,4},{3,5},{4,2},{5,3},{6,0},{7,1},{8,14},{9,15},{10,... | collective-permute-start | bytes 1081352 | tf_op jit(solution)/shard_map/ppermute | solution.py:1070
  57.2 14.2 %collective-permute-start.15 = (bf16[320,1024]{1,0:T(8,128)(2,1)}, bf16[320,1024]{1,0:T(8,128)(2,1)}, u32[]{:S(2)}, u32[]{:S(2)}) collective-permute-start(bf16[320,1024]{1,0:T(8,128)(2,1)} %get-tuple-element.110.refs_3_), channel_id=1, source_target_pairs={{0,1},{1,0},{2,3},{3,2},{4,5},{5,4},{6,7},{7,6},{8,9},{9,8},{10,11... | collective-permute-start | bytes 1966088 | tf_op jit(solution)/shard_map/ppermute | solution.py:1070
  69.6 18.1 %collective-permute-start.33 = (bf16[2,256,768]{2,1,0:T(8,128)(2,1)S(1)}, bf16[2,256,768]{2,1,0:T(8,128)(2,1)S(1)}, u32[]{:S(2)}, u32[]{:S(2)}) collective-permute-start(bf16[2,256,768]{2,1,0:T(8,128)(2,1)S(1)} %get-tuple-element.125), channel_id=1, source_target_pairs={{0,1},{1,0},{2,3},{3,2},{4,5},{5,4},{6,7},{7,6},{8,9},{9,8},{10,11... | collective-permute-start | bytes 2359304 | tf_op jit(solution)/shard_map/ppermute | solution.py:1070
  87.6 18.8 %collective-permute-start.34 = (bf16[2,256,768]{2,1,0:T(8,128)(2,1)S(1)}, bf16[2,256,768]{2,1,0:T(8,128)(2,1)S(1)}, u32[]{:S(2)}, u32[]{:S(2)}) collective-permute-start(bf16[2,256,768]{2,1,0:T(8,128)(2,1)S(1)} %collective-permute-done.33.refs_0_.refs_3_.refs_12_.refs_5_), channel_id=1, source_target_pairs={{0,16},{8,24},{16,0},{24,8},{1,17},{9,25},{17,1},{25,9},{2,18},{10... | collective-permute-start | bytes 2359304 | tf_op jit(solution)/shard_map/ppermute | solution.py:1073
  87.9 31.9 %collective-permute-start.31 = (bf16[2,256,768]{2,1,0:T(8,128)(2,1)S(1)}, bf16[2,256,768]{2,1,0:T(8,128)(2,1)S(1)}, u32[]{:S(2)}, u32[]{:S(2)}) collective-permute-start(bf16[2,256,768]{2,1,0:T(8,128)(2,1)S(1)} %get-tuple-element.124.refs_0_.refs_1_.refs_9_.refs_2_), channel_id=1, source_target_pairs={{0,8},{8,0},{16,24},{24,16},{1,9},{9,1},{17,25},{25,17},{2,10},{10... | collective-permute-start | bytes 2359304 | tf_op jit(solution)/shard_map/ppermute | solution.py:1073
  91.4 18.2 %collective-permute-start.18 = (bf16[56,2048]{1,0:T(8,128)(2,1)S(1)}, bf16[56,2048]{1,0:T(8,128)(2,1)S(1)}, u32[]{:S(2)}, u32[]{:S(2)}) collective-permute-start(bf16[56,2048]{1,0:T(8,128)(2,1)S(1)} %get-tuple-element.119), channel_id=1, source_target_pairs={{0,2},{1,3},{2,0},{3,1},{4,6},{5,7},{6,4},{7,5},{8,10},{9,11},{10,... | collective-permute-start | bytes 688136 | tf_op jit(solution)/shard_map/ppermute | solution.py:1070
  100.7 16.4 %collective-permute-start.20 = (bf16[56,2048]{1,0:T(8,128)(2,1)S(1)}, bf16[56,2048]{1,0:T(8,128)(2,1)S(1)}, u32[]{:S(2)}, u32[]{:S(2)}) collective-permute-start(bf16[56,2048]{1,0:T(8,128)(2,1)S(1)} %get-tuple-element.121), channel_id=1, source_target_pairs={{0,6},{1,7},{2,4},{3,5},{4,2},{5,3},{6,0},{7,1},{8,14},{9,15},{10,... | collective-permute-start | bytes 688136 | tf_op jit(solution)/shard_map/ppermute | solution.py:1070
  118.4 34.2 %collective-permute-start.35 = (bf16[2,2,256,768]{3,2,1,0:T(8,128)(2,1)}, bf16[2,2,256,768]{3,2,1,0:T(8,128)(2,1)}, u32[]{:S(2)}, u32[]{:S(2)}) collective-permute-start(bf16[2,2,256,768]{3,2,1,0:T(8,128)(2,1)} %stack.63), channel_id=1, source_target_pairs={{0,8},{8,0},{16,24},{24,16},{1,9},{9,1},{17,25},{25,17},{2,10},{10... | collective-permute-start | bytes 4718600 | tf_op jit(solution)/shard_map/ppermute | solution.py:1073
  121.2 34.4 %collective-permute-start.32 = (bf16[2,2,256,768]{3,2,1,0:T(8,128)(2,1)}, bf16[2,2,256,768]{3,2,1,0:T(8,128)(2,1)}, u32[]{:S(2)}, u32[]{:S(2)}) collective-permute-start(bf16[2,2,256,768]{3,2,1,0:T(8,128)(2,1)} %stack.62), channel_id=1, source_target_pairs={{0,16},{8,24},{16,0},{24,8},{1,17},{9,25},{17,1},{25,9},{2,18},{10... | collective-permute-start | bytes 4718600 | tf_op jit(solution)/shard_map/ppermute | solution.py:1073
  131.5 14.9 %collective-permute-start.22 = (bf16[48,2048]{1,0:T(8,128)(2,1)S(1)}, bf16[48,2048]{1,0:T(8,128)(2,1)S(1)}, u32[]{:S(2)}, u32[]{:S(2)}) collective-permute-start(bf16[48,2048]{1,0:T(8,128)(2,1)S(1)} %get-tuple-element.122.refs_1_), channel_id=1, source_target_pairs={{0,4},{1,5},{2,6},{3,7},{4,0},{5,1},{6,2},{7,3},{8,12},{9,13},{10,... | collective-permute-start | bytes 589832 | tf_op jit(solution)/shard_map/ppermute | solution.py:1070
  132.8 17.5 %collective-permute-start.23 = (bf16[48,2048]{1,0:T(8,128)(2,1)S(1)}, bf16[48,2048]{1,0:T(8,128)(2,1)S(1)}, u32[]{:S(2)}, u32[]{:S(2)}) collective-permute-start(bf16[48,2048]{1,0:T(8,128)(2,1)S(1)} %get-tuple-element.122.refs_1_), channel_id=1, source_target_pairs={{0,6},{1,7},{2,4},{3,5},{4,2},{5,3},{6,0},{7,1},{8,14},{9,15},{10,... | collective-permute-start | bytes 589832 | tf_op jit(solution)/shard_map/ppermute | solution.py:1070
  135.0 23.7 %collective-permute-start.24 = (bf16[48,2048]{1,0:T(8,128)(2,1)S(1)}, bf16[48,2048]{1,0:T(8,128)(2,1)S(1)}, u32[]{:S(2)}, u32[]{:S(2)}) collective-permute-start(bf16[48,2048]{1,0:T(8,128)(2,1)S(1)} %get-tuple-element.122.refs_1_), channel_id=1, source_target_pairs={{0,1},{1,0},{2,3},{3,2},{4,5},{5,4},{6,7},{7,6},{8,9},{9,8},{10,11... | collective-permute-start | bytes 589832 | tf_op jit(solution)/shard_map/ppermute | solution.py:1070
  146.5 12.2 %collective-permute-start.25 = (bf16[48,2048]{1,0:T(8,128)(2,1)S(1)}, bf16[48,2048]{1,0:T(8,128)(2,1)S(1)}, u32[]{:S(2)}, u32[]{:S(2)}) collective-permute-start(bf16[48,2048]{1,0:T(8,128)(2,1)S(1)} %collective-permute-done.21.refs_6_.refs_2_), channel_id=1, source_target_pairs={{0,1},{1,0},{2,3},{3,2},{4,5},{5,4},{6,7},{7,6},{8,9},{9,8},{10,11... | collective-permute-start | bytes 589832 | tf_op jit(solution)/shard_map/ppermute | solution.py:1070
  179.0 47.1 %collective-permute-start.47 = (bf16[192,2048]{1,0:T(8,128)(2,1)S(1)}, bf16[192,2048]{1,0:T(8,128)(2,1)S(1)}, u32[]{:S(2)}, u32[]{:S(2)}) collective-permute-start(bf16[192,2048]{1,0:T(8,128)(2,1)S(1)} %get-tuple-element.153), channel_id=1, source_target_pairs={{0,1},{1,0},{2,3},{3,2},{4,5},{5,4},{6,7},{7,6},{8,9},{9,8},{10,11... | collective-permute-start | bytes 2359304 | tf_op jit(solution)/shard_map/ppermute | solution.py:1070
  179.8 13.2 %collective-permute-start.37 = (bf16[48,2048]{1,0:T(8,128)(2,1)S(1)}, bf16[48,2048]{1,0:T(8,128)(2,1)S(1)}, u32[]{:S(2)}, u32[]{:S(2)}) collective-permute-start(bf16[48,2048]{1,0:T(8,128)(2,1)S(1)} %get-tuple-element.134), channel_id=1, source_target_pairs={{0,2},{1,3},{2,0},{3,1},{4,6},{5,7},{6,4},{7,5},{8,10},{9,11},{10,... | collective-permute-start | bytes 589832 | tf_op jit(solution)/shard_map/ppermute | solution.py:1070
  184.7 16.3 %collective-permute-start.38 = (bf16[48,2048]{1,0:T(8,128)(2,1)S(1)}, bf16[48,2048]{1,0:T(8,128)(2,1)S(1)}, u32[]{:S(2)}, u32[]{:S(2)}) collective-permute-start(bf16[48,2048]{1,0:T(8,128)(2,1)S(1)} %get-tuple-element.135), channel_id=1, source_target_pairs={{0,4},{1,5},{2,6},{3,7},{4,0},{5,1},{6,2},{7,3},{8,12},{9,13},{10,... | collective-permute-start | bytes 589832 | tf_op jit(solution)/shard_map/ppermute | solution.py:1070
  186.0 15.0 %collective-permute-start.39 = (bf16[48,2048]{1,0:T(8,128)(2,1)S(1)}, bf16[48,2048]{1,0:T(8,128)(2,1)S(1)}, u32[]{:S(2)}, u32[]{:S(2)}) collective-permute-start(bf16[48,2048]{1,0:T(8,128)(2,1)S(1)} %get-tuple-element.136), channel_id=1, source_target_pairs={{0,6},{1,7},{2,4},{3,5},{4,2},{5,3},{6,0},{7,1},{8,14},{9,15},{10,... | collective-permute-start | bytes 589832 | tf_op jit(solution)/shard_map/ppermute | solution.py:1070
  203.2 12.3 %collective-permute-start.40 = (bf16[56,2048]{1,0:T(8,128)(2,1)S(1)}, bf16[56,2048]{1,0:T(8,128)(2,1)S(1)}, u32[]{:S(2)}, u32[]{:S(2)}) collective-permute-start(bf16[56,2048]{1,0:T(8,128)(2,1)S(1)} %get-tuple-element.147.refs_3_.refs_1_), channel_id=1, source_target_pairs={{0,2},{1,3},{2,0},{3,1},{4,6},{5,7},{6,4},{7,5},{8,10},{9,11},{10,... | collective-permute-start | bytes 688136 | tf_op jit(solution)/shard_map/ppermute | solution.py:1070
  206.4 19.1 %collective-permute-start.41 = (bf16[56,2048]{1,0:T(8,128)(2,1)S(1)}, bf16[56,2048]{1,0:T(8,128)(2,1)S(1)}, u32[]{:S(2)}, u32[]{:S(2)}) collective-permute-start(bf16[56,2048]{1,0:T(8,128)(2,1)S(1)} %get-tuple-element.147.refs_3_.refs_1_), channel_id=1, source_target_pairs={{0,4},{1,5},{2,6},{3,7},{4,0},{5,1},{6,2},{7,3},{8,12},{9,13},{10,... | collective-permute-start | bytes 688136 | tf_op jit(solution)/shard_map/ppermute | solution.py:1070
  208.9 17.3 %collective-permute-start.46 = (bf16[56,2048]{1,0:T(8,128)(2,1)S(1)}, bf16[56,2048]{1,0:T(8,128)(2,1)S(1)}, u32[]{:S(2)}, u32[]{:S(2)}) collective-permute-start(bf16[56,2048]{1,0:T(8,128)(2,1)S(1)} %collective-permute-done.42.refs_4_), channel_id=1, source_target_pairs={{0,1},{1,0},{2,3},{3,2},{4,5},{5,4},{6,7},{7,6},{8,9},{9,8},{10,11... | collective-permute-start | bytes 688136 | tf_op jit(solution)/shard_map/ppermute | solution.py:1070
  213.5 13.4 %collective-permute-start.43 = (bf16[56,2048]{1,0:T(8,128)(2,1)S(1)}, bf16[56,2048]{1,0:T(8,128)(2,1)S(1)}, u32[]{:S(2)}, u32[]{:S(2)}) collective-permute-start(bf16[56,2048]{1,0:T(8,128)(2,1)S(1)} %get-tuple-element.147.refs_3_.refs_1_), channel_id=1, source_target_pairs={{0,1},{1,0},{2,3},{3,2},{4,5},{5,4},{6,7},{7,6},{8,9},{9,8},{10,11... | collective-permute-start | bytes 688136 | tf_op jit(solution)/shard_map/ppermute | solution.py:1070
  215.5 11.5 %collective-permute-start.44 = (bf16[56,2048]{1,0:T(8,128)(2,1)S(1)}, bf16[56,2048]{1,0:T(8,128)(2,1)S(1)}, u32[]{:S(2)}, u32[]{:S(2)}) collective-permute-start(bf16[56,2048]{1,0:T(8,128)(2,1)S(1)} %collective-permute-done.40.refs_2_), channel_id=1, source_target_pairs={{0,1},{1,0},{2,3},{3,2},{4,5},{5,4},{6,7},{7,6},{8,9},{9,8},{10,11... | collective-permute-start | bytes 688136 | tf_op jit(solution)/shard_map/ppermute | solution.py:1070
  237.5 16.4 %collective-permute-start.48 = (bf16[192,2048]{1,0:T(8,128)(2,1)S(1)}, bf16[192,2048]{1,0:T(8,128)(2,1)S(1)}, u32[]{:S(2)}, u32[]{:S(2)}) collective-permute-start(bf16[192,2048]{1,0:T(8,128)(2,1)S(1)} %get-tuple-element.156), channel_id=1, source_target_pairs={{0,1},{1,0},{2,3},{3,2},{4,5},{5,4},{6,7},{7,6},{8,9},{9,8},{10,11... | collective-permute-start | bytes 2359304 | tf_op jit(solution)/shard_map/ppermute | solution.py:1070
  237.6 19.3 %collective-permute-start.52 = (bf16[48,2048]{1,0:T(8,128)(2,1)S(1)}, bf16[48,2048]{1,0:T(8,128)(2,1)S(1)}, u32[]{:S(2)}, u32[]{:S(2)}) collective-permute-start(bf16[48,2048]{1,0:T(8,128)(2,1)S(1)} %get-tuple-element.183), channel_id=1, source_target_pairs={{0,2},{1,3},{2,0},{3,1},{4,6},{5,7},{6,4},{7,5},{8,10},{9,11},{10,... | collective-permute-start | bytes 589832 | tf_op jit(solution)/shard_map/ppermute | solution.py:1070
  237.7 20.8 %collective-permute-start.53 = (bf16[48,2048]{1,0:T(8,128)(2,1)S(1)}, bf16[48,2048]{1,0:T(8,128)(2,1)S(1)}, u32[]{:S(2)}, u32[]{:S(2)}) collective-permute-start(bf16[48,2048]{1,0:T(8,128)(2,1)S(1)} %get-tuple-element.184), channel_id=1, source_target_pairs={{0,4},{1,5},{2,6},{3,7},{4,0},{5,1},{6,2},{7,3},{8,12},{9,13},{10,... | collective-permute-start | bytes 589832 | tf_op jit(solution)/shard_map/ppermute | solution.py:1070
  239.6 21.0 %collective-permute-start.54 = (bf16[48,2048]{1,0:T(8,128)(2,1)S(1)}, bf16[48,2048]{1,0:T(8,128)(2,1)S(1)}, u32[]{:S(2)}, u32[]{:S(2)}) collective-permute-start(bf16[48,2048]{1,0:T(8,128)(2,1)S(1)} %get-tuple-element.185), channel_id=1, source_target_pairs={{0,6},{1,7},{2,4},{3,5},{4,2},{5,3},{6,0},{7,1},{8,14},{9,15},{10,... | collective-permute-start | bytes 589832 | tf_op jit(solution)/shard_map/ppermute | solution.py:1070
  256.9 11.9 %collective-permute-start.51 = (bf16[48,2048]{1,0:T(8,128)(2,1)S(1)}, bf16[48,2048]{1,0:T(8,128)(2,1)S(1)}, u32[]{:S(2)}, u32[]{:S(2)}) collective-permute-start(bf16[48,2048]{1,0:T(8,128)(2,1)S(1)} %get-tuple-element.181), channel_id=1, source_target_pairs={{0,6},{1,7},{2,4},{3,5},{4,2},{5,3},{6,0},{7,1},{8,14},{9,15},{10,... | collective-permute-start | bytes 589832 | tf_op jit(solution)/shard_map/ppermute | solution.py:1070
  258.5 16.7 %collective-permute-start.62 = (bf16[128,1024]{1,0:T(8,128)(2,1)S(1)}, bf16[128,1024]{1,0:T(8,128)(2,1)S(1)}, u32[]{:S(2)}, u32[]{:S(2)}) collective-permute-start(bf16[128,1024]{1,0:T(8,128)(2,1)S(1)} %get-tuple-element.177.refs_3_), channel_id=1, source_target_pairs={{0,1},{1,0},{2,3},{3,2},{4,5},{5,4},{6,7},{7,6},{8,9},{9,8},{10,11... | collective-permute-start | bytes 786440 | tf_op jit(solution)/shard_map/ppermute | solution.py:1070
  269.4 41.1 %collective-permute-start.56 = (bf16[96,2048]{1,0:T(8,128)(2,1)S(1)}, bf16[96,2048]{1,0:T(8,128)(2,1)S(1)}, u32[]{:S(2)}, u32[]{:S(2)}) collective-permute-start(bf16[96,2048]{1,0:T(8,128)(2,1)S(1)} %last_rows.1.refs_1_), channel_id=1, source_target_pairs={{0,4},{1,5},{2,6},{3,7},{4,0},{5,1},{6,2},{7,3},{8,12},{9,13},{10,... | collective-permute-start | bytes 1179656 | tf_op jit(solution)/shard_map/ppermute | solution.py:1070
  275.9 19.9 %collective-permute-start.64 = (bf16[32,1024]{1,0:T(8,128)(2,1)S(1)}, bf16[32,1024]{1,0:T(8,128)(2,1)S(1)}, u32[]{:S(2)}, u32[]{:S(2)}) collective-permute-start(bf16[32,1024]{1,0:T(8,128)(2,1)S(1)} %get-tuple-element.191), channel_id=1, source_target_pairs={{0,4},{1,5},{2,6},{3,7},{4,0},{5,1},{6,2},{7,3},{8,12},{9,13},{10,... | collective-permute-start | bytes 196616 | tf_op jit(solution)/shard_map/ppermute | solution.py:1070
  277.8 18.0 %collective-permute-start.65 = (bf16[32,1024]{1,0:T(8,128)(2,1)S(1)}, bf16[32,1024]{1,0:T(8,128)(2,1)S(1)}, u32[]{:S(2)}, u32[]{:S(2)}) collective-permute-start(bf16[32,1024]{1,0:T(8,128)(2,1)S(1)} %get-tuple-element.192), channel_id=1, source_target_pairs={{0,6},{1,7},{2,4},{3,5},{4,2},{5,3},{6,0},{7,1},{8,14},{9,15},{10,... | collective-permute-start | bytes 196616 | tf_op jit(solution)/shard_map/ppermute | solution.py:1070
  310.2 12.1 %collective-permute-start.74 = (bf16[96,1024]{1,0:T(8,128)(2,1)S(1)}, bf16[96,1024]{1,0:T(8,128)(2,1)}, u32[]{:S(2)}, u32[]{:S(2)}) collective-permute-start(bf16[96,1024]{1,0:T(8,128)(2,1)S(1)} %pad_maximum_fusion.2.refs_2_), channel_id=1, source_target_pairs={{0,24},{8,16},{16,8},{24,0},{1,25},{9,17},{17,9},{25,1},{2,26},{10... | collective-permute-start | bytes 589832 | tf_op jit(solution)/shard_map/ppermute | solution.py:1073
  310.2 16.8 %collective-permute-start.55 = (bf16[96,2048]{1,0:T(8,128)(2,1)S(1)}, bf16[96,2048]{1,0:T(8,128)(2,1)S(1)}, u32[]{:S(2)}, u32[]{:S(2)}) collective-permute-start(bf16[96,2048]{1,0:T(8,128)(2,1)S(1)} %last_rows.1.refs_1_), channel_id=1, source_target_pairs={{0,2},{1,3},{2,0},{3,1},{4,6},{5,7},{6,4},{7,5},{8,10},{9,11},{10,... | collective-permute-start | bytes 1179656 | tf_op jit(solution)/shard_map/ppermute | solution.py:1070
  310.6 16.9 %collective-permute-start.57 = (bf16[96,2048]{1,0:T(8,128)(2,1)S(1)}, bf16[96,2048]{1,0:T(8,128)(2,1)S(1)}, u32[]{:S(2)}, u32[]{:S(2)}) collective-permute-start(bf16[96,2048]{1,0:T(8,128)(2,1)S(1)} %collective-permute-done.56.refs_3_), channel_id=1, source_target_pairs={{0,2},{1,3},{2,0},{3,1},{4,6},{5,7},{6,4},{7,5},{8,10},{9,11},{10,... | collective-permute-start | bytes 1179656 | tf_op jit(solution)/shard_map/ppermute | solution.py:1070
  312.3 12.1 %collective-permute-start.75 = (bf16[96,1024]{1,0:T(8,128)(2,1)S(1)}, bf16[96,1024]{1,0:T(8,128)(2,1)S(1)}, u32[]{:S(2)}, u32[]{:S(2)}) collective-permute-start(bf16[96,1024]{1,0:T(8,128)(2,1)S(1)} %pad_maximum_fusion.2.refs_2_), channel_id=1, source_target_pairs={{0,1},{1,0},{2,3},{3,2},{4,5},{5,4},{6,7},{7,6},{8,9},{9,8},{10,11... | collective-permute-start | bytes 589832 | tf_op jit(solution)/shard_map/ppermute | solution.py:1070
  325.8 12.1 %collective-permute-start.58 = (bf16[96,2048]{1,0:T(8,128)(2,1)S(1)}, bf16[96,2048]{1,0:T(8,128)(2,1)S(1)}, u32[]{:S(2)}, u32[]{:S(2)}) collective-permute-start(bf16[96,2048]{1,0:T(8,128)(2,1)S(1)} %last_rows.1.refs_1_), channel_id=1, source_target_pairs={{0,1},{1,0},{2,3},{3,2},{4,5},{5,4},{6,7},{7,6},{8,9},{9,8},{10,11... | collective-permute-start | bytes 1179656 | tf_op jit(solution)/shard_map/ppermute | solution.py:1070
  (116 other events, 871.2 us)
where the time goes:
time: 346 us; the launch traced here: 341 us
  starting transfers between devices  131 us (38%)
  Pallas kernels  92.9 us (27%)
  waiting for transfers between devices  76 us (22%)
  local copies, waits for them, and re-layouts  32.2 us (9%)
  other arithmetic  6.58 us (2%)
    ppermute x61, starting transfers between devices, mp_swap(): return lax.ppermute(values, 'mp', [(i, i ^ step) for i in range(N_MP)])  114 us
    pallas_call x36, Pallas kernels, run(): pl.pallas_call(body, out_shape=list(outs), in_specs=[kinds[kind] for kind...  92.9 us
    ppermute x61, waiting for transfers between devices, mp_swap(): return lax.ppermute(values, 'mp', [(i, i ^ step) for i in range(N_MP)])  64.4 us
    unnamed x171, local copies, waits for them, and re-layouts  19.2 us
    ppermute x18, starting transfers between devices, dp_swap(): return lax.ppermute(values, 'dp', [(i, i ^ step) for i in range(N_DP)])  16.9 us
    ppermute x18, waiting for transfers between devices, dp_swap(): return lax.ppermute(values, 'dp', [(i, i ^ step) for i in range(N_DP)])  11.6 us
  transfers between devices with their start and end apart: 79, of which 25 were waited for; matrix products, arithmetic and copies ran while one was open for 5% of the time, Pallas kernels for 20%

commit v1 on v0

--- a/solution.py
+++ b/solution.py
@@ -417,6 +417,21 @@
     return mm_f(high, right) + mm_f(low, right)
 
 
+def twice(parts):
+    return jnp.concatenate([part for one in parts for part in (one, one)], axis=0)
+
+
+def only(part, position, count):
+    zero = jnp.zeros_like(part)
+    return twice([part if index == position else zero for index in range(count)])
+
+
+def high_low(value):
+    high = value.astype(bf16).astype(f32)
+    lanes = lax.broadcasted_iota(jnp.int32, value.shape, 1)
+    return jnp.where(jnp.bitwise_and(lanes, RANK) == 0, high, value - high).astype(bf16)
+
+
 def swap64(value):
     return pltpu.roll(value, 64, 1)
 
@@ -604,10 +619,12 @@
     t_index = lax.broadcasted_iota(jnp.int32, (rows, rows), 0)
     s_index = lax.broadcasted_iota(jnp.int32, (rows, rows), 1)
     allowed = jnp.logical_and(allowed, s_index <= t_index)
+    lows = mm_t(x[...], twice([flat[:, la[p] : la[p] + D] for p in range(3)]))
+    low_qkv[...] = lows
+    lows = high_low(lows)
     for p in range(3):
         upper = flat[:, lb[p] : lb[p] + width]
-        low = mm_t(x[...], flat[:, la[p] : la[p] + D])
-        total = dora_scale * mm2(low, upper)
+        total = dora_scale * mm(lows, only(upper, p, 3))
         square = jnp.zeros((1, width), f32)
         for index, block in enumerate(blocks):
             chunk = where[4 + index]
@@ -620,7 +637,6 @@
         scale = magnitude / norm
         lanes = slice(p * width, (p + 1) * width)
         mixed[:, lanes] = total
-        low_qkv[:, p * RANK : (p + 1) * RANK] = low
         stats[0:1, lanes] = scale
         stats[1:2, lanes] = norm
         stats[2:3, lanes] = magnitude
@@ -680,7 +696,30 @@
 
 
 def total_of(own, r1, r2, r3):
-    return own[...] + r1[...].astype(f32) + r2[...].astype(f32) + r3[...].astype(f32)
+    rows = own.shape[0]
+    return own[...] + r1[0:rows].astype(f32) + r2[0:rows].astype(f32) + r3[0:rows].astype(f32)
+
+
+def pair_grads_kernel(where, keep, received, kept, got, p1, p2, p3, own, own_grads):
+    share, unit = own.shape[0], own_grads.shape[0]
+    half = unit // 2
+
+    def line(index):
+        rows = at(index, share)
+        return keep[rows] + received[rows].astype(f32)
+
+    def grads(index):
+        rows = at(index, unit)
+        return kept[rows] + got[rows].astype(f32)
+
+    own[...] = line(where[2])
+    own_grads[...] = grads(where[2])
+    for step, piece in ((1, p1), (2, p2), (3, p3)):
+        index = jnp.bitwise_xor(where[2], step)
+        piece[0:share] = line(index).astype(bf16)
+        value = grads(index).astype(bf16)
+        piece[share:, 0:BLOCK] = value[0:half]
+        piece[share:, BLOCK:] = value[half:]
 
 
 def second_norm_kernel(own, more, r1, r2, r3, tokens, gains, mags, x_two, mixed, out, scale_o, norm_o, scale_d, norm_d):
@@ -774,11 +813,14 @@
                   send, keep, x, act, grads, throughs, lows, dots, part, mixed):
     blocks = eight(b0, b1, b2, b3, b4, b5)
     join_rows(where, (p0, p1, p2, p3, p4, p5, p6, p7), x)
+    la = [spans[("A", 4 + p)][0] for p in range(2)]
+    lb = [spans[("B", 4 + p)][0] for p in range(2)]
+    uppers = [flat[:, b : b + WIDE] for b in lb]
+    low = mm_t(x[...], twice([flat[:, a : a + D] for a in la]))
+    lows[...] = low
+    low = high_low(low)
     for p in range(2):
-        a, b = spans[("A", 4 + p)][0], spans[("B", 4 + p)][0]
-        low = mm_t(x[...], flat[:, a : a + D])
-        lows[:, p * RANK : (p + 1) * RANK] = low
-        total = dora_scale * mm2(low, flat[:, b : b + WIDE])
+        total = dora_scale * mm(low, only(uppers[p], p, 2))
         for index, block in enumerate(blocks):
             total += mm(x[:, at(where[4 + index], CHUNK)], block(p))
         mixed[:, p * WIDE : (p + 1) * WIDE] = total
@@ -796,21 +838,17 @@
     grad = back * silu
     dots[0:1, WIDE:] = jnp.sum(grad * mixed[:, WIDE:], axis=0, keepdims=True)
     grads[:, WIDE:] = (grad * stats[0:1, WIDE:]).astype(bf16)
-    through = []
-    for p in range(2):
-        b = spans[("B", 4 + p)][0]
-        low = dora_scale * mm_t(grads[:, p * WIDE : (p + 1) * WIDE], flat[:, b : b + WIDE])
-        throughs[:, p * RANK : (p + 1) * RANK] = low
-        through.append(halves(low))
+    through = dora_scale * (
+        mm_t(grads[:, :WIDE], only(uppers[0], 0, 2)) + mm_t(grads[:, WIDE:], only(uppers[1], 1, 2))
+    )
+    throughs[...] = through
+    through = high_low(through)
     for index, block in enumerate(blocks):
         chunk = where[4 + index]
-        total = None
+        lowers = [flat[:, pl.ds(pl.multiple_of(a + chunk * CHUNK, TILE), CHUNK)] for a in la]
+        total = mm(through, twice(lowers))
         for p in range(2):
-            a = spans[("A", 4 + p)][0]
-            lowers = flat[:, pl.ds(pl.multiple_of(a + chunk * CHUNK, TILE), CHUNK)]
-            one = mm_t(grads[:, p * WIDE : (p + 1) * WIDE], block(p))
-            one += mm(through[p][0], lowers) + mm(through[p][1], lowers)
-            total = one if total is None else total + one
+            total += mm_t(grads[:, p * WIDE : (p + 1) * WIDE], block(p))
         part[:, at(chunk, CHUNK)] = total
     split_rows(where, part, send, keep, send.shape[0] // N_Z)
 
@@ -884,21 +922,20 @@
         incoming[:, lanes[1]] = grad_key * cos[...] - swap64(grad_key) * sin[...]
     dots[...] = jnp.sum(incoming[...] * mixed[...], axis=0, keepdims=True)
     grads[...] = (incoming[...] * stats[0:1, :]).astype(bf16)
-    through = []
-    for p in range(3):
-        b = spans[("B", p)][0]
-        low = dora_scale * mm_t(grads[:, p * width : (p + 1) * width], flat[:, b : b + width])
-        throughs[:, p * RANK : (p + 1) * RANK] = low
-        through.append(halves(low))
+    la = [spans[("A", p)][0] for p in range(3)]
+    uppers = [flat[:, spans[("B", p)][0] : spans[("B", p)][0] + width] for p in range(3)]
+    through = mm_t(grads[:, :width], only(uppers[0], 0, 3))
+    for p in (1, 2):
+        through += mm_t(grads[:, p * width : (p + 1) * width], only(uppers[p], p, 3))
+    through = dora_scale * through
+    throughs[...] = through
+    through = high_low(through)
     for index, block in enumerate(blocks):
         chunk = where[4 + index]
-        total = None
+        lowers = [flat[:, pl.ds(pl.multiple_of(a + chunk * CHUNK, TILE), CHUNK)] for a in la]
+        total = mm(through, twice(lowers))
         for p in range(3):
-            a = spans[("A", p)][0]
-            lowers = flat[:, pl.ds(pl.multiple_of(a + chunk * CHUNK, TILE), CHUNK)]
-            one = mm_t(grads[:, p * width : (p + 1) * width], block(p))
-            one += mm(through[p][0], lowers) + mm(through[p][1], lowers)
-            total = one if total is None else total + one
+            total += mm_t(grads[:, p * width : (p + 1) * width], block(p))
         part[:, at(chunk, CHUNK)] = total
     split_rows(where, part, send, keep, send.shape[0] // N_Z)
 
@@ -920,7 +957,7 @@
     for position, p in enumerate(projections):
         a, b = spans[("A", p)][0], spans[("B", p)][0]
         lanes = slice(position * width, (position + 1) * width)
-        ranks = slice(position * RANK, (position + 1) * RANK)
+        ranks = slice(2 * position * RANK, (2 * position + 1) * RANK)
         upper = flat[:, b : b + width]
         norm = stats[1:2, lanes]
         inverse = 1.0 / norm
@@ -994,7 +1031,13 @@
 
 def local_kernel(where, own, r1, r2, r3, b_f, b_a, a_d, a_o, mine, p1, p2, p3, rows):
     begin = own.shape[0]
-    rows[0:begin] = total_of(own, r1, r2, r3)
+    half = begin // 2
+    for index in range(2):
+        lanes = slice(index * BLOCK, (index + 1) * BLOCK)
+        total = own[index * half : (index + 1) * half]
+        for piece in (r1, r2, r3):
+            total = total + piece[piece.shape[0] - half :, lanes].astype(f32)
+        rows[index * half : (index + 1) * half] = total
     for array in (b_f, b_a, a_d, a_o):
         rows[begin : begin + array.shape[0]] = array[...]
         begin += array.shape[0]
@@ -1263,7 +1306,7 @@
             shape_of((rows, 3 * width), bf16),
             shape_of((n_heads, rows, rows), f32),
             shape_of((rows, width), bf16),
-            shape_of((rows, 3 * RANK), f32),
+            shape_of((rows, 6 * RANK), f32),
             shape_of((rows, RANK), f32),
             shape_of((8, 3 * width), f32),
         ],
@@ -1283,7 +1326,7 @@
     )
     sums_o = [mp_swap(p1, 2), mp_swap(p2, 4), mp_swap(p3, 6)]
     first_f = columns_of(pieces_f, WIDE, WIDE - TILE, "line_f")
-    blocks_f = plane_second(*first_f, after=sums_o)
+    blocks_f = plane_second(*first_f, after=sums_o[1:2])
     row_of = shape_of((1, D), f32)
     x_two, mixed_o, features_two, scale_o, norm_o, scale_d, norm_d = run(
         second_norm_kernel,
@@ -1330,8 +1373,8 @@
             shape_of((rows, D), bf16),
             shape_of((rows, WIDE), bf16),
             shape_of((rows, 2 * WIDE), bf16),
-            shape_of((rows, 2 * RANK), f32),
-            shape_of((rows, 2 * RANK), f32),
+            shape_of((rows, 4 * RANK), f32),
+            shape_of((rows, 4 * RANK), f32),
             shape_of((1, 2 * WIDE), f32),
         ],
         [pltpu.VMEM((rows, D), f32), pltpu.VMEM((rows, 2 * WIDE), f32)],
@@ -1367,7 +1410,7 @@
         + [
             shape_of((rows, D), bf16),
             shape_of((rows, 3 * width), bf16),
-            shape_of((rows, 3 * RANK), f32),
+            shape_of((rows, 6 * RANK), f32),
             shape_of((rows, RANK), f32),
             shape_of((1, 3 * width), f32),
             row_of,
@@ -1405,10 +1448,18 @@
         name="pack_sums",
         us=0.1,
     )
-    sums = finish_rows(send, keep, [give])
-    own, p1, p2, p3 = run(
+    p1, p2, p3, own, own_grads = run(
+        pair_grads_kernel,
+        [where, keep, mp_swap(send, 1), kept, mp_swap(give, 1)],
+        "shhhh",
+        [shape_of((share + unit // 2, D), bf16)] * 3 + [shape_of((share, D), f32), shape_of((unit, BLOCK), f32)],
+        name="pair_grads",
+        us=1.2,
+    )
+    sums = [own, mp_swap(p1, 2), mp_swap(p2, 4), mp_swap(p3, 6)]
+    local_own, p1, p2, p3 = run(
         local_kernel,
-        [where, own, mp_swap(p1, 2), mp_swap(p2, 4), mp_swap(p3, 6), b_f, b_a, a_d, a_o],
+        [where, own_grads] + sums[1:] + [b_f, b_a, a_d, a_o],
         "s" + "h" * 8,
         [shape_of((part, BLOCK), f32)] + [shape_of((part, BLOCK), bf16)] * 3,
         [pltpu.VMEM((N_DP * part, BLOCK), f32)],
@@ -1417,7 +1468,7 @@
     )
     own = run(
         last_sum_kernel,
-        [own, dp_swap(p1, 1), dp_swap(p2, 2), dp_swap(p3, 3)],
+        [local_own, dp_swap(p1, 1), dp_swap(p2, 2), dp_swap(p3, 3)],
         "hhhh",
         [shape_of((part, BLOCK), bf16)],
         name="last_sums",

time: 346 us -> 335 us (0.968)
  starting transfers between devices: 131 us -> 108 us
  waiting for transfers between devices: 76 us -> 97.6 us
  Pallas kernels: 92.9 us -> 87.3 us
  local copies, waits for them, and re-layouts: 32.2 us -> 28.7 us
    ppermute x61 -> x58, starting transfers between devices: 114 us -> 91.6 us  [mp_swap(): return lax.ppermute(values, 'mp', [(i, i ^ step) for i in range(N_MP)])]
    ppermute x61 -> x58, waiting for transfers between devices: 64.4 us -> 86.8 us  [mp_swap(): return lax.ppermute(values, 'mp', [(i, i ^ step) for i in range(N_MP)])]
    pallas_call x36 -> x35, Pallas kernels: 92.9 us -> 87.3 us  [run(): pl.pallas_call(body, out_shape=list(outs), in_specs=[kinds[kind] for kind...]
    unnamed x171 -> x159, local copies, waits for them, and re-layouts: 19.2 us -> 15.7 us
  transfers between devices with their start and end apart: 79 -> 76, of which waited for: 25 -> 24; matrix products, arithmetic and copies ran while one was open for 5% -> 6% of each run, Pallas kernels for 20% -> 20%
where the time goes in v1:
time: 335 us; the launch traced here: 331 us
  starting transfers between devices  108 us (32%)
  waiting for transfers between devices  97.6 us (29%)
  Pallas kernels  87.3 us (26%)
  local copies, waits for them, and re-layouts  28.7 us (9%)
  other arithmetic  6.56 us (2%)
    ppermute x58, starting transfers between devices, mp_swap(): return lax.ppermute(values, 'mp', [(i, i ^ step) for i in range(N_MP)])  91.6 us
    pallas_call x35, Pallas kernels, run(): pl.pallas_call(body, out_shape=list(outs), in_specs=[kinds[kind] for kind...  87.3 us
    ppermute x58, waiting for transfers between devices, mp_swap(): return lax.ppermute(values, 'mp', [(i, i ^ step) for i in range(N_MP)])  86.8 us
    ppermute x18, starting transfers between devices, dp_swap(): return lax.ppermute(values, 'dp', [(i, i ^ step) for i in range(N_DP)])  16.7 us
    unnamed x159, local copies, waits for them, and re-layouts  15.7 us
    ppermute x18, waiting for transfers between devices, dp_swap(): return lax.ppermute(values, 'dp', [(i, i ^ step) for i in range(N_DP)])  10.8 us
  transfers between devices with their start and end apart: 76, of which 24 were waited for; matrix products, arithmetic and copies ran while one was open for 6% of the time, Pallas kernels for 20%

profile of v1, /device:TPU:1, one launch (start us, length us, event | category | flops | bytes accessed | tf_op | source)
XLA Modules:
  0.0 330.6 jit_solution(2069581874555503921)
XLA Ops:
  1.8 3.2 collective-permute-start
  11.7 2.9 collective-permute-start.4
  24.9 3.6 %collective-permute-start.7 = (bf16[3,256,256]{2,1,0:T(8,128)(2,1)S(1)}, bf16[3,256,256]{2,1,0:T(8,128)(2,1)S(1)}, u32[]{:S(2)}, u32[]{:S(2)}) collective-permute-start(bf16[3,256,256]{2,1,0:T(8,128)(2,1)S(1)} %get-tuple-element.104), channel_id=1, source_target_pairs={{0,1},{1,0},{2,3},{3,2},{4,5},{5,4},{6,7},{7,6},{8,9},{9,8},{10,11... | collective-permute-start | bytes 1179656 | tf_op jit(solution)/shard_map/ppermute | solution.py:1113
  30.9 2.1 gather_fusion
  35.4 2.2 constant_dynamic-slice_fusion.1
  37.5 3.1 collective-permute-start.28
  40.7 2.0 collective-permute-start.29
  49.0 2.8 collective-permute-done.12
  52.9 2.1 adapter_rows.1
  57.1 2.5 collective-permute-start.15
  64.6 2.3 collective-permute-done.30.refs_4_
  69.5 1.9 collective-permute-start.33
  71.4 5.2 %adapters.1 = (bf16[16,17664]{1,0:T(8,128)(2,1)S(1)}, f32[1,21504]{1,0:T(1,128)S(1)}) custom-call(s32[138,1]{1,0:T(8,128)S(1)} %get-tuple-element.210.refs_0_, s32[138,1]{1,0:T(8,128)S(1)} %get-tuple-element.209.refs_1_, s32[21,1]{1,0:T(8,128)S(1)} %copy-done.37, bf16[320,1024]{1,0:T(8,128)(2,1)} %get-tuple-element.107.refs_3_, ...), custom_call_target="tpu_custom_call" | custom-call | flops 300000000 | bytes 300000 | tf_op jit(solution)/shard_map/adapters/pallas_call | solution.py:490
  78.3 7.9 %attention.1 = (bf16[200,2048]{1,0:T(8,128)(2,1)S(1)}, f32[192,2048]{1,0:T(8,128)S(1)}, f32[384,768]{1,0:T(8,128)S(1)}, bf16[384,768]{1,0:T(8,128)(2,1)S(1)}, f3...) custom-call(s32[12]{0:T(128)S(1)} %stack.57.refs_0_, ...), custom_call_target="tpu_custom_call" | custom-call | flops 10000000000 | bytes 10000000 | tf_op jit(solution)/shard_map/attention/pallas_call | solution.py:490
  90.9 9.1 %collective-permute-start.19 = (bf16[56,2048]{1,0:T(8,128)(2,1)S(1)}, bf16[56,2048]{1,0:T(8,128)(2,1)S(1)}, u32[]{:S(2)}, u32[]{:S(2)}) collective-permute-start(bf16[56,2048]{1,0:T(8,128)(2,1)S(1)} %get-tuple-element.117), channel_id=1, source_target_pairs={{0,4},{1,5},{2,6},{3,7},{4,0},{5,1},{6,2},{7,3},{8,12},{9,13},{10,... | collective-permute-start | bytes 688136 | tf_op jit(solution)/shard_map/ppermute | solution.py:1113
  100.1 5.2 %collective-permute-done.34.refs_1_.refs_4_.refs_13_.refs_6_ = bf16[2,256,768]{2,1,0:T(8,128)(2,1)S(1)} collective-permute-done((bf16[2,256,768]{2,1,0:T(8,128)(2,1)S(1)}, bf16[2,256,768]{2,1,0:T(8,128)(2,1)S(1)}, u32[]{:S(2)}, u32[]{:S(2)}) %collective-permute-start.34) | collective-permute-done | bytes 786464 | tf_op jit(solution)/shard_map/ppermute | solution.py:1116
  105.2 5.4 %collective-permute-done.19.refs_3_.refs_2_ = bf16[56,2048]{1,0:T(8,128)(2,1)S(1)} collective-permute-done((bf16[56,2048]{1,0:T(8,128)(2,1)S(1)}, bf16[56,2048]{1,0:T(8,128)(2,1)S(1)}, u32[]{:S(2)}, u32[]{:S(2)}) %collective-permute-start.19) | collective-permute-done | bytes 229408 | tf_op jit(solution)/shard_map/ppermute | solution.py:1113
  114.7 2.6 collective-permute-start.18
  117.3 2.4 collective-permute-start.20
  121.8 7.0 %collective-permute-done.20.refs_4_ = bf16[56,2048]{1,0:T(8,128)(2,1)} collective-permute-done((bf16[56,2048]{1,0:T(8,128)(2,1)}, bf16[56,2048]{1,0:T(8,128)(2,1)}, u32[]{:S(2)}, u32[]{:S(2)}) %collective-permute-start.20) | collective-permute-done | bytes 229408 | tf_op jit(solution)/shard_map/ppermute | solution.py:1113
  133.4 2.4 collective-permute-start.23
  135.8 2.6 collective-permute-done.21.refs_6_.refs_2_
  138.4 6.3 %collective-permute-start.24 = (bf16[48,2048]{1,0:T(8,128)(2,1)S(1)}, bf16[48,2048]{1,0:T(8,128)(2,1)S(1)}, u32[]{:S(2)}, u32[]{:S(2)}) collective-permute-start(bf16[48,2048]{1,0:T(8,128)(2,1)S(1)} %get-tuple-element.119.refs_1_), channel_id=1, source_target_pairs={{0,1},{1,0},{2,3},{3,2},{4,5},{5,4},{6,7},{7,6},{8,9},{9,8},{10,11... | collective-permute-start | bytes 589832 | tf_op jit(solution)/shard_map/ppermute | solution.py:1113
  147.8 3.6 %down_back.1 = (f32[384,768]{1,0:T(8,128)S(1)}, bf16[384,2048]{1,0:T(8,128)(2,1)S(1)}, f32[384,16]{1,0:T(8,128)S(1)}) custom-call(s32[12]{0:T(128)S(1)} %stack.57.refs_0_, bf16[384,2048]{1,0:T(8,128)(2,1)S(1)} %copy-done.39, f32[1,2048]{1,0:T(1,128)S(1)} %get-tuple-element.123.refs_2_.refs_4_.refs_12_, bf16[704,2048]{1,0:T(8,128)(2,1)S(1)} %copy-done.1, ...), custom_call_target="tpu_custom_call" | custom-call | flops 3500000000 | bytes 3500000 | tf_op jit(solution)/shard_map/down_back/pallas_call | solution.py:490
  152.0 3.2 wide_norms.1.refs_17_.refs_9_
  155.2 10.5 %feed_forward.1 = (bf16[192,2048]{1,0:T(8,128)(2,1)S(1)}, f32[192,2048]{1,0:T(8,128)S(1)}, bf16[384,2048]{1,0:T(8,128)(2,1)S(1)}, bf16[384,768]{1,0:T(8,128)(2,1...) custom-call(s32[12]{0:T(128)S(1)} %stack.57.refs_0_, ...), custom_call_target="tpu_custom_call" | custom-call | flops 14000000000 | bytes 14000000 | tf_op jit(solution)/shard_map/feed_forward/pallas_call | solution.py:490
  166.2 3.5 %down.1 = (bf16[192,2048]{1,0:T(8,128)(2,1)S(1)}, f32[192,2048]{1,0:T(8,128)S(1)}, f32[384,16]{1,0:T(8,128)S(1)}, f32[1,2048]{1,0:T(1,128)S(1)}) custom-call(s32[12]{0:T(128)S(1)} %stack.57.refs_0_, bf16[384,768]{1,0:T(8,128)(2,1)S(1)} %get-tuple-element.128.refs_1_, bf16[704,2048]{1,0:T(8,128)(2,1)S(1)} %copy-done.1, ...), custom_call_target="tpu_custom_call" | custom-call | flops 3500000000 | bytes 3500000 | tf_op jit(solution)/shard_map/down/pallas_call | solution.py:490
  174.8 5.9 %collective-permute-done.37.refs_14_.refs_1_ = bf16[48,2048]{1,0:T(8,128)(2,1)S(1)} collective-permute-done((bf16[48,2048]{1,0:T(8,128)(2,1)S(1)}, bf16[48,2048]{1,0:T(8,128)(2,1)S(1)}, u32[]{:S(2)}, u32[]{:S(2)}) %collective-permute-start.37) | collective-permute-done | bytes 196640 | tf_op jit(solution)/shard_map/ppermute | solution.py:1113
  180.7 7.9 %column_grads.2 = (f32[64,1024]{1,0:T(8,128)S(1)}, f32[24,1024]{1,0:T(8,128)S(1)}, f32[1,1536]{1,0:T(1,128)S(1)}) custom-call(s32[12]{0:T(128)S(1)} %stack.57.refs_0_, bf16[384,2048]{1,0:T(8,128)(2,1)S(1)} %get-tuple-element.138.refs_1_, bf16[2,256,768]{2,1,0:T(8,128)(2,1)S(1)} %get-tuple-element.121.refs_0_.refs_1_.refs_9_.refs_2_, ...), custom_call_target="tpu_custom_call" | custom-call | flops 1000000000 | bytes 1000000 | tf_op jit(solution)/shard_map/column_grads/pallas_call | solution.py:490
  189.1 2.0 collective-permute-start.42
  191.1 2.9 collective-permute-start.40
  194.0 2.5 collective-permute-done.42.refs_4_
  196.5 4.6 %collective-permute-start.46 = (bf16[56,2048]{1,0:T(8,128)(2,1)S(1)}, bf16[56,2048]{1,0:T(8,128)(2,1)S(1)}, u32[]{:S(2)}, u32[]{:S(2)}) collective-permute-start(bf16[56,2048]{1,0:T(8,128)(2,1)S(1)} %collective-permute-done.42.refs_4_), channel_id=1, source_target_pairs={{0,1},{1,0},{2,3},{3,2},{4,5},{5,4},{6,7},{7,6},{8,9},{9,8},{10,11... | collective-permute-start | bytes 688136 | tf_op jit(solution)/shard_map/ppermute | solution.py:1113
  201.1 2.0 collective-permute-done.40.refs_2_
  204.1 9.0 %collective-permute-done.41.refs_3_ = bf16[56,2048]{1,0:T(8,128)(2,1)S(1)} collective-permute-done((bf16[56,2048]{1,0:T(8,128)(2,1)S(1)}, bf16[56,2048]{1,0:T(8,128)(2,1)S(1)}, u32[]{:S(2)}, u32[]{:S(2)}) %collective-permute-start.41) | collective-permute-done | bytes 229408 | tf_op jit(solution)/shard_map/ppermute | solution.py:1113
  215.9 6.9 %attention_back.1 = (bf16[192,2048]{1,0:T(8,128)(2,1)S(1)}, f32[192,2048]{1,0:T(8,128)S(1)}, bf16[384,2048]{1,0:T(8,128)(2,1)S(1)}, bf16[384,768]{1,0:T(8,128)(2...) custom-call(s32[12]{0:T(128)S(1)} %stack.57.refs_0_, ...), custom_call_target="tpu_custom_call" | custom-call | flops 100000000 | bytes 100000 | tf_op jit(solution)/shard_map/attention_back/pallas_call | solution.py:490
  223.0 2.2 row_grads.2
  225.2 6.1 %column_grads.3 = (f32[96,1024]{1,0:T(8,128)S(1)}, f32[12,1024]{1,0:T(8,128)S(1)}, f32[1,768]{1,0:T(1,128)S(1)}) custom-call(s32[12]{0:T(128)S(1)} %stack.57.refs_0_, bf16[384,2048]{1,0:T(8,128)(2,1)S(1)} %copy-done.10, bf16[3,256,256]{2,1,0:T(8,128)(2,1)S(1)} %get-tuple-element.103.refs_0_.refs_6_.refs_2_.refs_9_, bf16[3,256,256]{2,1,0:T(8,128)(2,1)S(1)} %copy-done.13, ...), custom_call_target="tpu_custom_call" | custom-call | flops 1000000000 | bytes 1000000 | tf_op jit(solution)/shard_map/column_grads/pallas_call | solution.py:490
  231.3 3.7 %row_grads.3 = (f32[12,1024]{1,0:T(8,128)S(1)}, f32[32,1024]{1,0:T(8,128)S(1)}) custom-call(s32[12]{0:T(128)S(1)} %stack.57.refs_0_, bf16[384,768]{1,0:T(8,128)(2,1)S(1)} %get-tuple-element.128.refs_1_, bf16[704,2048]{1,0:T(8,128)(2,1)S(1)} %copy-done.1, bf16[16,17664]{1,0:T(8,128)(2,1)S(1)} %get-tuple-element.109.refs_2_.refs_9_.refs_5_.refs_4_.refs_3_.refs_16_.refs_8_, ...), custom_call_target="tpu_custom_call" | custom-call | flops 100000000 | bytes 100000 | tf_op jit(solution)/shard_map/row_grads/pallas_call | solution.py:490
  241.9 5.9 %collective-permute-done.53.refs_8_ = bf16[48,2048]{1,0:T(8,128)(2,1)S(1)} collective-permute-done((bf16[48,2048]{1,0:T(8,128)(2,1)S(1)}, bf16[48,2048]{1,0:T(8,128)(2,1)S(1)}, u32[]{:S(2)}, u32[]{:S(2)}) %collective-permute-start.53) | collective-permute-done | bytes 196640 | tf_op jit(solution)/shard_map/ppermute | solution.py:1113
  247.8 1.9 collective-permute-start.55
  249.7 26.5 %collective-permute-done.54.refs_9_ = bf16[48,2048]{1,0:T(8,128)(2,1)S(1)} collective-permute-done((bf16[48,2048]{1,0:T(8,128)(2,1)S(1)}, bf16[48,2048]{1,0:T(8,128)(2,1)S(1)}, u32[]{:S(2)}, u32[]{:S(2)}) %collective-permute-start.54) | collective-permute-done | bytes 196640 | tf_op jit(solution)/shard_map/ppermute | solution.py:1113
  276.9 5.3 %collective-permute-start.57 = (bf16[96,2048]{1,0:T(8,128)(2,1)S(1)}, bf16[96,2048]{1,0:T(8,128)(2,1)S(1)}, u32[]{:S(2)}, u32[]{:S(2)}) collective-permute-start(bf16[96,2048]{1,0:T(8,128)(2,1)S(1)} %last_rows.1.refs_1_), channel_id=1, source_target_pairs={{0,4},{1,5},{2,6},{3,7},{4,0},{5,1},{6,2},{7,3},{8,12},{9,13},{10,... | collective-permute-start | bytes 1179656 | tf_op jit(solution)/shard_map/ppermute | solution.py:1113
  291.4 10.5 %collective-permute-done.67 = bf16[24,1024]{1,0:T(8,128)(2,1)S(1)} collective-permute-done((bf16[24,1024]{1,0:T(8,128)(2,1)S(1)}, bf16[24,1024]{1,0:T(8,128)(2,1)S(1)}, u32[]{:S(2)}, u32[]{:S(2)}) %collective-permute-start.67) | collective-permute-done | bytes 49184 | tf_op jit(solution)/shard_map/ppermute | solution.py:1113
  306.9 4.6 %collective-permute-start.72 = (bf16[96,1024]{1,0:T(8,128)(2,1)S(1)}, bf16[96,1024]{1,0:T(8,128)(2,1)S(1)}, u32[]{:S(2)}, u32[]{:S(2)}) collective-permute-start(bf16[96,1024]{1,0:T(8,128)(2,1)S(1)} %pad_maximum_fusion.2.refs_2_), channel_id=1, source_target_pairs={{0,1},{1,0},{2,3},{3,2},{4,5},{5,4},{6,7},{7,6},{8,9},{9,8},{10,11... | collective-permute-start | bytes 589832 | tf_op jit(solution)/shard_map/ppermute | solution.py:1113
  312.2 2.2 collective-permute-start.74
  324.3 3.0 update.1
  327.3 3.0 join_rows.1
  (349 shorter events, 102.3 us)
Async XLA Ops:
  7.6 15.9 %collective-permute-start.2 = (bf16[3,64,512]{2,1,0:T(8,128)(2,1)S(1)}, bf16[3,64,512]{2,1,0:T(8,128)(2,1)S(1)}, u32[]{:S(2)}, u32[]{:S(2)}) collective-permute-start(bf16[3,64,512]{2,1,0:T(8,128)(2,1)S(1)} %get-tuple-element.204), channel_id=1, source_target_pairs={{0,2},{1,3},{2,0},{3,1},{4,6},{5,7},{6,4},{7,5},{8,10},{9,11},{10,... | collective-permute-start | bytes 589832 | tf_op jit(solution)/shard_map/ppermute | solution.py:1113
  8.9 14.6 %collective-permute-start.3 = (bf16[3,64,512]{2,1,0:T(8,128)(2,1)S(1)}, bf16[3,64,512]{2,1,0:T(8,128)(2,1)S(1)}, u32[]{:S(2)}, u32[]{:S(2)}) collective-permute-start(bf16[3,64,512]{2,1,0:T(8,128)(2,1)S(1)} %get-tuple-element.206), channel_id=1, source_target_pairs={{0,4},{1,5},{2,6},{3,7},{4,0},{5,1},{6,2},{7,3},{8,12},{9,13},{10,... | collective-permute-start | bytes 589832 | tf_op jit(solution)/shard_map/ppermute | solution.py:1113
  11.7 12.6 %collective-permute-start.4 = (bf16[3,64,512]{2,1,0:T(8,128)(2,1)S(1)}, bf16[3,64,512]{2,1,0:T(8,128)(2,1)S(1)}, u32[]{:S(2)}, u32[]{:S(2)}) collective-permute-start(bf16[3,64,512]{2,1,0:T(8,128)(2,1)S(1)} %get-tuple-element.203), channel_id=1, source_target_pairs={{0,6},{1,7},{2,4},{3,5},{4,2},{5,3},{6,0},{7,1},{8,14},{9,15},{10,... | collective-permute-start | bytes 589832 | tf_op jit(solution)/shard_map/ppermute | solution.py:1113
  14.6 20.4 %collective-permute-start.13 = (bf16[80,1024]{1,0:T(8,128)(2,1)S(1)}, bf16[80,1024]{1,0:T(8,128)(2,1)S(1)}, u32[]{:S(2)}, u32[]{:S(2)}) collective-permute-start(bf16[80,1024]{1,0:T(8,128)(2,1)S(1)} %constant_dynamic-update-slice_fusion.refs_2_.refs_0_.refs_3_), channel_id=1, source_target_pairs={{0,16},{8,24},{16,0},{24,8},{1,17},{9,25},{17,1},{25,9},{2,18},{10... | collective-permute-start | bytes 491528 | tf_op jit(solution)/shard_map/ppermute | solution.py:1116
  16.0 24.7 %collective-permute-start.11 = (bf16[80,1024]{1,0:T(8,128)(2,1)S(1)}, bf16[80,1024]{1,0:T(8,128)(2,1)}, u32[]{:S(2)}, u32[]{:S(2)}) collective-permute-start(bf16[80,1024]{1,0:T(8,128)(2,1)S(1)} %pad_maximum_fusion.3.refs_0_), channel_id=1, source_target_pairs={{0,8},{8,0},{16,24},{24,16},{1,9},{9,1},{17,25},{25,17},{2,10},{10... | collective-permute-start | bytes 491528 | tf_op jit(solution)/shard_map/ppermute | solution.py:1116
  28.9 14.6 %collective-permute-start.5 = (bf16[3,256,256]{2,1,0:T(8,128)(2,1)S(1)}, bf16[3,256,256]{2,1,0:T(8,128)(2,1)S(1)}, u32[]{:S(2)}, u32[]{:S(2)}) collective-permute-start(bf16[3,256,256]{2,1,0:T(8,128)(2,1)S(1)} %get-tuple-element.103.refs_0_.refs_6_.refs_2_.refs_9_), channel_id=1, source_target_pairs={{0,8},{8,0},{16,24},{24,16},{1,9},{9,1},{17,25},{25,17},{2,10},{10... | collective-permute-start | bytes 1179656 | tf_op jit(solution)/shard_map/ppermute | solution.py:1116
  33.8 11.0 %collective-permute-start.8 = (bf16[3,256,256]{2,1,0:T(8,128)(2,1)S(1)}, bf16[3,256,256]{2,1,0:T(8,128)(2,1)S(1)}, u32[]{:S(2)}, u32[]{:S(2)}) collective-permute-start(bf16[3,256,256]{2,1,0:T(8,128)(2,1)S(1)} %collective-permute-done.7.refs_0_.refs_5_.refs_12_), channel_id=1, source_target_pairs={{0,16},{8,24},{16,0},{24,8},{1,17},{9,25},{17,1},{25,9},{2,18},{10... | collective-permute-start | bytes 1179656 | tf_op jit(solution)/shard_map/ppermute | solution.py:1116
  35.1 12.0 %collective-permute-start.14 = (bf16[2,80,1024]{2,1,0:T(8,128)(2,1)S(1)}, bf16[2,80,1024]{2,1,0:T(8,128)(2,1)S(1)}, u32[]{:S(2)}, u32[]{:S(2)}) collective-permute-start(bf16[2,80,1024]{2,1,0:T(8,128)(2,1)S(1)} %stack.61), channel_id=1, source_target_pairs={{0,8},{8,0},{16,24},{24,16},{1,9},{9,1},{17,25},{25,17},{2,10},{10... | collective-permute-start | bytes 983048 | tf_op jit(solution)/shard_map/ppermute | solution.py:1116
  37.5 18.9 %collective-permute-start.28 = (bf16[2,64,1408]{2,1,0:T(8,128)(2,1)S(1)}, bf16[2,64,1408]{2,1,0:T(8,128)(2,1)S(1)}, u32[]{:S(2)}, u32[]{:S(2)}) collective-permute-start(bf16[2,64,1408]{2,1,0:T(8,128)(2,1)S(1)} %get-tuple-element.201), channel_id=1, source_target_pairs={{0,2},{1,3},{2,0},{3,1},{4,6},{5,7},{6,4},{7,5},{8,10},{9,11},{10,... | collective-permute-start | bytes 1081352 | tf_op jit(solution)/shard_map/ppermute | solution.py:1113
  40.7 19.0 %collective-permute-start.29 = (bf16[2,64,1408]{2,1,0:T(8,128)(2,1)S(1)}, bf16[2,64,1408]{2,1,0:T(8,128)(2,1)S(1)}, u32[]{:S(2)}, u32[]{:S(2)}) collective-permute-start(bf16[2,64,1408]{2,1,0:T(8,128)(2,1)S(1)} %get-tuple-element.200), channel_id=1, source_target_pairs={{0,4},{1,5},{2,6},{3,7},{4,0},{5,1},{6,2},{7,3},{8,12},{9,13},{10,... | collective-permute-start | bytes 1081352 | tf_op jit(solution)/shard_map/ppermute | solution.py:1113
  44.8 33.4 %collective-permute-start.6 = (bf16[2,3,256,256]{3,2,1,0:T(8,128)(2,1)}, bf16[2,3,256,256]{3,2,1,0:T(8,128)(2,1)}, u32[]{:S(2)}, u32[]{:S(2)}) collective-permute-start(bf16[2,3,256,256]{3,2,1,0:T(8,128)(2,1)} %stack.58), channel_id=1, source_target_pairs={{0,16},{8,24},{16,0},{24,8},{1,17},{9,25},{17,1},{25,9},{2,18},{10... | collective-permute-start | bytes 2359304 | tf_op jit(solution)/shard_map/ppermute | solution.py:1116
  47.1 31.2 %collective-permute-start.9 = (bf16[2,3,256,256]{3,2,1,0:T(8,128)(2,1)}, bf16[2,3,256,256]{3,2,1,0:T(8,128)(2,1)}, u32[]{:S(2)}, u32[]{:S(2)}) collective-permute-start(bf16[2,3,256,256]{3,2,1,0:T(8,128)(2,1)} %stack.59), channel_id=1, source_target_pairs={{0,8},{8,0},{16,24},{24,16},{1,9},{9,1},{17,25},{25,17},{2,10},{10... | collective-permute-start | bytes 2359304 | tf_op jit(solution)/shard_map/ppermute | solution.py:1116
  51.7 15.1 %collective-permute-start.30 = (bf16[2,64,1408]{2,1,0:T(8,128)(2,1)}, bf16[2,64,1408]{2,1,0:T(8,128)(2,1)S(1)}, u32[]{:S(2)}, u32[]{:S(2)}) collective-permute-start(bf16[2,64,1408]{2,1,0:T(8,128)(2,1)} %get-tuple-element.199), channel_id=1, source_target_pairs={{0,6},{1,7},{2,4},{3,5},{4,2},{5,3},{6,0},{7,1},{8,14},{9,15},{10,... | collective-permute-start | bytes 1081352 | tf_op jit(solution)/shard_map/ppermute | solution.py:1113
  57.1 14.2 %collective-permute-start.15 = (bf16[320,1024]{1,0:T(8,128)(2,1)}, bf16[320,1024]{1,0:T(8,128)(2,1)}, u32[]{:S(2)}, u32[]{:S(2)}) collective-permute-start(bf16[320,1024]{1,0:T(8,128)(2,1)} %get-tuple-element.107.refs_3_), channel_id=1, source_target_pairs={{0,1},{1,0},{2,3},{3,2},{4,5},{5,4},{6,7},{7,6},{8,9},{9,8},{10,11... | collective-permute-start | bytes 1966088 | tf_op jit(solution)/shard_map/ppermute | solution.py:1113
  60.4 11.0 %collective-permute-start.16 = (bf16[320,1024]{1,0:T(8,128)(2,1)}, bf16[320,1024]{1,0:T(8,128)(2,1)}, u32[]{:S(2)}, u32[]{:S(2)}) collective-permute-start(bf16[320,1024]{1,0:T(8,128)(2,1)} %get-tuple-element.108.refs_4_), channel_id=1, source_target_pairs={{0,1},{1,0},{2,3},{3,2},{4,5},{5,4},{6,7},{7,6},{8,9},{9,8},{10,11... | collective-permute-start | bytes 1966088 | tf_op jit(solution)/shard_map/ppermute | solution.py:1113
  69.5 17.0 %collective-permute-start.33 = (bf16[2,256,768]{2,1,0:T(8,128)(2,1)S(1)}, bf16[2,256,768]{2,1,0:T(8,128)(2,1)S(1)}, u32[]{:S(2)}, u32[]{:S(2)}) collective-permute-start(bf16[2,256,768]{2,1,0:T(8,128)(2,1)S(1)} %get-tuple-element.122), channel_id=1, source_target_pairs={{0,1},{1,0},{2,3},{3,2},{4,5},{5,4},{6,7},{7,6},{8,9},{9,8},{10,11... | collective-permute-start | bytes 2359304 | tf_op jit(solution)/shard_map/ppermute | solution.py:1113
  86.5 18.8 %collective-permute-start.34 = (bf16[2,256,768]{2,1,0:T(8,128)(2,1)S(1)}, bf16[2,256,768]{2,1,0:T(8,128)(2,1)S(1)}, u32[]{:S(2)}, u32[]{:S(2)}) collective-permute-start(bf16[2,256,768]{2,1,0:T(8,128)(2,1)S(1)} %collective-permute-done.33.refs_0_.refs_3_.refs_12_.refs_5_), channel_id=1, source_target_pairs={{0,16},{8,24},{16,0},{24,8},{1,17},{9,25},{17,1},{25,9},{2,18},{10... | collective-permute-start | bytes 2359304 | tf_op jit(solution)/shard_map/ppermute | solution.py:1116
  86.7 26.6 %collective-permute-start.31 = (bf16[2,256,768]{2,1,0:T(8,128)(2,1)S(1)}, bf16[2,256,768]{2,1,0:T(8,128)(2,1)S(1)}, u32[]{:S(2)}, u32[]{:S(2)}) collective-permute-start(bf16[2,256,768]{2,1,0:T(8,128)(2,1)S(1)} %get-tuple-element.121.refs_0_.refs_1_.refs_9_.refs_2_), channel_id=1, source_target_pairs={{0,8},{8,0},{16,24},{24,16},{1,9},{9,1},{17,25},{25,17},{2,10},{10... | collective-permute-start | bytes 2359304 | tf_op jit(solution)/shard_map/ppermute | solution.py:1116
  90.9 19.7 %collective-permute-start.19 = (bf16[56,2048]{1,0:T(8,128)(2,1)S(1)}, bf16[56,2048]{1,0:T(8,128)(2,1)S(1)}, u32[]{:S(2)}, u32[]{:S(2)}) collective-permute-start(bf16[56,2048]{1,0:T(8,128)(2,1)S(1)} %get-tuple-element.117), channel_id=1, source_target_pairs={{0,4},{1,5},{2,6},{3,7},{4,0},{5,1},{6,2},{7,3},{8,12},{9,13},{10,... | collective-permute-start | bytes 688136 | tf_op jit(solution)/shard_map/ppermute | solution.py:1113
  111.9 40.0 %collective-permute-start.35 = (bf16[2,2,256,768]{3,2,1,0:T(8,128)(2,1)}, bf16[2,2,256,768]{3,2,1,0:T(8,128)(2,1)}, u32[]{:S(2)}, u32[]{:S(2)}) collective-permute-start(bf16[2,2,256,768]{3,2,1,0:T(8,128)(2,1)} %stack.63), channel_id=1, source_target_pairs={{0,8},{8,0},{16,24},{24,16},{1,9},{9,1},{17,25},{25,17},{2,10},{10... | collective-permute-start | bytes 4718600 | tf_op jit(solution)/shard_map/ppermute | solution.py:1116
  114.7 37.3 %collective-permute-start.32 = (bf16[2,2,256,768]{3,2,1,0:T(8,128)(2,1)}, bf16[2,2,256,768]{3,2,1,0:T(8,128)(2,1)}, u32[]{:S(2)}, u32[]{:S(2)}) collective-permute-start(bf16[2,2,256,768]{3,2,1,0:T(8,128)(2,1)} %stack.62), channel_id=1, source_target_pairs={{0,16},{8,24},{16,0},{24,8},{1,17},{9,25},{17,1},{25,9},{2,18},{10... | collective-permute-start | bytes 4718600 | tf_op jit(solution)/shard_map/ppermute | solution.py:1116
  117.3 11.5 %collective-permute-start.20 = (bf16[56,2048]{1,0:T(8,128)(2,1)}, bf16[56,2048]{1,0:T(8,128)(2,1)}, u32[]{:S(2)}, u32[]{:S(2)}) collective-permute-start(bf16[56,2048]{1,0:T(8,128)(2,1)} %get-tuple-element.118), channel_id=1, source_target_pairs={{0,6},{1,7},{2,4},{3,5},{4,2},{5,3},{6,0},{7,1},{8,14},{9,15},{10,... | collective-permute-start | bytes 688136 | tf_op jit(solution)/shard_map/ppermute | solution.py:1113
  132.3 19.0 %collective-permute-start.22 = (bf16[48,2048]{1,0:T(8,128)(2,1)S(1)}, bf16[48,2048]{1,0:T(8,128)(2,1)S(1)}, u32[]{:S(2)}, u32[]{:S(2)}) collective-permute-start(bf16[48,2048]{1,0:T(8,128)(2,1)S(1)} %get-tuple-element.119.refs_1_), channel_id=1, source_target_pairs={{0,4},{1,5},{2,6},{3,7},{4,0},{5,1},{6,2},{7,3},{8,12},{9,13},{10,... | collective-permute-start | bytes 589832 | tf_op jit(solution)/shard_map/ppermute | solution.py:1113
  133.4 18.0 %collective-permute-start.23 = (bf16[48,2048]{1,0:T(8,128)(2,1)S(1)}, bf16[48,2048]{1,0:T(8,128)(2,1)S(1)}, u32[]{:S(2)}, u32[]{:S(2)}) collective-permute-start(bf16[48,2048]{1,0:T(8,128)(2,1)S(1)} %get-tuple-element.119.refs_1_), channel_id=1, source_target_pairs={{0,6},{1,7},{2,4},{3,5},{4,2},{5,3},{6,0},{7,1},{8,14},{9,15},{10,... | collective-permute-start | bytes 589832 | tf_op jit(solution)/shard_map/ppermute | solution.py:1113
  138.4 16.8 %collective-permute-start.24 = (bf16[48,2048]{1,0:T(8,128)(2,1)S(1)}, bf16[48,2048]{1,0:T(8,128)(2,1)S(1)}, u32[]{:S(2)}, u32[]{:S(2)}) collective-permute-start(bf16[48,2048]{1,0:T(8,128)(2,1)S(1)} %get-tuple-element.119.refs_1_), channel_id=1, source_target_pairs={{0,1},{1,0},{2,3},{3,2},{4,5},{5,4},{6,7},{7,6},{8,9},{9,8},{10,11... | collective-permute-start | bytes 589832 | tf_op jit(solution)/shard_map/ppermute | solution.py:1113
  169.7 44.1 %collective-permute-start.47 = (bf16[192,2048]{1,0:T(8,128)(2,1)S(1)}, bf16[192,2048]{1,0:T(8,128)(2,1)S(1)}, u32[]{:S(2)}, u32[]{:S(2)}) collective-permute-start(bf16[192,2048]{1,0:T(8,128)(2,1)S(1)} %get-tuple-element.150), channel_id=1, source_target_pairs={{0,1},{1,0},{2,3},{3,2},{4,5},{5,4},{6,7},{7,6},{8,9},{9,8},{10,11... | collective-permute-start | bytes 2359304 | tf_op jit(solution)/shard_map/ppermute | solution.py:1113
  172.3 16.3 %collective-permute-start.38 = (bf16[48,2048]{1,0:T(8,128)(2,1)S(1)}, bf16[48,2048]{1,0:T(8,128)(2,1)S(1)}, u32[]{:S(2)}, u32[]{:S(2)}) collective-permute-start(bf16[48,2048]{1,0:T(8,128)(2,1)S(1)} %get-tuple-element.132), channel_id=1, source_target_pairs={{0,4},{1,5},{2,6},{3,7},{4,0},{5,1},{6,2},{7,3},{8,12},{9,13},{10,... | collective-permute-start | bytes 589832 | tf_op jit(solution)/shard_map/ppermute | solution.py:1113
  174.2 14.5 %collective-permute-start.39 = (bf16[48,2048]{1,0:T(8,128)(2,1)S(1)}, bf16[48,2048]{1,0:T(8,128)(2,1)S(1)}, u32[]{:S(2)}, u32[]{:S(2)}) collective-permute-start(bf16[48,2048]{1,0:T(8,128)(2,1)S(1)} %get-tuple-element.133), channel_id=1, source_target_pairs={{0,6},{1,7},{2,4},{3,5},{4,2},{5,3},{6,0},{7,1},{8,14},{9,15},{10,... | collective-permute-start | bytes 589832 | tf_op jit(solution)/shard_map/ppermute | solution.py:1113
  191.1 12.0 %collective-permute-start.40 = (bf16[56,2048]{1,0:T(8,128)(2,1)S(1)}, bf16[56,2048]{1,0:T(8,128)(2,1)S(1)}, u32[]{:S(2)}, u32[]{:S(2)}) collective-permute-start(bf16[56,2048]{1,0:T(8,128)(2,1)S(1)} %get-tuple-element.144.refs_3_.refs_1_), channel_id=1, source_target_pairs={{0,2},{1,3},{2,0},{3,1},{4,6},{5,7},{6,4},{7,5},{8,10},{9,11},{10,... | collective-permute-start | bytes 688136 | tf_op jit(solution)/shard_map/ppermute | solution.py:1113
  194.0 19.1 %collective-permute-start.41 = (bf16[56,2048]{1,0:T(8,128)(2,1)S(1)}, bf16[56,2048]{1,0:T(8,128)(2,1)S(1)}, u32[]{:S(2)}, u32[]{:S(2)}) collective-permute-start(bf16[56,2048]{1,0:T(8,128)(2,1)S(1)} %get-tuple-element.144.refs_3_.refs_1_), channel_id=1, source_target_pairs={{0,4},{1,5},{2,6},{3,7},{4,0},{5,1},{6,2},{7,3},{8,12},{9,13},{10,... | collective-permute-start | bytes 688136 | tf_op jit(solution)/shard_map/ppermute | solution.py:1113
  196.5 17.3 %collective-permute-start.46 = (bf16[56,2048]{1,0:T(8,128)(2,1)S(1)}, bf16[56,2048]{1,0:T(8,128)(2,1)S(1)}, u32[]{:S(2)}, u32[]{:S(2)}) collective-permute-start(bf16[56,2048]{1,0:T(8,128)(2,1)S(1)} %collective-permute-done.42.refs_4_), channel_id=1, source_target_pairs={{0,1},{1,0},{2,3},{3,2},{4,5},{5,4},{6,7},{7,6},{8,9},{9,8},{10,11... | collective-permute-start | bytes 688136 | tf_op jit(solution)/shard_map/ppermute | solution.py:1113
  201.1 13.4 %collective-permute-start.43 = (bf16[56,2048]{1,0:T(8,128)(2,1)S(1)}, bf16[56,2048]{1,0:T(8,128)(2,1)S(1)}, u32[]{:S(2)}, u32[]{:S(2)}) collective-permute-start(bf16[56,2048]{1,0:T(8,128)(2,1)S(1)} %get-tuple-element.144.refs_3_.refs_1_), channel_id=1, source_target_pairs={{0,1},{1,0},{2,3},{3,2},{4,5},{5,4},{6,7},{7,6},{8,9},{9,8},{10,11... | collective-permute-start | bytes 688136 | tf_op jit(solution)/shard_map/ppermute | solution.py:1113
  203.1 11.5 %collective-permute-start.44 = (bf16[56,2048]{1,0:T(8,128)(2,1)S(1)}, bf16[56,2048]{1,0:T(8,128)(2,1)S(1)}, u32[]{:S(2)}, u32[]{:S(2)}) collective-permute-start(bf16[56,2048]{1,0:T(8,128)(2,1)S(1)} %collective-permute-done.40.refs_2_), channel_id=1, source_target_pairs={{0,1},{1,0},{2,3},{3,2},{4,5},{5,4},{6,7},{7,6},{8,9},{9,8},{10,11... | collective-permute-start | bytes 688136 | tf_op jit(solution)/shard_map/ppermute | solution.py:1113
  222.8 14.6 %collective-permute-start.48 = (bf16[192,2048]{1,0:T(8,128)(2,1)S(1)}, bf16[192,2048]{1,0:T(8,128)(2,1)S(1)}, u32[]{:S(2)}, u32[]{:S(2)}) collective-permute-start(bf16[192,2048]{1,0:T(8,128)(2,1)S(1)} %get-tuple-element.153), channel_id=1, source_target_pairs={{0,1},{1,0},{2,3},{3,2},{4,5},{5,4},{6,7},{7,6},{8,9},{9,8},{10,11... | collective-permute-start | bytes 2359304 | tf_op jit(solution)/shard_map/ppermute | solution.py:1113
  236.2 11.6 %collective-permute-start.53 = (bf16[48,2048]{1,0:T(8,128)(2,1)S(1)}, bf16[48,2048]{1,0:T(8,128)(2,1)S(1)}, u32[]{:S(2)}, u32[]{:S(2)}) collective-permute-start(bf16[48,2048]{1,0:T(8,128)(2,1)S(1)} %get-tuple-element.181), channel_id=1, source_target_pairs={{0,2},{1,3},{2,0},{3,1},{4,6},{5,7},{6,4},{7,5},{8,10},{9,11},{10,... | collective-permute-start | bytes 589832 | tf_op jit(solution)/shard_map/ppermute | solution.py:1113
  238.2 38.1 %collective-permute-start.50 = (bf16[64,2048]{1,0:T(8,128)(2,1)S(1)}, bf16[64,2048]{1,0:T(8,128)(2,1)S(1)}, u32[]{:S(2)}, u32[]{:S(2)}) collective-permute-start(bf16[64,2048]{1,0:T(8,128)(2,1)S(1)} %get-tuple-element.177), channel_id=1, source_target_pairs={{0,2},{1,3},{2,0},{3,1},{4,6},{5,7},{6,4},{7,5},{8,10},{9,11},{10,... | collective-permute-start | bytes 786440 | tf_op jit(solution)/shard_map/ppermute | solution.py:1113
  238.5 37.7 %collective-permute-start.51 = (bf16[64,2048]{1,0:T(8,128)(2,1)S(1)}, bf16[64,2048]{1,0:T(8,128)(2,1)S(1)}, u32[]{:S(2)}, u32[]{:S(2)}) collective-permute-start(bf16[64,2048]{1,0:T(8,128)(2,1)S(1)} %get-tuple-element.178), channel_id=1, source_target_pairs={{0,4},{1,5},{2,6},{3,7},{4,0},{5,1},{6,2},{7,3},{8,12},{9,13},{10,... | collective-permute-start | bytes 786440 | tf_op jit(solution)/shard_map/ppermute | solution.py:1113
  240.4 35.9 %collective-permute-start.52 = (bf16[64,2048]{1,0:T(8,128)(2,1)S(1)}, bf16[64,2048]{1,0:T(8,128)(2,1)S(1)}, u32[]{:S(2)}, u32[]{:S(2)}) collective-permute-start(bf16[64,2048]{1,0:T(8,128)(2,1)S(1)} %get-tuple-element.179), channel_id=1, source_target_pairs={{0,6},{1,7},{2,4},{3,5},{4,2},{5,3},{6,0},{7,1},{8,14},{9,15},{10,... | collective-permute-start | bytes 786440 | tf_op jit(solution)/shard_map/ppermute | solution.py:1113
  241.8 34.5 %collective-permute-start.54 = (bf16[48,2048]{1,0:T(8,128)(2,1)S(1)}, bf16[48,2048]{1,0:T(8,128)(2,1)S(1)}, u32[]{:S(2)}, u32[]{:S(2)}) collective-permute-start(bf16[48,2048]{1,0:T(8,128)(2,1)S(1)} %get-tuple-element.182), channel_id=1, source_target_pairs={{0,4},{1,5},{2,6},{3,7},{4,0},{5,1},{6,2},{7,3},{8,12},{9,13},{10,... | collective-permute-start | bytes 589832 | tf_op jit(solution)/shard_map/ppermute | solution.py:1113
  247.8 28.4 %collective-permute-start.55 = (bf16[48,2048]{1,0:T(8,128)(2,1)S(1)}, bf16[48,2048]{1,0:T(8,128)(2,1)S(1)}, u32[]{:S(2)}, u32[]{:S(2)}) collective-permute-start(bf16[48,2048]{1,0:T(8,128)(2,1)S(1)} %get-tuple-element.183), channel_id=1, source_target_pairs={{0,6},{1,7},{2,4},{3,5},{4,2},{5,3},{6,0},{7,1},{8,14},{9,15},{10,... | collective-permute-start | bytes 589832 | tf_op jit(solution)/shard_map/ppermute | solution.py:1113
  276.9 27.8 %collective-permute-start.57 = (bf16[96,2048]{1,0:T(8,128)(2,1)S(1)}, bf16[96,2048]{1,0:T(8,128)(2,1)S(1)}, u32[]{:S(2)}, u32[]{:S(2)}) collective-permute-start(bf16[96,2048]{1,0:T(8,128)(2,1)S(1)} %last_rows.1.refs_1_), channel_id=1, source_target_pairs={{0,4},{1,5},{2,6},{3,7},{4,0},{5,1},{6,2},{7,3},{8,12},{9,13},{10,... | collective-permute-start | bytes 1179656 | tf_op jit(solution)/shard_map/ppermute | solution.py:1113
  287.9 14.1 %collective-permute-start.67 = (bf16[24,1024]{1,0:T(8,128)(2,1)S(1)}, bf16[24,1024]{1,0:T(8,128)(2,1)S(1)}, u32[]{:S(2)}, u32[]{:S(2)}) collective-permute-start(bf16[24,1024]{1,0:T(8,128)(2,1)S(1)} %last_sums.1), channel_id=1, source_target_pairs={{0,4},{1,5},{2,6},{3,7},{4,0},{5,1},{6,2},{7,3},{8,12},{9,13},{10,... | collective-permute-start | bytes 147464 | tf_op jit(solution)/shard_map/ppermute | solution.py:1113
  289.7 12.3 %collective-permute-start.68 = (bf16[24,1024]{1,0:T(8,128)(2,1)S(1)}, bf16[24,1024]{1,0:T(8,128)(2,1)S(1)}, u32[]{:S(2)}, u32[]{:S(2)}) collective-permute-start(bf16[24,1024]{1,0:T(8,128)(2,1)S(1)} %last_sums.1), channel_id=1, source_target_pairs={{0,6},{1,7},{2,4},{3,5},{4,2},{5,3},{6,0},{7,1},{8,14},{9,15},{10,... | collective-permute-start | bytes 147464 | tf_op jit(solution)/shard_map/ppermute | solution.py:1113
  291.4 24.4 %collective-permute-start.56 = (bf16[96,2048]{1,0:T(8,128)(2,1)S(1)}, bf16[96,2048]{1,0:T(8,128)(2,1)S(1)}, u32[]{:S(2)}, u32[]{:S(2)}) collective-permute-start(bf16[96,2048]{1,0:T(8,128)(2,1)S(1)} %last_rows.1.refs_1_), channel_id=1, source_target_pairs={{0,2},{1,3},{2,0},{3,1},{4,6},{5,7},{6,4},{7,5},{8,10},{9,11},{10,... | collective-permute-start | bytes 1179656 | tf_op jit(solution)/shard_map/ppermute | solution.py:1113
  304.7 14.6 %collective-permute-start.58 = (bf16[96,2048]{1,0:T(8,128)(2,1)S(1)}, bf16[96,2048]{1,0:T(8,128)(2,1)S(1)}, u32[]{:S(2)}, u32[]{:S(2)}) collective-permute-start(bf16[96,2048]{1,0:T(8,128)(2,1)S(1)} %collective-permute-done.57.refs_3_), channel_id=1, source_target_pairs={{0,2},{1,3},{2,0},{3,1},{4,6},{5,7},{6,4},{7,5},{8,10},{9,11},{10,... | collective-permute-start | bytes 1179656 | tf_op jit(solution)/shard_map/ppermute | solution.py:1113
  315.8 11.5 %collective-permute-start.59 = (bf16[96,2048]{1,0:T(8,128)(2,1)S(1)}, bf16[96,2048]{1,0:T(8,128)(2,1)S(1)}, u32[]{:S(2)}, u32[]{:S(2)}) collective-permute-start(bf16[96,2048]{1,0:T(8,128)(2,1)S(1)} %last_rows.1.refs_1_), channel_id=1, source_target_pairs={{0,1},{1,0},{2,3},{3,2},{4,5},{5,4},{6,7},{7,6},{8,9},{9,8},{10,11... | collective-permute-start | bytes 1179656 | tf_op jit(solution)/shard_map/ppermute | solution.py:1113
  317.0 10.3 %collective-permute-start.61 = (bf16[96,2048]{1,0:T(8,128)(2,1)S(1)}, bf16[96,2048]{1,0:T(8,128)(2,1)S(1)}, u32[]{:S(2)}, u32[]{:S(2)}) collective-permute-start(bf16[96,2048]{1,0:T(8,128)(2,1)S(1)} %collective-permute-done.57.refs_3_), channel_id=1, source_target_pairs={{0,1},{1,0},{2,3},{3,2},{4,5},{5,4},{6,7},{7,6},{8,9},{9,8},{10,11... | collective-permute-start | bytes 1179656 | tf_op jit(solution)/shard_map/ppermute | solution.py:1113
  317.0 10.3 %collective-permute-start.60 = (bf16[96,2048]{1,0:T(8,128)(2,1)S(1)}, bf16[96,2048]{1,0:T(8,128)(2,1)S(1)}, u32[]{:S(2)}, u32[]{:S(2)}) collective-permute-start(bf16[96,2048]{1,0:T(8,128)(2,1)S(1)} %collective-permute-done.56.refs_2_), channel_id=1, source_target_pairs={{0,1},{1,0},{2,3},{3,2},{4,5},{5,4},{6,7},{7,6},{8,9},{9,8},{10,11... | collective-permute-start | bytes 1179656 | tf_op jit(solution)/shard_map/ppermute | solution.py:1113
  (107 other events, 740.1 us)

commit v2 on v1

--- a/solution.py
+++ b/solution.py
@@ -1122,7 +1122,7 @@
     def stack(first, second, after=()):
         shape = (2,) + first.shape
         return run(
-            stack_kernel, [first, second], "hh", [shape_of(shape, bf16)], name="stack", after=after, us=0.6
+            stack_kernel, [first, second], "hh", [shape_of(shape, bf16)], name="stack", after=after, us=0.01
         )[0]
 
     def plane_first(a, b):
@@ -1480,7 +1480,7 @@
         "h" * 13,
         [shape_of((2 * share, D), bf16)],
         name="last_rows",
-        us=0.5,
+        us=20,
     )[0]
     lines = jnp.concatenate([own] + [mp_swap(own, 2 * step) for step in range(1, N_Z)])
     summed = [lines] + [dp_swap(lines, step) for step in range(1, N_DP)]
@@ -1496,7 +1496,7 @@
         [shape_of((rows, D), f32), shape_of((rows, D), bf16)],
         name="join_rows",
         megabytes=8,
-        us=4,
+        us=0.1,
     )
 
     table = np.zeros((n_blocks,), np.int32)

time: 335 us -> 328 us (0.979)
  local copies, waits for them, and re-layouts: 28.7 us -> 18.7 us
  waiting for transfers between devices: 97.6 us -> 101 us
    unnamed x159 -> x123, local copies, waits for them, and re-layouts: 15.7 us -> 8.03 us
  transfers between devices with their start and end apart: 76 -> 76, of which waited for: 24 -> 25; matrix products, arithmetic and copies ran while one was open for 6% -> 5% of each run, Pallas kernels for 20% -> 21%
where the time goes in v2:
time: 328 us; the launch traced here: 324 us
  starting transfers between devices  108 us (33%)
  waiting for transfers between devices  101 us (31%)
  Pallas kernels  88 us (27%)
  local copies, waits for them, and re-layouts  18.7 us (6%)
  other arithmetic  6.01 us (2%)
    ppermute x58, starting transfers between devices, mp_swap(): return lax.ppermute(values, 'mp', [(i, i ^ step) for i in range(N_MP)])  93.5 us
    ppermute x58, waiting for transfers between devices, mp_swap(): return lax.ppermute(values, 'mp', [(i, i ^ step) for i in range(N_MP)])  88.8 us
    pallas_call x35, Pallas kernels, run(): pl.pallas_call(body, out_shape=list(outs), in_specs=[kinds[kind] for kind...  88 us
    ppermute x18, starting transfers between devices, dp_swap(): return lax.ppermute(values, 'dp', [(i, i ^ step) for i in range(N_DP)])  14.2 us
    ppermute x18, waiting for transfers between devices, dp_swap(): return lax.ppermute(values, 'dp', [(i, i ^ step) for i in range(N_DP)])  12.4 us
    unnamed x123, local copies, waits for them, and re-layouts  8.03 us
  transfers between devices with their start and end apart: 76, of which 25 were waited for; matrix products, arithmetic and copies ran while one was open for 5% of the time, Pallas kernels for 21%

profile of v2, /device:TPU:1, one launch (start us, length us, event | category | flops | bytes accessed | tf_op | source)
XLA Modules:
  0.0 323.7 jit_solution(2592871360445613214)
XLA Ops:
  1.8 3.2 collective-permute-start
  11.1 3.5 %collective-permute-start.4 = (bf16[3,64,512]{2,1,0:T(8,128)(2,1)S(1)}, bf16[3,64,512]{2,1,0:T(8,128)(2,1)S(1)}, u32[]{:S(2)}, u32[]{:S(2)}) collective-permute-start(bf16[3,64,512]{2,1,0:T(8,128)(2,1)S(1)} %get-tuple-element.203), channel_id=1, source_target_pairs={{0,6},{1,7},{2,4},{3,5},{4,2},{5,3},{6,0},{7,1},{8,14},{9,15},{10,... | collective-permute-start | bytes 589832 | tf_op jit(solution)/shard_map/ppermute | solution.py:1113
  22.2 2.1 collective-permute-done.4.refs_4_
  24.9 3.7 %collective-permute-start.7 = (bf16[3,256,256]{2,1,0:T(8,128)(2,1)S(1)}, bf16[3,256,256]{2,1,0:T(8,128)(2,1)S(1)}, u32[]{:S(2)}, u32[]{:S(2)}) collective-permute-start(bf16[3,256,256]{2,1,0:T(8,128)(2,1)S(1)} %get-tuple-element.104), channel_id=1, source_target_pairs={{0,1},{1,0},{2,3},{3,2},{4,5},{5,4},{6,7},{7,6},{8,9},{9,8},{10,11... | collective-permute-start | bytes 1179656 | tf_op jit(solution)/shard_map/ppermute | solution.py:1113
  33.8 2.4 constant_dynamic-slice_fusion.1
  36.3 3.1 collective-permute-start.28
  39.4 2.0 collective-permute-start.29
  44.6 2.1 gather_fusion
  52.3 2.2 collective-permute-start.30
  54.5 2.2 adapter_rows.1
  56.7 3.5 %collective-permute-start.15 = (bf16[320,1024]{1,0:T(8,128)(2,1)}, bf16[320,1024]{1,0:T(8,128)(2,1)}, u32[]{:S(2)}, u32[]{:S(2)}) collective-permute-start(bf16[320,1024]{1,0:T(8,128)(2,1)} %get-tuple-element.107.refs_3_), channel_id=1, source_target_pairs={{0,1},{1,0},{2,3},{3,2},{4,5},{5,4},{6,7},{7,6},{8,9},{9,8},{10,11... | collective-permute-start | bytes 1966088 | tf_op jit(solution)/shard_map/ppermute | solution.py:1113
  63.1 2.5 collective-permute-done.30.refs_4_
  68.0 2.2 collective-permute-start.33
  70.2 5.2 %adapters.1 = (bf16[16,17664]{1,0:T(8,128)(2,1)S(1)}, f32[1,21504]{1,0:T(1,128)S(1)}) custom-call(s32[138,1]{1,0:T(8,128)S(1)} %get-tuple-element.210.refs_0_, s32[138,1]{1,0:T(8,128)S(1)} %get-tuple-element.209.refs_1_, s32[21,1]{1,0:T(8,128)S(1)} %copy.60.refs_2_, bf16[320,1024]{1,0:T(8,128)(2,1)} %get-tuple-element.107.refs_3_, ...), custom_call_target="tpu_custom_call" | custom-call | flops 300000000 | bytes 300000 | tf_op jit(solution)/shard_map/adapters/pallas_call | solution.py:490
  77.1 7.9 %attention.1 = (bf16[200,2048]{1,0:T(8,128)(2,1)S(1)}, f32[192,2048]{1,0:T(8,128)S(1)}, f32[384,768]{1,0:T(8,128)S(1)}, bf16[384,768]{1,0:T(8,128)(2,1)S(1)}, f3...) custom-call(s32[12]{0:T(128)S(1)} %stack.57.refs_0_, ...), custom_call_target="tpu_custom_call" | custom-call | flops 10000000000 | bytes 10000000 | tf_op jit(solution)/shard_map/attention/pallas_call | solution.py:490
  89.6 9.1 %collective-permute-start.19 = (bf16[56,2048]{1,0:T(8,128)(2,1)S(1)}, bf16[56,2048]{1,0:T(8,128)(2,1)S(1)}, u32[]{:S(2)}, u32[]{:S(2)}) collective-permute-start(bf16[56,2048]{1,0:T(8,128)(2,1)S(1)} %get-tuple-element.117), channel_id=1, source_target_pairs={{0,4},{1,5},{2,6},{3,7},{4,0},{5,1},{6,2},{7,3},{8,12},{9,13},{10,... | collective-permute-start | bytes 688136 | tf_op jit(solution)/shard_map/ppermute | solution.py:1113
  98.7 5.5 %collective-permute-done.34.refs_1_.refs_4_.refs_13_.refs_6_ = bf16[2,256,768]{2,1,0:T(8,128)(2,1)S(1)} collective-permute-done((bf16[2,256,768]{2,1,0:T(8,128)(2,1)S(1)}, bf16[2,256,768]{2,1,0:T(8,128)(2,1)S(1)}, u32[]{:S(2)}, u32[]{:S(2)}) %collective-permute-start.34) | collective-permute-done | bytes 786464 | tf_op jit(solution)/shard_map/ppermute | solution.py:1116
  104.2 5.3 %collective-permute-done.19.refs_3_.refs_2_ = bf16[56,2048]{1,0:T(8,128)(2,1)S(1)} collective-permute-done((bf16[56,2048]{1,0:T(8,128)(2,1)S(1)}, bf16[56,2048]{1,0:T(8,128)(2,1)S(1)}, u32[]{:S(2)}, u32[]{:S(2)}) %collective-permute-start.19) | collective-permute-done | bytes 229408 | tf_op jit(solution)/shard_map/ppermute | solution.py:1113
  112.5 3.0 collective-permute-start.18
  115.4 2.4 collective-permute-start.20
  120.0 7.0 %collective-permute-done.20.refs_4_ = bf16[56,2048]{1,0:T(8,128)(2,1)} collective-permute-done((bf16[56,2048]{1,0:T(8,128)(2,1)}, bf16[56,2048]{1,0:T(8,128)(2,1)}, u32[]{:S(2)}, u32[]{:S(2)}) %collective-permute-start.20) | collective-permute-done | bytes 229408 | tf_op jit(solution)/shard_map/ppermute | solution.py:1113
  131.4 2.4 collective-permute-start.23
  133.8 2.8 collective-permute-done.21.refs_6_.refs_2_
  136.7 5.6 %collective-permute-start.24 = (bf16[48,2048]{1,0:T(8,128)(2,1)S(1)}, bf16[48,2048]{1,0:T(8,128)(2,1)S(1)}, u32[]{:S(2)}, u32[]{:S(2)}) collective-permute-start(bf16[48,2048]{1,0:T(8,128)(2,1)S(1)} %get-tuple-element.119.refs_1_), channel_id=1, source_target_pairs={{0,1},{1,0},{2,3},{3,2},{4,5},{5,4},{6,7},{7,6},{8,9},{9,8},{10,11... | collective-permute-start | bytes 589832 | tf_op jit(solution)/shard_map/ppermute | solution.py:1113
  146.4 3.5 %down_back.1 = (f32[384,768]{1,0:T(8,128)S(1)}, bf16[384,2048]{1,0:T(8,128)(2,1)S(1)}, f32[384,16]{1,0:T(8,128)S(1)}) custom-call(s32[12]{0:T(128)S(1)} %stack.57.refs_0_, bf16[384,2048]{1,0:T(8,128)(2,1)S(1)} %copy-done.34, f32[1,2048]{1,0:T(1,128)S(1)} %get-tuple-element.123.refs_2_.refs_4_.refs_12_, bf16[704,2048]{1,0:T(8,128)(2,1)S(1)} %copy-done.1, ...), custom_call_target="tpu_custom_call" | custom-call | flops 3500000000 | bytes 3500000 | tf_op jit(solution)/shard_map/down_back/pallas_call | solution.py:490
  150.6 3.3 %wide_norms.1.refs_17_.refs_9_ = f32[8,1536]{1,0:T(8,128)S(1)} custom-call(s32[12]{0:T(128)S(1)} %stack.57.refs_0_, bf16[2,2,256,768]{3,2,1,0:T(8,128)(2,1)} %collective-permute-done.32.refs_1_.refs_11_.refs_4_, bf16[2,2,256,768]{3,2,1,0:T(8,128)(2,1)} %collective-permute-done.35.refs_2_.refs_14_.refs_7_, ...), custom_call_target="tpu_custom_call" | custom-call | flops 3000000000 | bytes 3000000 | tf_op jit(solution)/shard_map/wide_norms/pallas_call | solution.py:490
  154.0 10.1 %feed_forward.1 = (bf16[192,2048]{1,0:T(8,128)(2,1)S(1)}, f32[192,2048]{1,0:T(8,128)S(1)}, bf16[384,2048]{1,0:T(8,128)(2,1)S(1)}, bf16[384,768]{1,0:T(8,128)(2,1...) custom-call(s32[12]{0:T(128)S(1)} %stack.57.refs_0_, ...), custom_call_target="tpu_custom_call" | custom-call | flops 14000000000 | bytes 14000000 | tf_op jit(solution)/shard_map/feed_forward/pallas_call | solution.py:490
  164.5 3.7 %down.1 = (bf16[192,2048]{1,0:T(8,128)(2,1)S(1)}, f32[192,2048]{1,0:T(8,128)S(1)}, f32[384,16]{1,0:T(8,128)S(1)}, f32[1,2048]{1,0:T(1,128)S(1)}) custom-call(s32[12]{0:T(128)S(1)} %stack.57.refs_0_, bf16[384,768]{1,0:T(8,128)(2,1)S(1)} %get-tuple-element.128.refs_1_, bf16[704,2048]{1,0:T(8,128)(2,1)S(1)} %copy-done.1, ...), custom_call_target="tpu_custom_call" | custom-call | flops 3500000000 | bytes 3500000 | tf_op jit(solution)/shard_map/down/pallas_call | solution.py:490
  172.9 5.9 %collective-permute-done.37.refs_14_.refs_1_ = bf16[48,2048]{1,0:T(8,128)(2,1)S(1)} collective-permute-done((bf16[48,2048]{1,0:T(8,128)(2,1)S(1)}, bf16[48,2048]{1,0:T(8,128)(2,1)S(1)}, u32[]{:S(2)}, u32[]{:S(2)}) %collective-permute-start.37) | collective-permute-done | bytes 196640 | tf_op jit(solution)/shard_map/ppermute | solution.py:1113
  178.8 7.9 %column_grads.2 = (f32[64,1024]{1,0:T(8,128)S(1)}, f32[24,1024]{1,0:T(8,128)S(1)}, f32[1,1536]{1,0:T(1,128)S(1)}) custom-call(s32[12]{0:T(128)S(1)} %stack.57.refs_0_, bf16[384,2048]{1,0:T(8,128)(2,1)S(1)} %get-tuple-element.138.refs_1_, bf16[2,256,768]{2,1,0:T(8,128)(2,1)S(1)} %copy-done.3, bf16[2,256,768]{2,1,0:T(8,128)(2,1)S(1)} %copy-done.11, ...), custom_call_target="tpu_custom_call" | custom-call | flops 1000000000 | bytes 1000000 | tf_op jit(solution)/shard_map/column_grads/pallas_call | solution.py:490
  188.9 3.2 collective-permute-start.40
  192.1 2.5 collective-permute-done.42.refs_4_
  194.6 4.6 %collective-permute-start.46 = (bf16[56,2048]{1,0:T(8,128)(2,1)S(1)}, bf16[56,2048]{1,0:T(8,128)(2,1)S(1)}, u32[]{:S(2)}, u32[]{:S(2)}) collective-permute-start(bf16[56,2048]{1,0:T(8,128)(2,1)S(1)} %collective-permute-done.42.refs_4_), channel_id=1, source_target_pairs={{0,1},{1,0},{2,3},{3,2},{4,5},{5,4},{6,7},{7,6},{8,9},{9,8},{10,11... | collective-permute-start | bytes 688136 | tf_op jit(solution)/shard_map/ppermute | solution.py:1113
  199.2 2.0 collective-permute-done.40.refs_2_
  202.2 9.1 %collective-permute-done.41.refs_3_ = bf16[56,2048]{1,0:T(8,128)(2,1)S(1)} collective-permute-done((bf16[56,2048]{1,0:T(8,128)(2,1)S(1)}, bf16[56,2048]{1,0:T(8,128)(2,1)S(1)}, u32[]{:S(2)}, u32[]{:S(2)}) %collective-permute-start.41) | collective-permute-done | bytes 229408 | tf_op jit(solution)/shard_map/ppermute | solution.py:1113
  213.7 7.1 %attention_back.1 = (bf16[192,2048]{1,0:T(8,128)(2,1)S(1)}, f32[192,2048]{1,0:T(8,128)S(1)}, bf16[384,2048]{1,0:T(8,128)(2,1)S(1)}, bf16[384,768]{1,0:T(8,128)(2...) custom-call(s32[12]{0:T(128)S(1)} %stack.57.refs_0_, ...), custom_call_target="tpu_custom_call" | custom-call | flops 100000000 | bytes 100000 | tf_op jit(solution)/shard_map/attention_back/pallas_call | solution.py:490
  221.0 2.2 row_grads.2
  223.3 6.1 %column_grads.3 = (f32[96,1024]{1,0:T(8,128)S(1)}, f32[12,1024]{1,0:T(8,128)S(1)}, f32[1,768]{1,0:T(1,128)S(1)}) custom-call(s32[12]{0:T(128)S(1)} %stack.57.refs_0_, bf16[384,2048]{1,0:T(8,128)(2,1)S(1)} %copy-done.14, bf16[3,256,256]{2,1,0:T(8,128)(2,1)S(1)} %get-tuple-element.103.refs_0_.refs_6_.refs_2_.refs_9_, ...), custom_call_target="tpu_custom_call" | custom-call | flops 1000000000 | bytes 1000000 | tf_op jit(solution)/shard_map/column_grads/pallas_call | solution.py:490
  229.3 3.7 %row_grads.3 = (f32[12,1024]{1,0:T(8,128)S(1)}, f32[32,1024]{1,0:T(8,128)S(1)}) custom-call(s32[12]{0:T(128)S(1)} %stack.57.refs_0_, bf16[384,768]{1,0:T(8,128)(2,1)S(1)} %get-tuple-element.128.refs_1_, bf16[704,2048]{1,0:T(8,128)(2,1)S(1)} %copy-done.1, bf16[16,17664]{1,0:T(8,128)(2,1)S(1)} %get-tuple-element.109.refs_2_.refs_9_.refs_5_.refs_4_.refs_3_.refs_16_.refs_8_, ...), custom_call_target="tpu_custom_call" | custom-call | flops 100000000 | bytes 100000 | tf_op jit(solution)/shard_map/row_grads/pallas_call | solution.py:490
  239.8 6.1 %collective-permute-done.53.refs_8_ = bf16[48,2048]{1,0:T(8,128)(2,1)S(1)} collective-permute-done((bf16[48,2048]{1,0:T(8,128)(2,1)S(1)}, bf16[48,2048]{1,0:T(8,128)(2,1)S(1)}, u32[]{:S(2)}, u32[]{:S(2)}) %collective-permute-start.53) | collective-permute-done | bytes 196640 | tf_op jit(solution)/shard_map/ppermute | solution.py:1113
  247.5 26.8 %collective-permute-done.54.refs_9_ = bf16[48,2048]{1,0:T(8,128)(2,1)S(1)} collective-permute-done((bf16[48,2048]{1,0:T(8,128)(2,1)S(1)}, bf16[48,2048]{1,0:T(8,128)(2,1)S(1)}, u32[]{:S(2)}, u32[]{:S(2)}) %collective-permute-start.54) | collective-permute-done | bytes 196640 | tf_op jit(solution)/shard_map/ppermute | solution.py:1113
  274.9 5.0 %collective-permute-start.57 = (bf16[96,2048]{1,0:T(8,128)(2,1)S(1)}, bf16[96,2048]{1,0:T(8,128)(2,1)S(1)}, u32[]{:S(2)}, u32[]{:S(2)}) collective-permute-start(bf16[96,2048]{1,0:T(8,128)(2,1)S(1)} %last_rows.1.refs_1_), channel_id=1, source_target_pairs={{0,4},{1,5},{2,6},{3,7},{4,0},{5,1},{6,2},{7,3},{8,12},{9,13},{10,... | collective-permute-start | bytes 1179656 | tf_op jit(solution)/shard_map/ppermute | solution.py:1113
  287.1 2.2 collective-permute-start.67
  290.6 8.9 %collective-permute-done.67 = bf16[24,1024]{1,0:T(8,128)(2,1)S(1)} collective-permute-done((bf16[24,1024]{1,0:T(8,128)(2,1)S(1)}, bf16[24,1024]{1,0:T(8,128)(2,1)S(1)}, u32[]{:S(2)}, u32[]{:S(2)}) %collective-permute-start.67) | collective-permute-done | bytes 49184 | tf_op jit(solution)/shard_map/ppermute | solution.py:1113
  304.4 5.0 %collective-permute-start.72 = (bf16[96,1024]{1,0:T(8,128)(2,1)S(1)}, bf16[96,1024]{1,0:T(8,128)(2,1)S(1)}, u32[]{:S(2)}, u32[]{:S(2)}) collective-permute-start(bf16[96,1024]{1,0:T(8,128)(2,1)S(1)} %pad_maximum_fusion.2.refs_2_), channel_id=1, source_target_pairs={{0,1},{1,0},{2,3},{3,2},{4,5},{5,4},{6,7},{7,6},{8,9},{9,8},{10,11... | collective-permute-start | bytes 589832 | tf_op jit(solution)/shard_map/ppermute | solution.py:1113
  309.4 3.1 collective-permute-start.73
  314.2 3.3 %collective-permute-done.58.refs_4_ = bf16[96,2048]{1,0:T(8,128)(2,1)S(1)} collective-permute-done((bf16[96,2048]{1,0:T(8,128)(2,1)S(1)}, bf16[96,2048]{1,0:T(8,128)(2,1)S(1)}, u32[]{:S(2)}, u32[]{:S(2)}) %collective-permute-start.58) | collective-permute-done | bytes 393248 | tf_op jit(solution)/shard_map/ppermute | solution.py:1113
  320.5 3.0 join_rows.1
  (313 shorter events, 92.8 us)
Async XLA Ops:
  6.1 22.8 %collective-permute-start.10 = (bf16[40,1024]{1,0:T(8,128)(2,1)S(1)}, bf16[40,1024]{1,0:T(8,128)(2,1)S(1)}, u32[]{:S(2)}, u32[]{:S(2)}) collective-permute-start(bf16[40,1024]{1,0:T(8,128)(2,1)S(1)} %convert_element_type.20), channel_id=1, source_target_pairs={{0,2},{1,3},{2,0},{3,1},{4,6},{5,7},{6,4},{7,5},{8,10},{9,11},{10,... | collective-permute-start | bytes 245768 | tf_op jit(solution)/shard_map/ppermute | solution.py:1113
  7.6 14.5 %collective-permute-start.2 = (bf16[3,64,512]{2,1,0:T(8,128)(2,1)S(1)}, bf16[3,64,512]{2,1,0:T(8,128)(2,1)S(1)}, u32[]{:S(2)}, u32[]{:S(2)}) collective-permute-start(bf16[3,64,512]{2,1,0:T(8,128)(2,1)S(1)} %get-tuple-element.204), channel_id=1, source_target_pairs={{0,2},{1,3},{2,0},{3,1},{4,6},{5,7},{6,4},{7,5},{8,10},{9,11},{10,... | collective-permute-start | bytes 589832 | tf_op jit(solution)/shard_map/ppermute | solution.py:1113
  9.0 13.2 %collective-permute-start.3 = (bf16[3,64,512]{2,1,0:T(8,128)(2,1)S(1)}, bf16[3,64,512]{2,1,0:T(8,128)(2,1)S(1)}, u32[]{:S(2)}, u32[]{:S(2)}) collective-permute-start(bf16[3,64,512]{2,1,0:T(8,128)(2,1)S(1)} %get-tuple-element.206), channel_id=1, source_target_pairs={{0,4},{1,5},{2,6},{3,7},{4,0},{5,1},{6,2},{7,3},{8,12},{9,13},{10,... | collective-permute-start | bytes 589832 | tf_op jit(solution)/shard_map/ppermute | solution.py:1113
  11.1 13.2 %collective-permute-start.4 = (bf16[3,64,512]{2,1,0:T(8,128)(2,1)S(1)}, bf16[3,64,512]{2,1,0:T(8,128)(2,1)S(1)}, u32[]{:S(2)}, u32[]{:S(2)}) collective-permute-start(bf16[3,64,512]{2,1,0:T(8,128)(2,1)S(1)} %get-tuple-element.203), channel_id=1, source_target_pairs={{0,6},{1,7},{2,4},{3,5},{4,2},{5,3},{6,0},{7,1},{8,14},{9,15},{10,... | collective-permute-start | bytes 589832 | tf_op jit(solution)/shard_map/ppermute | solution.py:1113
  14.6 15.9 %collective-permute-start.13 = (bf16[80,1024]{1,0:T(8,128)(2,1)S(1)}, bf16[80,1024]{1,0:T(8,128)(2,1)S(1)}, u32[]{:S(2)}, u32[]{:S(2)}) collective-permute-start(bf16[80,1024]{1,0:T(8,128)(2,1)S(1)} %constant_dynamic-update-slice_fusion.refs_2_.refs_0_.refs_3_), channel_id=1, source_target_pairs={{0,16},{8,24},{16,0},{24,8},{1,17},{9,25},{17,1},{25,9},{2,18},{10... | collective-permute-start | bytes 491528 | tf_op jit(solution)/shard_map/ppermute | solution.py:1116
  28.9 10.4 %collective-permute-start.11 = (bf16[80,1024]{1,0:T(8,128)(2,1)S(1)}, bf16[80,1024]{1,0:T(8,128)(2,1)S(1)}, u32[]{:S(2)}, u32[]{:S(2)}) collective-permute-start(bf16[80,1024]{1,0:T(8,128)(2,1)S(1)} %pad_maximum_fusion.3.refs_0_), channel_id=1, source_target_pairs={{0,8},{8,0},{16,24},{24,16},{1,9},{9,1},{17,25},{25,17},{2,10},{10... | collective-permute-start | bytes 491528 | tf_op jit(solution)/shard_map/ppermute | solution.py:1116
  30.3 13.1 %collective-permute-start.5 = (bf16[3,256,256]{2,1,0:T(8,128)(2,1)S(1)}, bf16[3,256,256]{2,1,0:T(8,128)(2,1)S(1)}, u32[]{:S(2)}, u32[]{:S(2)}) collective-permute-start(bf16[3,256,256]{2,1,0:T(8,128)(2,1)S(1)} %get-tuple-element.103.refs_0_.refs_6_.refs_2_.refs_9_), channel_id=1, source_target_pairs={{0,8},{8,0},{16,24},{24,16},{1,9},{9,1},{17,25},{25,17},{2,10},{10... | collective-permute-start | bytes 1179656 | tf_op jit(solution)/shard_map/ppermute | solution.py:1116
  31.3 19.0 %collective-permute-start.14 = (bf16[2,80,1024]{2,1,0:T(8,128)(2,1)}, bf16[2,80,1024]{2,1,0:T(8,128)(2,1)}, u32[]{:S(2)}, u32[]{:S(2)}) collective-permute-start(bf16[2,80,1024]{2,1,0:T(8,128)(2,1)} %stack.61), channel_id=1, source_target_pairs={{0,8},{8,0},{16,24},{24,16},{1,9},{9,1},{17,25},{25,17},{2,10},{10... | collective-permute-start | bytes 983048 | tf_op jit(solution)/shard_map/ppermute | solution.py:1116
  32.6 15.3 %collective-permute-start.8 = (bf16[3,256,256]{2,1,0:T(8,128)(2,1)S(1)}, bf16[3,256,256]{2,1,0:T(8,128)(2,1)S(1)}, u32[]{:S(2)}, u32[]{:S(2)}) collective-permute-start(bf16[3,256,256]{2,1,0:T(8,128)(2,1)S(1)} %collective-permute-done.7.refs_0_.refs_5_.refs_12_), channel_id=1, source_target_pairs={{0,16},{8,24},{16,0},{24,8},{1,17},{9,25},{17,1},{25,9},{2,18},{10... | collective-permute-start | bytes 1179656 | tf_op jit(solution)/shard_map/ppermute | solution.py:1116
  36.3 20.4 %collective-permute-start.28 = (bf16[2,64,1408]{2,1,0:T(8,128)(2,1)}, bf16[2,64,1408]{2,1,0:T(8,128)(2,1)}, u32[]{:S(2)}, u32[]{:S(2)}) collective-permute-start(bf16[2,64,1408]{2,1,0:T(8,128)(2,1)} %get-tuple-element.201), channel_id=1, source_target_pairs={{0,2},{1,3},{2,0},{3,1},{4,6},{5,7},{6,4},{7,5},{8,10},{9,11},{10,... | collective-permute-start | bytes 1081352 | tf_op jit(solution)/shard_map/ppermute | solution.py:1113
  39.4 20.8 %collective-permute-start.29 = (bf16[2,64,1408]{2,1,0:T(8,128)(2,1)}, bf16[2,64,1408]{2,1,0:T(8,128)(2,1)}, u32[]{:S(2)}, u32[]{:S(2)}) collective-permute-start(bf16[2,64,1408]{2,1,0:T(8,128)(2,1)} %get-tuple-element.200), channel_id=1, source_target_pairs={{0,4},{1,5},{2,6},{3,7},{4,0},{5,1},{6,2},{7,3},{8,12},{9,13},{10,... | collective-permute-start | bytes 1081352 | tf_op jit(solution)/shard_map/ppermute | solution.py:1113
  47.9 29.2 %collective-permute-start.6 = (bf16[2,3,256,256]{3,2,1,0:T(8,128)(2,1)}, bf16[2,3,256,256]{3,2,1,0:T(8,128)(2,1)}, u32[]{:S(2)}, u32[]{:S(2)}) collective-permute-start(bf16[2,3,256,256]{3,2,1,0:T(8,128)(2,1)} %stack.58), channel_id=1, source_target_pairs={{0,16},{8,24},{16,0},{24,8},{1,17},{9,25},{17,1},{25,9},{2,18},{10... | collective-permute-start | bytes 2359304 | tf_op jit(solution)/shard_map/ppermute | solution.py:1116
  50.4 26.7 %collective-permute-start.9 = (bf16[2,3,256,256]{3,2,1,0:T(8,128)(2,1)}, bf16[2,3,256,256]{3,2,1,0:T(8,128)(2,1)}, u32[]{:S(2)}, u32[]{:S(2)}) collective-permute-start(bf16[2,3,256,256]{3,2,1,0:T(8,128)(2,1)} %stack.59), channel_id=1, source_target_pairs={{0,8},{8,0},{16,24},{24,16},{1,9},{9,1},{17,25},{25,17},{2,10},{10... | collective-permute-start | bytes 2359304 | tf_op jit(solution)/shard_map/ppermute | solution.py:1116
  52.3 13.3 %collective-permute-start.30 = (bf16[2,64,1408]{2,1,0:T(8,128)(2,1)}, bf16[2,64,1408]{2,1,0:T(8,128)(2,1)}, u32[]{:S(2)}, u32[]{:S(2)}) collective-permute-start(bf16[2,64,1408]{2,1,0:T(8,128)(2,1)} %get-tuple-element.199), channel_id=1, source_target_pairs={{0,6},{1,7},{2,4},{3,5},{4,2},{5,3},{6,0},{7,1},{8,14},{9,15},{10,... | collective-permute-start | bytes 1081352 | tf_op jit(solution)/shard_map/ppermute | solution.py:1113
  56.7 13.6 %collective-permute-start.15 = (bf16[320,1024]{1,0:T(8,128)(2,1)}, bf16[320,1024]{1,0:T(8,128)(2,1)}, u32[]{:S(2)}, u32[]{:S(2)}) collective-permute-start(bf16[320,1024]{1,0:T(8,128)(2,1)} %get-tuple-element.107.refs_3_), channel_id=1, source_target_pairs={{0,1},{1,0},{2,3},{3,2},{4,5},{5,4},{6,7},{7,6},{8,9},{9,8},{10,11... | collective-permute-start | bytes 1966088 | tf_op jit(solution)/shard_map/ppermute | solution.py:1113
  60.1 10.1 %collective-permute-start.16 = (bf16[320,1024]{1,0:T(8,128)(2,1)}, bf16[320,1024]{1,0:T(8,128)(2,1)}, u32[]{:S(2)}, u32[]{:S(2)}) collective-permute-start(bf16[320,1024]{1,0:T(8,128)(2,1)} %get-tuple-element.108.refs_4_), channel_id=1, source_target_pairs={{0,1},{1,0},{2,3},{3,2},{4,5},{5,4},{6,7},{7,6},{8,9},{9,8},{10,11... | collective-permute-start | bytes 1966088 | tf_op jit(solution)/shard_map/ppermute | solution.py:1113
  68.0 17.3 %collective-permute-start.33 = (bf16[2,256,768]{2,1,0:T(8,128)(2,1)S(1)}, bf16[2,256,768]{2,1,0:T(8,128)(2,1)S(1)}, u32[]{:S(2)}, u32[]{:S(2)}) collective-permute-start(bf16[2,256,768]{2,1,0:T(8,128)(2,1)S(1)} %get-tuple-element.122), channel_id=1, source_target_pairs={{0,1},{1,0},{2,3},{3,2},{4,5},{5,4},{6,7},{7,6},{8,9},{9,8},{10,11... | collective-permute-start | bytes 2359304 | tf_op jit(solution)/shard_map/ppermute | solution.py:1113
  85.3 18.8 %collective-permute-start.34 = (bf16[2,256,768]{2,1,0:T(8,128)(2,1)S(1)}, bf16[2,256,768]{2,1,0:T(8,128)(2,1)S(1)}, u32[]{:S(2)}, u32[]{:S(2)}) collective-permute-start(bf16[2,256,768]{2,1,0:T(8,128)(2,1)S(1)} %collective-permute-done.33.refs_0_.refs_3_.refs_12_.refs_5_), channel_id=1, source_target_pairs={{0,16},{8,24},{16,0},{24,8},{1,17},{9,25},{17,1},{25,9},{2,18},{10... | collective-permute-start | bytes 2359304 | tf_op jit(solution)/shard_map/ppermute | solution.py:1116
  85.6 25.5 %collective-permute-start.31 = (bf16[2,256,768]{2,1,0:T(8,128)(2,1)S(1)}, bf16[2,256,768]{2,1,0:T(8,128)(2,1)S(1)}, u32[]{:S(2)}, u32[]{:S(2)}) collective-permute-start(bf16[2,256,768]{2,1,0:T(8,128)(2,1)S(1)} %get-tuple-element.121.refs_0_.refs_1_.refs_9_.refs_2_), channel_id=1, source_target_pairs={{0,8},{8,0},{16,24},{24,16},{1,9},{9,1},{17,25},{25,17},{2,10},{10... | collective-permute-start | bytes 2359304 | tf_op jit(solution)/shard_map/ppermute | solution.py:1116
  89.6 19.9 %collective-permute-start.19 = (bf16[56,2048]{1,0:T(8,128)(2,1)S(1)}, bf16[56,2048]{1,0:T(8,128)(2,1)S(1)}, u32[]{:S(2)}, u32[]{:S(2)}) collective-permute-start(bf16[56,2048]{1,0:T(8,128)(2,1)S(1)} %get-tuple-element.117), channel_id=1, source_target_pairs={{0,4},{1,5},{2,6},{3,7},{4,0},{5,1},{6,2},{7,3},{8,12},{9,13},{10,... | collective-permute-start | bytes 688136 | tf_op jit(solution)/shard_map/ppermute | solution.py:1113
  110.7 39.8 %collective-permute-start.35 = (bf16[2,2,256,768]{3,2,1,0:T(8,128)(2,1)}, bf16[2,2,256,768]{3,2,1,0:T(8,128)(2,1)}, u32[]{:S(2)}, u32[]{:S(2)}) collective-permute-start(bf16[2,2,256,768]{3,2,1,0:T(8,128)(2,1)} %stack.63), channel_id=1, source_target_pairs={{0,8},{8,0},{16,24},{24,16},{1,9},{9,1},{17,25},{25,17},{2,10},{10... | collective-permute-start | bytes 4718600 | tf_op jit(solution)/shard_map/ppermute | solution.py:1116
  112.5 38.1 %collective-permute-start.32 = (bf16[2,2,256,768]{3,2,1,0:T(8,128)(2,1)}, bf16[2,2,256,768]{3,2,1,0:T(8,128)(2,1)}, u32[]{:S(2)}, u32[]{:S(2)}) collective-permute-start(bf16[2,2,256,768]{3,2,1,0:T(8,128)(2,1)} %stack.62), channel_id=1, source_target_pairs={{0,16},{8,24},{16,0},{24,8},{1,17},{9,25},{17,1},{25,9},{2,18},{10... | collective-permute-start | bytes 4718600 | tf_op jit(solution)/shard_map/ppermute | solution.py:1116
  115.4 11.6 %collective-permute-start.20 = (bf16[56,2048]{1,0:T(8,128)(2,1)}, bf16[56,2048]{1,0:T(8,128)(2,1)}, u32[]{:S(2)}, u32[]{:S(2)}) collective-permute-start(bf16[56,2048]{1,0:T(8,128)(2,1)} %get-tuple-element.118), channel_id=1, source_target_pairs={{0,6},{1,7},{2,4},{3,5},{4,2},{5,3},{6,0},{7,1},{8,14},{9,15},{10,... | collective-permute-start | bytes 688136 | tf_op jit(solution)/shard_map/ppermute | solution.py:1113
  130.3 19.6 %collective-permute-start.22 = (bf16[48,2048]{1,0:T(8,128)(2,1)S(1)}, bf16[48,2048]{1,0:T(8,128)(2,1)S(1)}, u32[]{:S(2)}, u32[]{:S(2)}) collective-permute-start(bf16[48,2048]{1,0:T(8,128)(2,1)S(1)} %get-tuple-element.119.refs_1_), channel_id=1, source_target_pairs={{0,4},{1,5},{2,6},{3,7},{4,0},{5,1},{6,2},{7,3},{8,12},{9,13},{10,... | collective-permute-start | bytes 589832 | tf_op jit(solution)/shard_map/ppermute | solution.py:1113
  131.4 18.6 %collective-permute-start.23 = (bf16[48,2048]{1,0:T(8,128)(2,1)S(1)}, bf16[48,2048]{1,0:T(8,128)(2,1)S(1)}, u32[]{:S(2)}, u32[]{:S(2)}) collective-permute-start(bf16[48,2048]{1,0:T(8,128)(2,1)S(1)} %get-tuple-element.119.refs_1_), channel_id=1, source_target_pairs={{0,6},{1,7},{2,4},{3,5},{4,2},{5,3},{6,0},{7,1},{8,14},{9,15},{10,... | collective-permute-start | bytes 589832 | tf_op jit(solution)/shard_map/ppermute | solution.py:1113
  136.7 17.2 %collective-permute-start.24 = (bf16[48,2048]{1,0:T(8,128)(2,1)S(1)}, bf16[48,2048]{1,0:T(8,128)(2,1)S(1)}, u32[]{:S(2)}, u32[]{:S(2)}) collective-permute-start(bf16[48,2048]{1,0:T(8,128)(2,1)S(1)} %get-tuple-element.119.refs_1_), channel_id=1, source_target_pairs={{0,1},{1,0},{2,3},{3,2},{4,5},{5,4},{6,7},{7,6},{8,9},{9,8},{10,11... | collective-permute-start | bytes 589832 | tf_op jit(solution)/shard_map/ppermute | solution.py:1113
  168.2 43.6 %collective-permute-start.47 = (bf16[192,2048]{1,0:T(8,128)(2,1)S(1)}, bf16[192,2048]{1,0:T(8,128)(2,1)S(1)}, u32[]{:S(2)}, u32[]{:S(2)}) collective-permute-start(bf16[192,2048]{1,0:T(8,128)(2,1)S(1)} %get-tuple-element.150), channel_id=1, source_target_pairs={{0,1},{1,0},{2,3},{3,2},{4,5},{5,4},{6,7},{7,6},{8,9},{9,8},{10,11... | collective-permute-start | bytes 2359304 | tf_op jit(solution)/shard_map/ppermute | solution.py:1113
  169.1 9.6 %collective-permute-start.37 = (bf16[48,2048]{1,0:T(8,128)(2,1)S(1)}, bf16[48,2048]{1,0:T(8,128)(2,1)S(1)}, u32[]{:S(2)}, u32[]{:S(2)}) collective-permute-start(bf16[48,2048]{1,0:T(8,128)(2,1)S(1)} %get-tuple-element.131), channel_id=1, source_target_pairs={{0,2},{1,3},{2,0},{3,1},{4,6},{5,7},{6,4},{7,5},{8,10},{9,11},{10,... | collective-permute-start | bytes 589832 | tf_op jit(solution)/shard_map/ppermute | solution.py:1113
  170.4 16.3 %collective-permute-start.38 = (bf16[48,2048]{1,0:T(8,128)(2,1)S(1)}, bf16[48,2048]{1,0:T(8,128)(2,1)S(1)}, u32[]{:S(2)}, u32[]{:S(2)}) collective-permute-start(bf16[48,2048]{1,0:T(8,128)(2,1)S(1)} %get-tuple-element.132), channel_id=1, source_target_pairs={{0,4},{1,5},{2,6},{3,7},{4,0},{5,1},{6,2},{7,3},{8,12},{9,13},{10,... | collective-permute-start | bytes 589832 | tf_op jit(solution)/shard_map/ppermute | solution.py:1113
  171.7 15.0 %collective-permute-start.39 = (bf16[48,2048]{1,0:T(8,128)(2,1)S(1)}, bf16[48,2048]{1,0:T(8,128)(2,1)S(1)}, u32[]{:S(2)}, u32[]{:S(2)}) collective-permute-start(bf16[48,2048]{1,0:T(8,128)(2,1)S(1)} %get-tuple-element.133), channel_id=1, source_target_pairs={{0,6},{1,7},{2,4},{3,5},{4,2},{5,3},{6,0},{7,1},{8,14},{9,15},{10,... | collective-permute-start | bytes 589832 | tf_op jit(solution)/shard_map/ppermute | solution.py:1113
  188.9 12.3 %collective-permute-start.40 = (bf16[56,2048]{1,0:T(8,128)(2,1)S(1)}, bf16[56,2048]{1,0:T(8,128)(2,1)S(1)}, u32[]{:S(2)}, u32[]{:S(2)}) collective-permute-start(bf16[56,2048]{1,0:T(8,128)(2,1)S(1)} %get-tuple-element.144.refs_3_.refs_1_), channel_id=1, source_target_pairs={{0,2},{1,3},{2,0},{3,1},{4,6},{5,7},{6,4},{7,5},{8,10},{9,11},{10,... | collective-permute-start | bytes 688136 | tf_op jit(solution)/shard_map/ppermute | solution.py:1113
  192.1 19.1 %collective-permute-start.41 = (bf16[56,2048]{1,0:T(8,128)(2,1)S(1)}, bf16[56,2048]{1,0:T(8,128)(2,1)S(1)}, u32[]{:S(2)}, u32[]{:S(2)}) collective-permute-start(bf16[56,2048]{1,0:T(8,128)(2,1)S(1)} %get-tuple-element.144.refs_3_.refs_1_), channel_id=1, source_target_pairs={{0,4},{1,5},{2,6},{3,7},{4,0},{5,1},{6,2},{7,3},{8,12},{9,13},{10,... | collective-permute-start | bytes 688136 | tf_op jit(solution)/shard_map/ppermute | solution.py:1113
  194.6 17.3 %collective-permute-start.46 = (bf16[56,2048]{1,0:T(8,128)(2,1)S(1)}, bf16[56,2048]{1,0:T(8,128)(2,1)S(1)}, u32[]{:S(2)}, u32[]{:S(2)}) collective-permute-start(bf16[56,2048]{1,0:T(8,128)(2,1)S(1)} %collective-permute-done.42.refs_4_), channel_id=1, source_target_pairs={{0,1},{1,0},{2,3},{3,2},{4,5},{5,4},{6,7},{7,6},{8,9},{9,8},{10,11... | collective-permute-start | bytes 688136 | tf_op jit(solution)/shard_map/ppermute | solution.py:1113
  199.2 13.4 %collective-permute-start.43 = (bf16[56,2048]{1,0:T(8,128)(2,1)S(1)}, bf16[56,2048]{1,0:T(8,128)(2,1)S(1)}, u32[]{:S(2)}, u32[]{:S(2)}) collective-permute-start(bf16[56,2048]{1,0:T(8,128)(2,1)S(1)} %get-tuple-element.144.refs_3_.refs_1_), channel_id=1, source_target_pairs={{0,1},{1,0},{2,3},{3,2},{4,5},{5,4},{6,7},{7,6},{8,9},{9,8},{10,11... | collective-permute-start | bytes 688136 | tf_op jit(solution)/shard_map/ppermute | solution.py:1113
  201.2 11.4 %collective-permute-start.44 = (bf16[56,2048]{1,0:T(8,128)(2,1)S(1)}, bf16[56,2048]{1,0:T(8,128)(2,1)S(1)}, u32[]{:S(2)}, u32[]{:S(2)}) collective-permute-start(bf16[56,2048]{1,0:T(8,128)(2,1)S(1)} %collective-permute-done.40.refs_2_), channel_id=1, source_target_pairs={{0,1},{1,0},{2,3},{3,2},{4,5},{5,4},{6,7},{7,6},{8,9},{9,8},{10,11... | collective-permute-start | bytes 688136 | tf_op jit(solution)/shard_map/ppermute | solution.py:1113
  220.9 14.5 %collective-permute-start.48 = (bf16[192,2048]{1,0:T(8,128)(2,1)S(1)}, bf16[192,2048]{1,0:T(8,128)(2,1)S(1)}, u32[]{:S(2)}, u32[]{:S(2)}) collective-permute-start(bf16[192,2048]{1,0:T(8,128)(2,1)S(1)} %get-tuple-element.153), channel_id=1, source_target_pairs={{0,1},{1,0},{2,3},{3,2},{4,5},{5,4},{6,7},{7,6},{8,9},{9,8},{10,11... | collective-permute-start | bytes 2359304 | tf_op jit(solution)/shard_map/ppermute | solution.py:1113
  234.2 11.6 %collective-permute-start.53 = (bf16[48,2048]{1,0:T(8,128)(2,1)S(1)}, bf16[48,2048]{1,0:T(8,128)(2,1)S(1)}, u32[]{:S(2)}, u32[]{:S(2)}) collective-permute-start(bf16[48,2048]{1,0:T(8,128)(2,1)S(1)} %get-tuple-element.181), channel_id=1, source_target_pairs={{0,2},{1,3},{2,0},{3,1},{4,6},{5,7},{6,4},{7,5},{8,10},{9,11},{10,... | collective-permute-start | bytes 589832 | tf_op jit(solution)/shard_map/ppermute | solution.py:1113
  236.1 38.1 %collective-permute-start.50 = (bf16[64,2048]{1,0:T(8,128)(2,1)S(1)}, bf16[64,2048]{1,0:T(8,128)(2,1)S(1)}, u32[]{:S(2)}, u32[]{:S(2)}) collective-permute-start(bf16[64,2048]{1,0:T(8,128)(2,1)S(1)} %get-tuple-element.177), channel_id=1, source_target_pairs={{0,2},{1,3},{2,0},{3,1},{4,6},{5,7},{6,4},{7,5},{8,10},{9,11},{10,... | collective-permute-start | bytes 786440 | tf_op jit(solution)/shard_map/ppermute | solution.py:1113
  236.5 37.7 %collective-permute-start.51 = (bf16[64,2048]{1,0:T(8,128)(2,1)S(1)}, bf16[64,2048]{1,0:T(8,128)(2,1)S(1)}, u32[]{:S(2)}, u32[]{:S(2)}) collective-permute-start(bf16[64,2048]{1,0:T(8,128)(2,1)S(1)} %get-tuple-element.178), channel_id=1, source_target_pairs={{0,4},{1,5},{2,6},{3,7},{4,0},{5,1},{6,2},{7,3},{8,12},{9,13},{10,... | collective-permute-start | bytes 786440 | tf_op jit(solution)/shard_map/ppermute | solution.py:1113
  238.1 36.1 %collective-permute-start.52 = (bf16[64,2048]{1,0:T(8,128)(2,1)S(1)}, bf16[64,2048]{1,0:T(8,128)(2,1)S(1)}, u32[]{:S(2)}, u32[]{:S(2)}) collective-permute-start(bf16[64,2048]{1,0:T(8,128)(2,1)S(1)} %get-tuple-element.179), channel_id=1, source_target_pairs={{0,6},{1,7},{2,4},{3,5},{4,2},{5,3},{6,0},{7,1},{8,14},{9,15},{10,... | collective-permute-start | bytes 786440 | tf_op jit(solution)/shard_map/ppermute | solution.py:1113
  239.8 34.5 %collective-permute-start.54 = (bf16[48,2048]{1,0:T(8,128)(2,1)S(1)}, bf16[48,2048]{1,0:T(8,128)(2,1)S(1)}, u32[]{:S(2)}, u32[]{:S(2)}) collective-permute-start(bf16[48,2048]{1,0:T(8,128)(2,1)S(1)} %get-tuple-element.182), channel_id=1, source_target_pairs={{0,4},{1,5},{2,6},{3,7},{4,0},{5,1},{6,2},{7,3},{8,12},{9,13},{10,... | collective-permute-start | bytes 589832 | tf_op jit(solution)/shard_map/ppermute | solution.py:1113
  245.8 28.4 %collective-permute-start.55 = (bf16[48,2048]{1,0:T(8,128)(2,1)S(1)}, bf16[48,2048]{1,0:T(8,128)(2,1)S(1)}, u32[]{:S(2)}, u32[]{:S(2)}) collective-permute-start(bf16[48,2048]{1,0:T(8,128)(2,1)S(1)} %get-tuple-element.183), channel_id=1, source_target_pairs={{0,6},{1,7},{2,4},{3,5},{4,2},{5,3},{6,0},{7,1},{8,14},{9,15},{10,... | collective-permute-start | bytes 589832 | tf_op jit(solution)/shard_map/ppermute | solution.py:1113
  274.9 27.4 %collective-permute-start.57 = (bf16[96,2048]{1,0:T(8,128)(2,1)S(1)}, bf16[96,2048]{1,0:T(8,128)(2,1)S(1)}, u32[]{:S(2)}, u32[]{:S(2)}) collective-permute-start(bf16[96,2048]{1,0:T(8,128)(2,1)S(1)} %last_rows.1.refs_1_), channel_id=1, source_target_pairs={{0,4},{1,5},{2,6},{3,7},{4,0},{5,1},{6,2},{7,3},{8,12},{9,13},{10,... | collective-permute-start | bytes 1179656 | tf_op jit(solution)/shard_map/ppermute | solution.py:1113
  287.1 12.4 %collective-permute-start.67 = (bf16[24,1024]{1,0:T(8,128)(2,1)S(1)}, bf16[24,1024]{1,0:T(8,128)(2,1)S(1)}, u32[]{:S(2)}, u32[]{:S(2)}) collective-permute-start(bf16[24,1024]{1,0:T(8,128)(2,1)S(1)} %last_sums.1), channel_id=1, source_target_pairs={{0,4},{1,5},{2,6},{3,7},{4,0},{5,1},{6,2},{7,3},{8,12},{9,13},{10,... | collective-permute-start | bytes 147464 | tf_op jit(solution)/shard_map/ppermute | solution.py:1113
  289.2 10.3 %collective-permute-start.68 = (bf16[24,1024]{1,0:T(8,128)(2,1)S(1)}, bf16[24,1024]{1,0:T(8,128)(2,1)S(1)}, u32[]{:S(2)}, u32[]{:S(2)}) collective-permute-start(bf16[24,1024]{1,0:T(8,128)(2,1)S(1)} %last_sums.1), channel_id=1, source_target_pairs={{0,6},{1,7},{2,4},{3,5},{4,2},{5,3},{6,0},{7,1},{8,14},{9,15},{10,... | collective-permute-start | bytes 147464 | tf_op jit(solution)/shard_map/ppermute | solution.py:1113
  290.6 22.5 %collective-permute-start.56 = (bf16[96,2048]{1,0:T(8,128)(2,1)S(1)}, bf16[96,2048]{1,0:T(8,128)(2,1)S(1)}, u32[]{:S(2)}, u32[]{:S(2)}) collective-permute-start(bf16[96,2048]{1,0:T(8,128)(2,1)S(1)} %last_rows.1.refs_1_), channel_id=1, source_target_pairs={{0,2},{1,3},{2,0},{3,1},{4,6},{5,7},{6,4},{7,5},{8,10},{9,11},{10,... | collective-permute-start | bytes 1179656 | tf_op jit(solution)/shard_map/ppermute | solution.py:1113
  301.6 10.9 %collective-permute-start.71 = (bf16[96,1024]{1,0:T(8,128)(2,1)S(1)}, bf16[96,1024]{1,0:T(8,128)(2,1)S(1)}, u32[]{:S(2)}, u32[]{:S(2)}) collective-permute-start(bf16[96,1024]{1,0:T(8,128)(2,1)S(1)} %pad_maximum_fusion.2.refs_2_), channel_id=1, source_target_pairs={{0,24},{8,16},{16,8},{24,0},{1,25},{9,17},{17,9},{25,1},{2,26},{10... | collective-permute-start | bytes 589832 | tf_op jit(solution)/shard_map/ppermute | solution.py:1116
  302.2 15.2 %collective-permute-start.58 = (bf16[96,2048]{1,0:T(8,128)(2,1)S(1)}, bf16[96,2048]{1,0:T(8,128)(2,1)S(1)}, u32[]{:S(2)}, u32[]{:S(2)}) collective-permute-start(bf16[96,2048]{1,0:T(8,128)(2,1)S(1)} %collective-permute-done.57.refs_3_), channel_id=1, source_target_pairs={{0,2},{1,3},{2,0},{3,1},{4,6},{5,7},{6,4},{7,5},{8,10},{9,11},{10,... | collective-permute-start | bytes 1179656 | tf_op jit(solution)/shard_map/ppermute | solution.py:1113
  (89 other events, 760.0 us)

commit v3 on v2

--- a/solution.py
+++ b/solution.py
@@ -1426,7 +1426,7 @@
         3, att, w_out, flat, scale_o, norm_o, mag_o, grad_o, through_o, low_o, dots_all_o, []
     )
     a_a, b_a, m_a = column_grads(
-        (0, 1, 2), width, features, blocks_a, flat, stats_a, grads_a, through_a, low_a, dots_a, [a_o]
+        (0, 1, 2), width, features, blocks_a, flat, stats_a, grads_a, through_a, low_a, dots_a, sums_d[2:3]
     )
     a_d, b_d = row_grads(
         6, act, w_down, flat, scale_d, norm_d, mag_d, grad_d, through_d, low_d, dots_all_d, [m_a]

time: 328 us -> 321 us (0.979)
  waiting for transfers between devices: 101 us -> 91.9 us
    ppermute x58, waiting for transfers between devices: 88.8 us -> 79.3 us  [mp_swap(): return lax.ppermute(values, 'mp', [(i, i ^ step) for i in range(N_MP)])]
  transfers between devices with their start and end apart: 76 -> 76, of which waited for: 25 -> 27; matrix products, arithmetic and copies ran while one was open for 5% -> 5% of each run, Pallas kernels for 21% -> 23%
where the time goes in v3:
time: 321 us; the launch traced here: 316 us
  starting transfers between devices  110 us (34%)
  waiting for transfers between devices  91.9 us (29%)
  Pallas kernels  88.1 us (27%)
  local copies, waits for them, and re-layouts  18.7 us (6%)
  other arithmetic  6.01 us (2%)
    ppermute x58, starting transfers between devices, mp_swap(): return lax.ppermute(values, 'mp', [(i, i ^ step) for i in range(N_MP)])  95.4 us
    pallas_call x35, Pallas kernels, run(): pl.pallas_call(body, out_shape=list(outs), in_specs=[kinds[kind] for kind...  88.1 us
    ppermute x58, waiting for transfers between devices, mp_swap(): return lax.ppermute(values, 'mp', [(i, i ^ step) for i in range(N_MP)])  79.3 us
    ppermute x18, starting transfers between devices, dp_swap(): return lax.ppermute(values, 'dp', [(i, i ^ step) for i in range(N_DP)])  14.2 us
    ppermute x18, waiting for transfers between devices, dp_swap(): return lax.ppermute(values, 'dp', [(i, i ^ step) for i in range(N_DP)])  12.6 us
    unnamed x123, local copies, waits for them, and re-layouts  8.03 us
  transfers between devices with their start and end apart: 76, of which 27 were waited for; matrix products, arithmetic and copies ran while one was open for 5% of the time, Pallas kernels for 23%

profile of v3, /device:TPU:1, one launch (start us, length us, event | category | flops | bytes accessed | tf_op | source)
XLA Modules:
  0.0 316.3 jit_solution(17773498957468002966)
XLA Ops:
  1.8 3.2 %collective-permute-start = (bf16[40,1024]{1,0:T(8,128)(2,1)S(1)}, bf16[40,1024]{1,0:T(8,128)(2,1)S(1)}, u32[]{:S(2)}, u32[]{:S(2)}) collective-permute-start(bf16[40,1024]{1,0:T(8,128)(2,1)S(1)} %convert_element_type.20), channel_id=1, source_target_pairs={{0,4},{1,5},{2,6},{3,7},{4,0},{5,1},{6,2},{7,3},{8,12},{9,13},{10,... | collective-permute-start | bytes 245768 | tf_op jit(solution)/shard_map/ppermute | solution.py:1113
  11.1 3.5 %collective-permute-start.4 = (bf16[3,64,512]{2,1,0:T(8,128)(2,1)S(1)}, bf16[3,64,512]{2,1,0:T(8,128)(2,1)S(1)}, u32[]{:S(2)}, u32[]{:S(2)}) collective-permute-start(bf16[3,64,512]{2,1,0:T(8,128)(2,1)S(1)} %get-tuple-element.203), channel_id=1, source_target_pairs={{0,6},{1,7},{2,4},{3,5},{4,2},{5,3},{6,0},{7,1},{8,14},{9,15},{10,... | collective-permute-start | bytes 589832 | tf_op jit(solution)/shard_map/ppermute | solution.py:1113
  22.2 2.1 collective-permute-done.4.refs_4_
  24.9 3.7 %collective-permute-start.7 = (bf16[3,256,256]{2,1,0:T(8,128)(2,1)S(1)}, bf16[3,256,256]{2,1,0:T(8,128)(2,1)S(1)}, u32[]{:S(2)}, u32[]{:S(2)}) collective-permute-start(bf16[3,256,256]{2,1,0:T(8,128)(2,1)S(1)} %get-tuple-element.104), channel_id=1, source_target_pairs={{0,1},{1,0},{2,3},{3,2},{4,5},{5,4},{6,7},{7,6},{8,9},{9,8},{10,11... | collective-permute-start | bytes 1179656 | tf_op jit(solution)/shard_map/ppermute | solution.py:1113
  33.8 2.4 constant_dynamic-slice_fusion.1
  36.3 3.1 collective-permute-start.28
  39.4 2.0 collective-permute-start.29
  44.6 2.1 gather_fusion
  52.3 2.2 collective-permute-start.30
  54.5 2.2 adapter_rows.1
  56.7 3.5 %collective-permute-start.15 = (bf16[320,1024]{1,0:T(8,128)(2,1)}, bf16[320,1024]{1,0:T(8,128)(2,1)}, u32[]{:S(2)}, u32[]{:S(2)}) collective-permute-start(bf16[320,1024]{1,0:T(8,128)(2,1)} %get-tuple-element.107.refs_3_), channel_id=1, source_target_pairs={{0,1},{1,0},{2,3},{3,2},{4,5},{5,4},{6,7},{7,6},{8,9},{9,8},{10,11... | collective-permute-start | bytes 1966088 | tf_op jit(solution)/shard_map/ppermute | solution.py:1113
  63.1 2.5 collective-permute-done.30.refs_4_
  68.0 2.2 collective-permute-start.33
  70.2 5.2 %adapters.1 = (bf16[16,17664]{1,0:T(8,128)(2,1)S(1)}, f32[1,21504]{1,0:T(1,128)S(1)}) custom-call(s32[138,1]{1,0:T(8,128)S(1)} %get-tuple-element.210.refs_0_, s32[138,1]{1,0:T(8,128)S(1)} %get-tuple-element.209.refs_1_, s32[21,1]{1,0:T(8,128)S(1)} %copy.60.refs_2_, bf16[320,1024]{1,0:T(8,128)(2,1)} %get-tuple-element.107.refs_3_, ...), custom_call_target="tpu_custom_call" | custom-call | flops 300000000 | bytes 300000 | tf_op jit(solution)/shard_map/adapters/pallas_call | solution.py:490
  77.1 7.9 %attention.1 = (bf16[200,2048]{1,0:T(8,128)(2,1)S(1)}, f32[192,2048]{1,0:T(8,128)S(1)}, f32[384,768]{1,0:T(8,128)S(1)}, bf16[384,768]{1,0:T(8,128)(2,1)S(1)}, f3...) custom-call(s32[12]{0:T(128)S(1)} %stack.57.refs_0_, ...), custom_call_target="tpu_custom_call" | custom-call | flops 10000000000 | bytes 10000000 | tf_op jit(solution)/shard_map/attention/pallas_call | solution.py:490
  89.6 9.1 %collective-permute-start.19 = (bf16[56,2048]{1,0:T(8,128)(2,1)S(1)}, bf16[56,2048]{1,0:T(8,128)(2,1)S(1)}, u32[]{:S(2)}, u32[]{:S(2)}) collective-permute-start(bf16[56,2048]{1,0:T(8,128)(2,1)S(1)} %get-tuple-element.117), channel_id=1, source_target_pairs={{0,4},{1,5},{2,6},{3,7},{4,0},{5,1},{6,2},{7,3},{8,12},{9,13},{10,... | collective-permute-start | bytes 688136 | tf_op jit(solution)/shard_map/ppermute | solution.py:1113
  98.7 5.5 %collective-permute-done.34.refs_1_.refs_4_.refs_13_.refs_6_ = bf16[2,256,768]{2,1,0:T(8,128)(2,1)S(1)} collective-permute-done((bf16[2,256,768]{2,1,0:T(8,128)(2,1)S(1)}, bf16[2,256,768]{2,1,0:T(8,128)(2,1)S(1)}, u32[]{:S(2)}, u32[]{:S(2)}) %collective-permute-start.34) | collective-permute-done | bytes 786464 | tf_op jit(solution)/shard_map/ppermute | solution.py:1116
  104.2 5.3 %collective-permute-done.19.refs_3_.refs_2_ = bf16[56,2048]{1,0:T(8,128)(2,1)S(1)} collective-permute-done((bf16[56,2048]{1,0:T(8,128)(2,1)S(1)}, bf16[56,2048]{1,0:T(8,128)(2,1)S(1)}, u32[]{:S(2)}, u32[]{:S(2)}) %collective-permute-start.19) | collective-permute-done | bytes 229408 | tf_op jit(solution)/shard_map/ppermute | solution.py:1113
  112.5 3.0 collective-permute-start.18
  115.4 2.4 collective-permute-start.20
  120.0 7.0 %collective-permute-done.20.refs_4_ = bf16[56,2048]{1,0:T(8,128)(2,1)} collective-permute-done((bf16[56,2048]{1,0:T(8,128)(2,1)}, bf16[56,2048]{1,0:T(8,128)(2,1)}, u32[]{:S(2)}, u32[]{:S(2)}) %collective-permute-start.20) | collective-permute-done | bytes 229408 | tf_op jit(solution)/shard_map/ppermute | solution.py:1113
  131.4 2.4 collective-permute-start.23
  133.8 2.8 collective-permute-done.21.refs_6_.refs_2_
  136.7 5.6 %collective-permute-start.24 = (bf16[48,2048]{1,0:T(8,128)(2,1)S(1)}, bf16[48,2048]{1,0:T(8,128)(2,1)S(1)}, u32[]{:S(2)}, u32[]{:S(2)}) collective-permute-start(bf16[48,2048]{1,0:T(8,128)(2,1)S(1)} %get-tuple-element.119.refs_1_), channel_id=1, source_target_pairs={{0,1},{1,0},{2,3},{3,2},{4,5},{5,4},{6,7},{7,6},{8,9},{9,8},{10,11... | collective-permute-start | bytes 589832 | tf_op jit(solution)/shard_map/ppermute | solution.py:1113
  146.4 3.5 %down_back.1 = (f32[384,768]{1,0:T(8,128)S(1)}, bf16[384,2048]{1,0:T(8,128)(2,1)S(1)}, f32[384,16]{1,0:T(8,128)S(1)}) custom-call(s32[12]{0:T(128)S(1)} %stack.57.refs_0_, bf16[384,2048]{1,0:T(8,128)(2,1)S(1)} %copy-done.34, f32[1,2048]{1,0:T(1,128)S(1)} %get-tuple-element.123.refs_2_.refs_4_.refs_12_, bf16[704,2048]{1,0:T(8,128)(2,1)S(1)} %copy-done.1, ...), custom_call_target="tpu_custom_call" | custom-call | flops 3500000000 | bytes 3500000 | tf_op jit(solution)/shard_map/down_back/pallas_call | solution.py:490
  150.6 3.3 %wide_norms.1.refs_17_.refs_9_ = f32[8,1536]{1,0:T(8,128)S(1)} custom-call(s32[12]{0:T(128)S(1)} %stack.57.refs_0_, bf16[2,2,256,768]{3,2,1,0:T(8,128)(2,1)} %collective-permute-done.32.refs_1_.refs_11_.refs_4_, bf16[2,2,256,768]{3,2,1,0:T(8,128)(2,1)} %collective-permute-done.35.refs_2_.refs_14_.refs_7_, ...), custom_call_target="tpu_custom_call" | custom-call | flops 3000000000 | bytes 3000000 | tf_op jit(solution)/shard_map/wide_norms/pallas_call | solution.py:490
  154.0 10.1 %feed_forward.1 = (bf16[192,2048]{1,0:T(8,128)(2,1)S(1)}, f32[192,2048]{1,0:T(8,128)S(1)}, bf16[384,2048]{1,0:T(8,128)(2,1)S(1)}, bf16[384,768]{1,0:T(8,128)(2,1...) custom-call(s32[12]{0:T(128)S(1)} %stack.57.refs_0_, ...), custom_call_target="tpu_custom_call" | custom-call | flops 14000000000 | bytes 14000000 | tf_op jit(solution)/shard_map/feed_forward/pallas_call | solution.py:490
  164.5 3.7 %down.1 = (bf16[192,2048]{1,0:T(8,128)(2,1)S(1)}, f32[192,2048]{1,0:T(8,128)S(1)}, f32[384,16]{1,0:T(8,128)S(1)}, f32[1,2048]{1,0:T(1,128)S(1)}) custom-call(s32[12]{0:T(128)S(1)} %stack.57.refs_0_, bf16[384,768]{1,0:T(8,128)(2,1)S(1)} %get-tuple-element.128.refs_1_, bf16[704,2048]{1,0:T(8,128)(2,1)S(1)} %copy-done.1, ...), custom_call_target="tpu_custom_call" | custom-call | flops 3500000000 | bytes 3500000 | tf_op jit(solution)/shard_map/down/pallas_call | solution.py:490
  172.9 5.9 %collective-permute-done.37.refs_14_.refs_1_ = bf16[48,2048]{1,0:T(8,128)(2,1)S(1)} collective-permute-done((bf16[48,2048]{1,0:T(8,128)(2,1)S(1)}, bf16[48,2048]{1,0:T(8,128)(2,1)S(1)}, u32[]{:S(2)}, u32[]{:S(2)}) %collective-permute-start.37) | collective-permute-done | bytes 196640 | tf_op jit(solution)/shard_map/ppermute | solution.py:1113
  178.8 7.9 %column_grads.2 = (f32[64,1024]{1,0:T(8,128)S(1)}, f32[24,1024]{1,0:T(8,128)S(1)}, f32[1,1536]{1,0:T(1,128)S(1)}) custom-call(s32[12]{0:T(128)S(1)} %stack.57.refs_0_, bf16[384,2048]{1,0:T(8,128)(2,1)S(1)} %get-tuple-element.138.refs_1_, bf16[2,256,768]{2,1,0:T(8,128)(2,1)S(1)} %copy-done.3, bf16[2,256,768]{2,1,0:T(8,128)(2,1)S(1)} %copy-done.11, ...), custom_call_target="tpu_custom_call" | custom-call | flops 1000000000 | bytes 1000000 | tf_op jit(solution)/shard_map/column_grads/pallas_call | solution.py:490
  188.9 3.2 collective-permute-start.40
  192.1 2.5 collective-permute-done.42.refs_4_
  194.6 4.6 %collective-permute-start.46 = (bf16[56,2048]{1,0:T(8,128)(2,1)S(1)}, bf16[56,2048]{1,0:T(8,128)(2,1)S(1)}, u32[]{:S(2)}, u32[]{:S(2)}) collective-permute-start(bf16[56,2048]{1,0:T(8,128)(2,1)S(1)} %collective-permute-done.42.refs_4_), channel_id=1, source_target_pairs={{0,1},{1,0},{2,3},{3,2},{4,5},{5,4},{6,7},{7,6},{8,9},{9,8},{10,11... | collective-permute-start | bytes 688136 | tf_op jit(solution)/shard_map/ppermute | solution.py:1113
  199.2 2.0 collective-permute-done.40.refs_2_
  202.2 9.1 %collective-permute-done.41.refs_3_ = bf16[56,2048]{1,0:T(8,128)(2,1)S(1)} collective-permute-done((bf16[56,2048]{1,0:T(8,128)(2,1)S(1)}, bf16[56,2048]{1,0:T(8,128)(2,1)S(1)}, u32[]{:S(2)}, u32[]{:S(2)}) %collective-permute-start.41) | collective-permute-done | bytes 229408 | tf_op jit(solution)/shard_map/ppermute | solution.py:1113
  213.7 7.2 %attention_back.1 = (bf16[192,2048]{1,0:T(8,128)(2,1)S(1)}, f32[192,2048]{1,0:T(8,128)S(1)}, bf16[384,2048]{1,0:T(8,128)(2,1)S(1)}, bf16[384,768]{1,0:T(8,128)(2...) custom-call(s32[12]{0:T(128)S(1)} %stack.57.refs_0_, ...), custom_call_target="tpu_custom_call" | custom-call | flops 100000000 | bytes 100000 | tf_op jit(solution)/shard_map/attention_back/pallas_call | solution.py:490
  221.0 2.2 row_grads.3
  223.9 6.1 %column_grads.3 = (f32[96,1024]{1,0:T(8,128)S(1)}, f32[12,1024]{1,0:T(8,128)S(1)}, f32[1,768]{1,0:T(1,128)S(1)}) custom-call(s32[12]{0:T(128)S(1)} %stack.57.refs_0_, bf16[384,2048]{1,0:T(8,128)(2,1)S(1)} %copy-done.14, bf16[3,256,256]{2,1,0:T(8,128)(2,1)S(1)} %get-tuple-element.103.refs_0_.refs_6_.refs_2_.refs_9_, ...), custom_call_target="tpu_custom_call" | custom-call | flops 1000000000 | bytes 1000000 | tf_op jit(solution)/shard_map/column_grads/pallas_call | solution.py:490
  230.0 3.7 %row_grads.2 = (f32[12,1024]{1,0:T(8,128)S(1)}, f32[32,1024]{1,0:T(8,128)S(1)}) custom-call(s32[12]{0:T(128)S(1)} %stack.57.refs_0_, bf16[384,768]{1,0:T(8,128)(2,1)S(1)} %get-tuple-element.128.refs_1_, bf16[704,2048]{1,0:T(8,128)(2,1)S(1)} %copy-done.1, bf16[16,17664]{1,0:T(8,128)(2,1)S(1)} %get-tuple-element.109.refs_2_.refs_9_.refs_5_.refs_4_.refs_3_.refs_16_.refs_8_, ...), custom_call_target="tpu_custom_call" | custom-call | flops 100000000 | bytes 100000 | tf_op jit(solution)/shard_map/row_grads/pallas_call | solution.py:490
  242.0 17.8 %collective-permute-done.54.refs_8_ = bf16[48,2048]{1,0:T(8,128)(2,1)S(1)} collective-permute-done((bf16[48,2048]{1,0:T(8,128)(2,1)S(1)}, bf16[48,2048]{1,0:T(8,128)(2,1)S(1)}, u32[]{:S(2)}, u32[]{:S(2)}) %collective-permute-start.54) | collective-permute-done | bytes 196640 | tf_op jit(solution)/shard_map/ppermute | solution.py:1113
  259.8 5.2 %collective-permute-done.55.refs_10_ = bf16[48,2048]{1,0:T(8,128)(2,1)S(1)} collective-permute-done((bf16[48,2048]{1,0:T(8,128)(2,1)S(1)}, bf16[48,2048]{1,0:T(8,128)(2,1)S(1)}, u32[]{:S(2)}, u32[]{:S(2)}) %collective-permute-start.55) | collective-permute-done | bytes 196640 | tf_op jit(solution)/shard_map/ppermute | solution.py:1113
  265.7 6.8 %collective-permute-start.57 = (bf16[96,2048]{1,0:T(8,128)(2,1)S(1)}, bf16[96,2048]{1,0:T(8,128)(2,1)S(1)}, u32[]{:S(2)}, u32[]{:S(2)}) collective-permute-start(bf16[96,2048]{1,0:T(8,128)(2,1)S(1)} %last_rows.1.refs_1_), channel_id=1, source_target_pairs={{0,4},{1,5},{2,6},{3,7},{4,0},{5,1},{6,2},{7,3},{8,12},{9,13},{10,... | collective-permute-start | bytes 1179656 | tf_op jit(solution)/shard_map/ppermute | solution.py:1113
  277.6 2.1 collective-permute-done.65.refs_3_
  283.5 8.7 %collective-permute-done.67 = bf16[24,1024]{1,0:T(8,128)(2,1)S(1)} collective-permute-done((bf16[24,1024]{1,0:T(8,128)(2,1)S(1)}, bf16[24,1024]{1,0:T(8,128)(2,1)S(1)}, u32[]{:S(2)}, u32[]{:S(2)}) %collective-permute-start.67) | collective-permute-done | bytes 49184 | tf_op jit(solution)/shard_map/ppermute | solution.py:1113
  297.1 4.9 %collective-permute-start.72 = (bf16[96,1024]{1,0:T(8,128)(2,1)S(1)}, bf16[96,1024]{1,0:T(8,128)(2,1)S(1)}, u32[]{:S(2)}, u32[]{:S(2)}) collective-permute-start(bf16[96,1024]{1,0:T(8,128)(2,1)S(1)} %pad_maximum_fusion.2.refs_2_), channel_id=1, source_target_pairs={{0,1},{1,0},{2,3},{3,2},{4,5},{5,4},{6,7},{7,6},{8,9},{9,8},{10,11... | collective-permute-start | bytes 589832 | tf_op jit(solution)/shard_map/ppermute | solution.py:1113
  302.0 3.3 %collective-permute-start.73 = (bf16[96,1024]{1,0:T(8,128)(2,1)S(1)}, bf16[96,1024]{1,0:T(8,128)(2,1)S(1)}, u32[]{:S(2)}, u32[]{:S(2)}) collective-permute-start(bf16[96,1024]{1,0:T(8,128)(2,1)S(1)} %collective-permute-done.69.refs_3_), channel_id=1, source_target_pairs={{0,1},{1,0},{2,3},{3,2},{4,5},{5,4},{6,7},{7,6},{8,9},{9,8},{10,11... | collective-permute-start | bytes 589832 | tf_op jit(solution)/shard_map/ppermute | solution.py:1113
  307.0 3.1 collective-permute-done.58.refs_4_
  313.1 3.0 join_rows.1
  (313 shorter events, 93.7 us)
Async XLA Ops:
  6.1 22.8 %collective-permute-start.10 = (bf16[40,1024]{1,0:T(8,128)(2,1)S(1)}, bf16[40,1024]{1,0:T(8,128)(2,1)S(1)}, u32[]{:S(2)}, u32[]{:S(2)}) collective-permute-start(bf16[40,1024]{1,0:T(8,128)(2,1)S(1)} %convert_element_type.20), channel_id=1, source_target_pairs={{0,2},{1,3},{2,0},{3,1},{4,6},{5,7},{6,4},{7,5},{8,10},{9,11},{10,... | collective-permute-start | bytes 245768 | tf_op jit(solution)/shard_map/ppermute | solution.py:1113
  7.6 14.5 %collective-permute-start.2 = (bf16[3,64,512]{2,1,0:T(8,128)(2,1)S(1)}, bf16[3,64,512]{2,1,0:T(8,128)(2,1)S(1)}, u32[]{:S(2)}, u32[]{:S(2)}) collective-permute-start(bf16[3,64,512]{2,1,0:T(8,128)(2,1)S(1)} %get-tuple-element.204), channel_id=1, source_target_pairs={{0,2},{1,3},{2,0},{3,1},{4,6},{5,7},{6,4},{7,5},{8,10},{9,11},{10,... | collective-permute-start | bytes 589832 | tf_op jit(solution)/shard_map/ppermute | solution.py:1113
  9.0 13.2 %collective-permute-start.3 = (bf16[3,64,512]{2,1,0:T(8,128)(2,1)S(1)}, bf16[3,64,512]{2,1,0:T(8,128)(2,1)S(1)}, u32[]{:S(2)}, u32[]{:S(2)}) collective-permute-start(bf16[3,64,512]{2,1,0:T(8,128)(2,1)S(1)} %get-tuple-element.206), channel_id=1, source_target_pairs={{0,4},{1,5},{2,6},{3,7},{4,0},{5,1},{6,2},{7,3},{8,12},{9,13},{10,... | collective-permute-start | bytes 589832 | tf_op jit(solution)/shard_map/ppermute | solution.py:1113
  11.1 13.2 %collective-permute-start.4 = (bf16[3,64,512]{2,1,0:T(8,128)(2,1)S(1)}, bf16[3,64,512]{2,1,0:T(8,128)(2,1)S(1)}, u32[]{:S(2)}, u32[]{:S(2)}) collective-permute-start(bf16[3,64,512]{2,1,0:T(8,128)(2,1)S(1)} %get-tuple-element.203), channel_id=1, source_target_pairs={{0,6},{1,7},{2,4},{3,5},{4,2},{5,3},{6,0},{7,1},{8,14},{9,15},{10,... | collective-permute-start | bytes 589832 | tf_op jit(solution)/shard_map/ppermute | solution.py:1113
  14.6 15.9 %collective-permute-start.13 = (bf16[80,1024]{1,0:T(8,128)(2,1)S(1)}, bf16[80,1024]{1,0:T(8,128)(2,1)S(1)}, u32[]{:S(2)}, u32[]{:S(2)}) collective-permute-start(bf16[80,1024]{1,0:T(8,128)(2,1)S(1)} %constant_dynamic-update-slice_fusion.refs_2_.refs_0_.refs_3_), channel_id=1, source_target_pairs={{0,16},{8,24},{16,0},{24,8},{1,17},{9,25},{17,1},{25,9},{2,18},{10... | collective-permute-start | bytes 491528 | tf_op jit(solution)/shard_map/ppermute | solution.py:1116
  28.9 10.4 %collective-permute-start.11 = (bf16[80,1024]{1,0:T(8,128)(2,1)S(1)}, bf16[80,1024]{1,0:T(8,128)(2,1)S(1)}, u32[]{:S(2)}, u32[]{:S(2)}) collective-permute-start(bf16[80,1024]{1,0:T(8,128)(2,1)S(1)} %pad_maximum_fusion.3.refs_0_), channel_id=1, source_target_pairs={{0,8},{8,0},{16,24},{24,16},{1,9},{9,1},{17,25},{25,17},{2,10},{10... | collective-permute-start | bytes 491528 | tf_op jit(solution)/shard_map/ppermute | solution.py:1116
  30.3 13.1 %collective-permute-start.5 = (bf16[3,256,256]{2,1,0:T(8,128)(2,1)S(1)}, bf16[3,256,256]{2,1,0:T(8,128)(2,1)S(1)}, u32[]{:S(2)}, u32[]{:S(2)}) collective-permute-start(bf16[3,256,256]{2,1,0:T(8,128)(2,1)S(1)} %get-tuple-element.103.refs_0_.refs_6_.refs_2_.refs_9_), channel_id=1, source_target_pairs={{0,8},{8,0},{16,24},{24,16},{1,9},{9,1},{17,25},{25,17},{2,10},{10... | collective-permute-start | bytes 1179656 | tf_op jit(solution)/shard_map/ppermute | solution.py:1116
  31.3 19.0 %collective-permute-start.14 = (bf16[2,80,1024]{2,1,0:T(8,128)(2,1)}, bf16[2,80,1024]{2,1,0:T(8,128)(2,1)}, u32[]{:S(2)}, u32[]{:S(2)}) collective-permute-start(bf16[2,80,1024]{2,1,0:T(8,128)(2,1)} %stack.61), channel_id=1, source_target_pairs={{0,8},{8,0},{16,24},{24,16},{1,9},{9,1},{17,25},{25,17},{2,10},{10... | collective-permute-start | bytes 983048 | tf_op jit(solution)/shard_map/ppermute | solution.py:1116
  32.6 15.3 %collective-permute-start.8 = (bf16[3,256,256]{2,1,0:T(8,128)(2,1)S(1)}, bf16[3,256,256]{2,1,0:T(8,128)(2,1)S(1)}, u32[]{:S(2)}, u32[]{:S(2)}) collective-permute-start(bf16[3,256,256]{2,1,0:T(8,128)(2,1)S(1)} %collective-permute-done.7.refs_0_.refs_5_.refs_12_), channel_id=1, source_target_pairs={{0,16},{8,24},{16,0},{24,8},{1,17},{9,25},{17,1},{25,9},{2,18},{10... | collective-permute-start | bytes 1179656 | tf_op jit(solution)/shard_map/ppermute | solution.py:1116
  36.3 20.4 %collective-permute-start.28 = (bf16[2,64,1408]{2,1,0:T(8,128)(2,1)}, bf16[2,64,1408]{2,1,0:T(8,128)(2,1)}, u32[]{:S(2)}, u32[]{:S(2)}) collective-permute-start(bf16[2,64,1408]{2,1,0:T(8,128)(2,1)} %get-tuple-element.201), channel_id=1, source_target_pairs={{0,2},{1,3},{2,0},{3,1},{4,6},{5,7},{6,4},{7,5},{8,10},{9,11},{10,... | collective-permute-start | bytes 1081352 | tf_op jit(solution)/shard_map/ppermute | solution.py:1113
  39.4 20.8 %collective-permute-start.29 = (bf16[2,64,1408]{2,1,0:T(8,128)(2,1)}, bf16[2,64,1408]{2,1,0:T(8,128)(2,1)}, u32[]{:S(2)}, u32[]{:S(2)}) collective-permute-start(bf16[2,64,1408]{2,1,0:T(8,128)(2,1)} %get-tuple-element.200), channel_id=1, source_target_pairs={{0,4},{1,5},{2,6},{3,7},{4,0},{5,1},{6,2},{7,3},{8,12},{9,13},{10,... | collective-permute-start | bytes 1081352 | tf_op jit(solution)/shard_map/ppermute | solution.py:1113
  47.9 29.2 %collective-permute-start.6 = (bf16[2,3,256,256]{3,2,1,0:T(8,128)(2,1)}, bf16[2,3,256,256]{3,2,1,0:T(8,128)(2,1)}, u32[]{:S(2)}, u32[]{:S(2)}) collective-permute-start(bf16[2,3,256,256]{3,2,1,0:T(8,128)(2,1)} %stack.58), channel_id=1, source_target_pairs={{0,16},{8,24},{16,0},{24,8},{1,17},{9,25},{17,1},{25,9},{2,18},{10... | collective-permute-start | bytes 2359304 | tf_op jit(solution)/shard_map/ppermute | solution.py:1116
  50.4 26.7 %collective-permute-start.9 = (bf16[2,3,256,256]{3,2,1,0:T(8,128)(2,1)}, bf16[2,3,256,256]{3,2,1,0:T(8,128)(2,1)}, u32[]{:S(2)}, u32[]{:S(2)}) collective-permute-start(bf16[2,3,256,256]{3,2,1,0:T(8,128)(2,1)} %stack.59), channel_id=1, source_target_pairs={{0,8},{8,0},{16,24},{24,16},{1,9},{9,1},{17,25},{25,17},{2,10},{10... | collective-permute-start | bytes 2359304 | tf_op jit(solution)/shard_map/ppermute | solution.py:1116
  52.3 13.3 %collective-permute-start.30 = (bf16[2,64,1408]{2,1,0:T(8,128)(2,1)}, bf16[2,64,1408]{2,1,0:T(8,128)(2,1)}, u32[]{:S(2)}, u32[]{:S(2)}) collective-permute-start(bf16[2,64,1408]{2,1,0:T(8,128)(2,1)} %get-tuple-element.199), channel_id=1, source_target_pairs={{0,6},{1,7},{2,4},{3,5},{4,2},{5,3},{6,0},{7,1},{8,14},{9,15},{10,... | collective-permute-start | bytes 1081352 | tf_op jit(solution)/shard_map/ppermute | solution.py:1113
  56.7 13.6 %collective-permute-start.15 = (bf16[320,1024]{1,0:T(8,128)(2,1)}, bf16[320,1024]{1,0:T(8,128)(2,1)}, u32[]{:S(2)}, u32[]{:S(2)}) collective-permute-start(bf16[320,1024]{1,0:T(8,128)(2,1)} %get-tuple-element.107.refs_3_), channel_id=1, source_target_pairs={{0,1},{1,0},{2,3},{3,2},{4,5},{5,4},{6,7},{7,6},{8,9},{9,8},{10,11... | collective-permute-start | bytes 1966088 | tf_op jit(solution)/shard_map/ppermute | solution.py:1113
  60.1 10.1 %collective-permute-start.16 = (bf16[320,1024]{1,0:T(8,128)(2,1)}, bf16[320,1024]{1,0:T(8,128)(2,1)}, u32[]{:S(2)}, u32[]{:S(2)}) collective-permute-start(bf16[320,1024]{1,0:T(8,128)(2,1)} %get-tuple-element.108.refs_4_), channel_id=1, source_target_pairs={{0,1},{1,0},{2,3},{3,2},{4,5},{5,4},{6,7},{7,6},{8,9},{9,8},{10,11... | collective-permute-start | bytes 1966088 | tf_op jit(solution)/shard_map/ppermute | solution.py:1113
  68.0 17.3 %collective-permute-start.33 = (bf16[2,256,768]{2,1,0:T(8,128)(2,1)S(1)}, bf16[2,256,768]{2,1,0:T(8,128)(2,1)S(1)}, u32[]{:S(2)}, u32[]{:S(2)}) collective-permute-start(bf16[2,256,768]{2,1,0:T(8,128)(2,1)S(1)} %get-tuple-element.122), channel_id=1, source_target_pairs={{0,1},{1,0},{2,3},{3,2},{4,5},{5,4},{6,7},{7,6},{8,9},{9,8},{10,11... | collective-permute-start | bytes 2359304 | tf_op jit(solution)/shard_map/ppermute | solution.py:1113
  85.3 18.8 %collective-permute-start.34 = (bf16[2,256,768]{2,1,0:T(8,128)(2,1)S(1)}, bf16[2,256,768]{2,1,0:T(8,128)(2,1)S(1)}, u32[]{:S(2)}, u32[]{:S(2)}) collective-permute-start(bf16[2,256,768]{2,1,0:T(8,128)(2,1)S(1)} %collective-permute-done.33.refs_0_.refs_3_.refs_12_.refs_5_), channel_id=1, source_target_pairs={{0,16},{8,24},{16,0},{24,8},{1,17},{9,25},{17,1},{25,9},{2,18},{10... | collective-permute-start | bytes 2359304 | tf_op jit(solution)/shard_map/ppermute | solution.py:1116
  85.6 25.5 %collective-permute-start.31 = (bf16[2,256,768]{2,1,0:T(8,128)(2,1)S(1)}, bf16[2,256,768]{2,1,0:T(8,128)(2,1)S(1)}, u32[]{:S(2)}, u32[]{:S(2)}) collective-permute-start(bf16[2,256,768]{2,1,0:T(8,128)(2,1)S(1)} %get-tuple-element.121.refs_0_.refs_1_.refs_9_.refs_2_), channel_id=1, source_target_pairs={{0,8},{8,0},{16,24},{24,16},{1,9},{9,1},{17,25},{25,17},{2,10},{10... | collective-permute-start | bytes 2359304 | tf_op jit(solution)/shard_map/ppermute | solution.py:1116
  89.6 19.9 %collective-permute-start.19 = (bf16[56,2048]{1,0:T(8,128)(2,1)S(1)}, bf16[56,2048]{1,0:T(8,128)(2,1)S(1)}, u32[]{:S(2)}, u32[]{:S(2)}) collective-permute-start(bf16[56,2048]{1,0:T(8,128)(2,1)S(1)} %get-tuple-element.117), channel_id=1, source_target_pairs={{0,4},{1,5},{2,6},{3,7},{4,0},{5,1},{6,2},{7,3},{8,12},{9,13},{10,... | collective-permute-start | bytes 688136 | tf_op jit(solution)/shard_map/ppermute | solution.py:1113
  110.7 39.8 %collective-permute-start.35 = (bf16[2,2,256,768]{3,2,1,0:T(8,128)(2,1)}, bf16[2,2,256,768]{3,2,1,0:T(8,128)(2,1)}, u32[]{:S(2)}, u32[]{:S(2)}) collective-permute-start(bf16[2,2,256,768]{3,2,1,0:T(8,128)(2,1)} %stack.63), channel_id=1, source_target_pairs={{0,8},{8,0},{16,24},{24,16},{1,9},{9,1},{17,25},{25,17},{2,10},{10... | collective-permute-start | bytes 4718600 | tf_op jit(solution)/shard_map/ppermute | solution.py:1116
  112.5 38.1 %collective-permute-start.32 = (bf16[2,2,256,768]{3,2,1,0:T(8,128)(2,1)}, bf16[2,2,256,768]{3,2,1,0:T(8,128)(2,1)}, u32[]{:S(2)}, u32[]{:S(2)}) collective-permute-start(bf16[2,2,256,768]{3,2,1,0:T(8,128)(2,1)} %stack.62), channel_id=1, source_target_pairs={{0,16},{8,24},{16,0},{24,8},{1,17},{9,25},{17,1},{25,9},{2,18},{10... | collective-permute-start | bytes 4718600 | tf_op jit(solution)/shard_map/ppermute | solution.py:1116
  115.4 11.6 %collective-permute-start.20 = (bf16[56,2048]{1,0:T(8,128)(2,1)}, bf16[56,2048]{1,0:T(8,128)(2,1)}, u32[]{:S(2)}, u32[]{:S(2)}) collective-permute-start(bf16[56,2048]{1,0:T(8,128)(2,1)} %get-tuple-element.118), channel_id=1, source_target_pairs={{0,6},{1,7},{2,4},{3,5},{4,2},{5,3},{6,0},{7,1},{8,14},{9,15},{10,... | collective-permute-start | bytes 688136 | tf_op jit(solution)/shard_map/ppermute | solution.py:1113
  130.3 19.6 %collective-permute-start.22 = (bf16[48,2048]{1,0:T(8,128)(2,1)S(1)}, bf16[48,2048]{1,0:T(8,128)(2,1)S(1)}, u32[]{:S(2)}, u32[]{:S(2)}) collective-permute-start(bf16[48,2048]{1,0:T(8,128)(2,1)S(1)} %get-tuple-element.119.refs_1_), channel_id=1, source_target_pairs={{0,4},{1,5},{2,6},{3,7},{4,0},{5,1},{6,2},{7,3},{8,12},{9,13},{10,... | collective-permute-start | bytes 589832 | tf_op jit(solution)/shard_map/ppermute | solution.py:1113
  131.4 18.6 %collective-permute-start.23 = (bf16[48,2048]{1,0:T(8,128)(2,1)S(1)}, bf16[48,2048]{1,0:T(8,128)(2,1)S(1)}, u32[]{:S(2)}, u32[]{:S(2)}) collective-permute-start(bf16[48,2048]{1,0:T(8,128)(2,1)S(1)} %get-tuple-element.119.refs_1_), channel_id=1, source_target_pairs={{0,6},{1,7},{2,4},{3,5},{4,2},{5,3},{6,0},{7,1},{8,14},{9,15},{10,... | collective-permute-start | bytes 589832 | tf_op jit(solution)/shard_map/ppermute | solution.py:1113
  136.7 17.2 %collective-permute-start.24 = (bf16[48,2048]{1,0:T(8,128)(2,1)S(1)}, bf16[48,2048]{1,0:T(8,128)(2,1)S(1)}, u32[]{:S(2)}, u32[]{:S(2)}) collective-permute-start(bf16[48,2048]{1,0:T(8,128)(2,1)S(1)} %get-tuple-element.119.refs_1_), channel_id=1, source_target_pairs={{0,1},{1,0},{2,3},{3,2},{4,5},{5,4},{6,7},{7,6},{8,9},{9,8},{10,11... | collective-permute-start | bytes 589832 | tf_op jit(solution)/shard_map/ppermute | solution.py:1113
  168.2 43.6 %collective-permute-start.47 = (bf16[192,2048]{1,0:T(8,128)(2,1)S(1)}, bf16[192,2048]{1,0:T(8,128)(2,1)S(1)}, u32[]{:S(2)}, u32[]{:S(2)}) collective-permute-start(bf16[192,2048]{1,0:T(8,128)(2,1)S(1)} %get-tuple-element.150), channel_id=1, source_target_pairs={{0,1},{1,0},{2,3},{3,2},{4,5},{5,4},{6,7},{7,6},{8,9},{9,8},{10,11... | collective-permute-start | bytes 2359304 | tf_op jit(solution)/shard_map/ppermute | solution.py:1113
  169.1 9.6 %collective-permute-start.37 = (bf16[48,2048]{1,0:T(8,128)(2,1)S(1)}, bf16[48,2048]{1,0:T(8,128)(2,1)S(1)}, u32[]{:S(2)}, u32[]{:S(2)}) collective-permute-start(bf16[48,2048]{1,0:T(8,128)(2,1)S(1)} %get-tuple-element.131), channel_id=1, source_target_pairs={{0,2},{1,3},{2,0},{3,1},{4,6},{5,7},{6,4},{7,5},{8,10},{9,11},{10,... | collective-permute-start | bytes 589832 | tf_op jit(solution)/shard_map/ppermute | solution.py:1113
  170.4 16.3 %collective-permute-start.38 = (bf16[48,2048]{1,0:T(8,128)(2,1)S(1)}, bf16[48,2048]{1,0:T(8,128)(2,1)S(1)}, u32[]{:S(2)}, u32[]{:S(2)}) collective-permute-start(bf16[48,2048]{1,0:T(8,128)(2,1)S(1)} %get-tuple-element.132), channel_id=1, source_target_pairs={{0,4},{1,5},{2,6},{3,7},{4,0},{5,1},{6,2},{7,3},{8,12},{9,13},{10,... | collective-permute-start | bytes 589832 | tf_op jit(solution)/shard_map/ppermute | solution.py:1113
  171.7 15.0 %collective-permute-start.39 = (bf16[48,2048]{1,0:T(8,128)(2,1)S(1)}, bf16[48,2048]{1,0:T(8,128)(2,1)S(1)}, u32[]{:S(2)}, u32[]{:S(2)}) collective-permute-start(bf16[48,2048]{1,0:T(8,128)(2,1)S(1)} %get-tuple-element.133), channel_id=1, source_target_pairs={{0,6},{1,7},{2,4},{3,5},{4,2},{5,3},{6,0},{7,1},{8,14},{9,15},{10,... | collective-permute-start | bytes 589832 | tf_op jit(solution)/shard_map/ppermute | solution.py:1113
  188.9 12.3 %collective-permute-start.40 = (bf16[56,2048]{1,0:T(8,128)(2,1)S(1)}, bf16[56,2048]{1,0:T(8,128)(2,1)S(1)}, u32[]{:S(2)}, u32[]{:S(2)}) collective-permute-start(bf16[56,2048]{1,0:T(8,128)(2,1)S(1)} %get-tuple-element.144.refs_3_.refs_1_), channel_id=1, source_target_pairs={{0,2},{1,3},{2,0},{3,1},{4,6},{5,7},{6,4},{7,5},{8,10},{9,11},{10,... | collective-permute-start | bytes 688136 | tf_op jit(solution)/shard_map/ppermute | solution.py:1113
  192.1 19.1 %collective-permute-start.41 = (bf16[56,2048]{1,0:T(8,128)(2,1)S(1)}, bf16[56,2048]{1,0:T(8,128)(2,1)S(1)}, u32[]{:S(2)}, u32[]{:S(2)}) collective-permute-start(bf16[56,2048]{1,0:T(8,128)(2,1)S(1)} %get-tuple-element.144.refs_3_.refs_1_), channel_id=1, source_target_pairs={{0,4},{1,5},{2,6},{3,7},{4,0},{5,1},{6,2},{7,3},{8,12},{9,13},{10,... | collective-permute-start | bytes 688136 | tf_op jit(solution)/shard_map/ppermute | solution.py:1113
  194.6 17.3 %collective-permute-start.46 = (bf16[56,2048]{1,0:T(8,128)(2,1)S(1)}, bf16[56,2048]{1,0:T(8,128)(2,1)S(1)}, u32[]{:S(2)}, u32[]{:S(2)}) collective-permute-start(bf16[56,2048]{1,0:T(8,128)(2,1)S(1)} %collective-permute-done.42.refs_4_), channel_id=1, source_target_pairs={{0,1},{1,0},{2,3},{3,2},{4,5},{5,4},{6,7},{7,6},{8,9},{9,8},{10,11... | collective-permute-start | bytes 688136 | tf_op jit(solution)/shard_map/ppermute | solution.py:1113
  199.2 13.4 %collective-permute-start.43 = (bf16[56,2048]{1,0:T(8,128)(2,1)S(1)}, bf16[56,2048]{1,0:T(8,128)(2,1)S(1)}, u32[]{:S(2)}, u32[]{:S(2)}) collective-permute-start(bf16[56,2048]{1,0:T(8,128)(2,1)S(1)} %get-tuple-element.144.refs_3_.refs_1_), channel_id=1, source_target_pairs={{0,1},{1,0},{2,3},{3,2},{4,5},{5,4},{6,7},{7,6},{8,9},{9,8},{10,11... | collective-permute-start | bytes 688136 | tf_op jit(solution)/shard_map/ppermute | solution.py:1113
  201.2 11.5 %collective-permute-start.44 = (bf16[56,2048]{1,0:T(8,128)(2,1)S(1)}, bf16[56,2048]{1,0:T(8,128)(2,1)S(1)}, u32[]{:S(2)}, u32[]{:S(2)}) collective-permute-start(bf16[56,2048]{1,0:T(8,128)(2,1)S(1)} %collective-permute-done.40.refs_2_), channel_id=1, source_target_pairs={{0,1},{1,0},{2,3},{3,2},{4,5},{5,4},{6,7},{7,6},{8,9},{9,8},{10,11... | collective-permute-start | bytes 688136 | tf_op jit(solution)/shard_map/ppermute | solution.py:1113
  212.6 11.4 %collective-permute-start.49 = (bf16[48,2048]{1,0:T(8,128)(2,1)S(1)}, bf16[48,2048]{1,0:T(8,128)(2,1)S(1)}, u32[]{:S(2)}, u32[]{:S(2)}) collective-permute-start(bf16[48,2048]{1,0:T(8,128)(2,1)S(1)} %get-tuple-element.159), channel_id=1, source_target_pairs={{0,4},{1,5},{2,6},{3,7},{4,0},{5,1},{6,2},{7,3},{8,12},{9,13},{10,... | collective-permute-start | bytes 589832 | tf_op jit(solution)/shard_map/ppermute | solution.py:1113
  220.9 15.2 %collective-permute-start.48 = (bf16[192,2048]{1,0:T(8,128)(2,1)S(1)}, bf16[192,2048]{1,0:T(8,128)(2,1)S(1)}, u32[]{:S(2)}, u32[]{:S(2)}) collective-permute-start(bf16[192,2048]{1,0:T(8,128)(2,1)S(1)} %get-tuple-element.153), channel_id=1, source_target_pairs={{0,1},{1,0},{2,3},{3,2},{4,5},{5,4},{6,7},{7,6},{8,9},{9,8},{10,11... | collective-permute-start | bytes 2359304 | tf_op jit(solution)/shard_map/ppermute | solution.py:1113
  236.8 28.3 %collective-permute-start.51 = (bf16[64,2048]{1,0:T(8,128)(2,1)S(1)}, bf16[64,2048]{1,0:T(8,128)(2,1)S(1)}, u32[]{:S(2)}, u32[]{:S(2)}) collective-permute-start(bf16[64,2048]{1,0:T(8,128)(2,1)S(1)} %get-tuple-element.177), channel_id=1, source_target_pairs={{0,2},{1,3},{2,0},{3,1},{4,6},{5,7},{6,4},{7,5},{8,10},{9,11},{10,... | collective-permute-start | bytes 786440 | tf_op jit(solution)/shard_map/ppermute | solution.py:1113
  237.4 27.6 %collective-permute-start.52 = (bf16[64,2048]{1,0:T(8,128)(2,1)S(1)}, bf16[64,2048]{1,0:T(8,128)(2,1)S(1)}, u32[]{:S(2)}, u32[]{:S(2)}) collective-permute-start(bf16[64,2048]{1,0:T(8,128)(2,1)S(1)} %get-tuple-element.178), channel_id=1, source_target_pairs={{0,4},{1,5},{2,6},{3,7},{4,0},{5,1},{6,2},{7,3},{8,12},{9,13},{10,... | collective-permute-start | bytes 786440 | tf_op jit(solution)/shard_map/ppermute | solution.py:1113
  238.8 26.3 %collective-permute-start.53 = (bf16[64,2048]{1,0:T(8,128)(2,1)S(1)}, bf16[64,2048]{1,0:T(8,128)(2,1)S(1)}, u32[]{:S(2)}, u32[]{:S(2)}) collective-permute-start(bf16[64,2048]{1,0:T(8,128)(2,1)S(1)} %get-tuple-element.179), channel_id=1, source_target_pairs={{0,6},{1,7},{2,4},{3,5},{4,2},{5,3},{6,0},{7,1},{8,14},{9,15},{10,... | collective-permute-start | bytes 786440 | tf_op jit(solution)/shard_map/ppermute | solution.py:1113
  240.4 19.4 %collective-permute-start.54 = (bf16[48,2048]{1,0:T(8,128)(2,1)S(1)}, bf16[48,2048]{1,0:T(8,128)(2,1)S(1)}, u32[]{:S(2)}, u32[]{:S(2)}) collective-permute-start(bf16[48,2048]{1,0:T(8,128)(2,1)S(1)} %get-tuple-element.181), channel_id=1, source_target_pairs={{0,2},{1,3},{2,0},{3,1},{4,6},{5,7},{6,4},{7,5},{8,10},{9,11},{10,... | collective-permute-start | bytes 589832 | tf_op jit(solution)/shard_map/ppermute | solution.py:1113
  240.4 24.7 %collective-permute-start.55 = (bf16[48,2048]{1,0:T(8,128)(2,1)S(1)}, bf16[48,2048]{1,0:T(8,128)(2,1)S(1)}, u32[]{:S(2)}, u32[]{:S(2)}) collective-permute-start(bf16[48,2048]{1,0:T(8,128)(2,1)S(1)} %get-tuple-element.182), channel_id=1, source_target_pairs={{0,6},{1,7},{2,4},{3,5},{4,2},{5,3},{6,0},{7,1},{8,14},{9,15},{10,... | collective-permute-start | bytes 589832 | tf_op jit(solution)/shard_map/ppermute | solution.py:1113
  265.7 29.2 %collective-permute-start.57 = (bf16[96,2048]{1,0:T(8,128)(2,1)S(1)}, bf16[96,2048]{1,0:T(8,128)(2,1)S(1)}, u32[]{:S(2)}, u32[]{:S(2)}) collective-permute-start(bf16[96,2048]{1,0:T(8,128)(2,1)S(1)} %last_rows.1.refs_1_), channel_id=1, source_target_pairs={{0,4},{1,5},{2,6},{3,7},{4,0},{5,1},{6,2},{7,3},{8,12},{9,13},{10,... | collective-permute-start | bytes 1179656 | tf_op jit(solution)/shard_map/ppermute | solution.py:1113
  279.9 12.3 %collective-permute-start.67 = (bf16[24,1024]{1,0:T(8,128)(2,1)S(1)}, bf16[24,1024]{1,0:T(8,128)(2,1)S(1)}, u32[]{:S(2)}, u32[]{:S(2)}) collective-permute-start(bf16[24,1024]{1,0:T(8,128)(2,1)S(1)} %last_sums.1), channel_id=1, source_target_pairs={{0,4},{1,5},{2,6},{3,7},{4,0},{5,1},{6,2},{7,3},{8,12},{9,13},{10,... | collective-permute-start | bytes 147464 | tf_op jit(solution)/shard_map/ppermute | solution.py:1113
  281.5 10.7 %collective-permute-start.68 = (bf16[24,1024]{1,0:T(8,128)(2,1)S(1)}, bf16[24,1024]{1,0:T(8,128)(2,1)S(1)}, u32[]{:S(2)}, u32[]{:S(2)}) collective-permute-start(bf16[24,1024]{1,0:T(8,128)(2,1)S(1)} %last_sums.1), channel_id=1, source_target_pairs={{0,6},{1,7},{2,4},{3,5},{4,2},{5,3},{6,0},{7,1},{8,14},{9,15},{10,... | collective-permute-start | bytes 147464 | tf_op jit(solution)/shard_map/ppermute | solution.py:1113
  283.4 22.5 %collective-permute-start.56 = (bf16[96,2048]{1,0:T(8,128)(2,1)S(1)}, bf16[96,2048]{1,0:T(8,128)(2,1)S(1)}, u32[]{:S(2)}, u32[]{:S(2)}) collective-permute-start(bf16[96,2048]{1,0:T(8,128)(2,1)S(1)} %last_rows.1.refs_1_), channel_id=1, source_target_pairs={{0,2},{1,3},{2,0},{3,1},{4,6},{5,7},{6,4},{7,5},{8,10},{9,11},{10,... | collective-permute-start | bytes 1179656 | tf_op jit(solution)/shard_map/ppermute | solution.py:1113
  294.6 10.7 %collective-permute-start.71 = (bf16[96,1024]{1,0:T(8,128)(2,1)S(1)}, bf16[96,1024]{1,0:T(8,128)(2,1)S(1)}, u32[]{:S(2)}, u32[]{:S(2)}) collective-permute-start(bf16[96,1024]{1,0:T(8,128)(2,1)S(1)} %pad_maximum_fusion.2.refs_2_), channel_id=1, source_target_pairs={{0,24},{8,16},{16,8},{24,0},{1,25},{9,17},{17,9},{25,1},{2,26},{10... | collective-permute-start | bytes 589832 | tf_op jit(solution)/shard_map/ppermute | solution.py:1116
  294.9 15.1 %collective-permute-start.58 = (bf16[96,2048]{1,0:T(8,128)(2,1)S(1)}, bf16[96,2048]{1,0:T(8,128)(2,1)S(1)}, u32[]{:S(2)}, u32[]{:S(2)}) collective-permute-start(bf16[96,2048]{1,0:T(8,128)(2,1)S(1)} %collective-permute-done.57.refs_3_), channel_id=1, source_target_pairs={{0,2},{1,3},{2,0},{3,1},{4,6},{5,7},{6,4},{7,5},{8,10},{9,11},{10,... | collective-permute-start | bytes 1179656 | tf_op jit(solution)/shard_map/ppermute | solution.py:1113
  (89 other events, 768.0 us)
